TPU v7x, 256 devices: a whole 4x4x8 slice. The times are simulated.
256 devices in a mesh: wide: 32 (over z, x), narrow: 8 (over y, core).
Axes of the slice: x: 4, y: 4, z: 8, core: 2. Of those that a mesh axis runs over, the one named last changes fastest.
Arguments:
- tractions: float32 [64, 16, 3, 256], P('wide', 'narrow'), may hold values from -6 to 6
- centers: float32 [64, 16, 3], P('wide', 'narrow'), may hold values from 0 to 272, as said below
- node_offsets: float32 [3, 256], replicated, may hold values from -3 to 3
- occupied: int32 [64, 16], P('wide', 'narrow'), may hold values from 0 to 1, as said below
- anchors: int32 [64, 16, 3], P('wide', 'narrow'), may hold values from 0 to 255, as said below
- near_list: int32 [64, 16, 2], P('wide', 'narrow'), may hold values from 0 to 1023, as said below
- contact_pairs: int32 [2, 8192], P(None, ('wide', 'narrow')), may hold values from 0 to 1023, as said below
- contact_gap: float32 [8192], P(('wide', 'narrow')), may hold values from -1 to 1
- contact_angles: float32 [2, 8192], P(None, ('wide', 'narrow')), may hold values from -3.140625 to 3.140625
Outputs:
- node_velocity: float32 [64, 16, 3, 256], P('wide', 'narrow')
- contact_force: float32 [8192], P(('wide', 'narrow'))
- moved_centers: float32 [64, 16, 3], P('wide', 'narrow')
Inputs may be any that keep to these rules, and one draw needn't show every extreme that they name: `occupied`: in every device's 2 x 2 block of slots the live slots come first in row-major order, and each device holds at least one; some device has all 4 slots live. `anchors`: for a slot of the device with indices w along wide and n along narrow, the first entry lies in [w * 8, (w + 1) * 8) and the second in [n * 32, (n + 1) * 32). `centers`: each component of a centre is its slot's anchor entry plus 16/2 plus at most 0.5 either way. `near_list`: entries of live slots name live spheres other than the slot's own, held by the same device or by one whose wide and narrow indices each differ by at most one, cyclically; entries may repeat. `contact_pairs`: the first sphere of a contact is live and held by the device that holds the contact; the second is an entry of the first's near list.
All inputs are finite; a program needn't handle non-finite values.
Results may differ from a plain program's by a relative error of at most 0.0003.
Values sent between devices are 32-bit elements; how exact they have to be, the bound alone decides.
A program may use at most 128 MiB of HBM per device.

v0:
```python
import jax
import jax.numpy as jnp
from jax import lax
from jax.sharding import PartitionSpec as P

NODES = 256
GRID = 256
BLOCK = 16
NEAR = 2
SWEEPS = 6


soften = 1.0
screen = 0.0625
near_scale = 0.05
spread_norm = 0.17958712212516656
mobility = 0.2
time_step = 0.5
relaxation = 0.35
ewald_split = 0.5


def extended_2(block, sides, width):
    for axis, dim in sides:
        count = lax.axis_size(axis)
        forward = [(i, i + 1) for i in range(count - 1)]
        forward.append((count - 1, 0))
        backward = [(target, source) for source, target in forward]
        low = lax.ppermute(
            lax.slice_in_dim(block, block.shape[dim] - width, None, axis=dim), axis, forward
        )
        high = lax.ppermute(lax.slice_in_dim(block, 0, width, axis=dim), axis, backward)
        block = jnp.concatenate([low, block, high], axis=dim)
    return block


def from_behind(block, axis, distance):
    devices = range(lax.axis_size(axis))
    route = [((i - distance) % len(devices), i) for i in devices]
    return lax.ppermute(block, axis, route)


def block_weights(coordinate, anchor_cell):
    cell_centres = anchor_cell.astype(jnp.float32) + jnp.arange(BLOCK).astype(jnp.float32)
    distance = coordinate[:, None] - cell_centres[None, :]
    return jnp.exp(-distance * distance)


def spread_block(forces, position, anchor):
    weight_x = block_weights(position[0], anchor[0])
    weight_y = block_weights(position[1], anchor[1])
    weight_z = block_weights(position[2], anchor[2])
    planar = weight_x[:, :, None] * weight_y[:, None, :]
    loaded = forces[:, :, None, None] * planar[None]
    return spread_norm * jnp.einsum(
        "cnab,ne->cabe", loaded, weight_z, precision=lax.Precision.HIGHEST
    )


def interp_block(mesh_block, position, anchor):
    weight_x = block_weights(position[0], anchor[0])
    weight_y = block_weights(position[1], anchor[1])
    weight_z = block_weights(position[2], anchor[2])
    along_z = jnp.einsum("cabe,ne->cabn", mesh_block, weight_z, precision=lax.Precision.HIGHEST)
    along_y = jnp.einsum("cabn,nb->can", along_z, weight_y, precision=lax.Precision.HIGHEST)
    return spread_norm * jnp.einsum(
        "can,na->cn", along_y, weight_x, precision=lax.Precision.HIGHEST
    )


def stokes_tile(displacement, offsets, forces):
    separation = [
        displacement[component] + offsets[component][:, None] - offsets[component][None, :]
        for component in range(3)
    ]
    radius_sq = (
        separation[0] * separation[0]
        + separation[1] * separation[1]
        + separation[2] * separation[2]
    )
    softened = radius_sq + soften
    weight = jnp.exp(-radius_sq * screen) / (softened * jnp.sqrt(softened))
    projected = (
        separation[0] * forces[0][None, :]
        + separation[1] * forces[1][None, :]
        + separation[2] * forces[2][None, :]
    )
    diagonal = (radius_sq + 2.0 * soften) * weight
    velocity = [
        jnp.sum(
            diagonal * forces[component][None, :] + separation[component] * projected * weight,
            axis=1,
        )
        for component in range(3)
    ]
    return near_scale * jnp.stack(velocity)


def nearest_image(difference):
    return difference - GRID * jnp.floor(difference / GRID + 0.5)


def far_kernel(wave_x, wave_y, wave_z, real_part, imag_part):
    wave_sq = wave_x * wave_x + wave_y * wave_y + wave_z * wave_z
    safe_sq = jnp.maximum(wave_sq, 1.0)
    damping = (ewald_split * jnp.pi / GRID) ** 2
    factor = jnp.where(wave_sq > 0.5, jnp.exp(-damping * wave_sq) / safe_sq, 0.0) * (
        GRID * GRID / (4.0 * jnp.pi * jnp.pi)
    )
    waves = (wave_x, wave_y, wave_z)
    results = []
    for values in (real_part, imag_part):
        inner = waves[0] * values[0] + waves[1] * values[1] + waves[2] * values[2]
        results.append(
            jnp.stack(
                [
                    factor * (values[component] - waves[component] * inner / safe_sq)
                    for component in range(3)
                ]
            )
        )
    return (results[0], results[1])


def along(values, table, dimension):
    letters = "pqrs"
    output = letters[:dimension] + "t" + letters[dimension + 1 :]
    return jnp.einsum(
        letters + "," + letters[dimension] + "t->" + output,
        values,
        table,
        precision=lax.Precision.HIGHEST,
    )


def signed_waves(indices):
    return jnp.where(indices < GRID // 2, indices, indices - GRID).astype(jnp.float32)


def local(
    tractions,
    centers,
    node_offsets,
    occupied,
    anchors,
    near_list,
    contact_pairs,
    contact_gap,
    contact_angles,
):
    side = tractions.shape[0]
    per_device = side * side
    wide_count = lax.axis_size("wide")
    narrow_count = lax.axis_size("narrow")
    wide_rank = lax.axis_index("wide")
    narrow_rank = lax.axis_index("narrow")
    pencil_x = GRID // wide_count
    pencil_y = GRID // narrow_count
    reach_x = -(-BLOCK // pencil_x)
    reach_y = -(-BLOCK // pencil_y)
    forces = tractions.reshape(per_device, 3, NODES)
    centres = centers.reshape(per_device, 3)
    starts = anchors.reshape(per_device, 3)
    neighbours = near_list.reshape(per_device, NEAR)
    live_count = jnp.sum(occupied)
    zero_index = jnp.zeros((), jnp.int32)
    lower_x = wide_rank * pencil_x
    lower_y = narrow_rank * pencil_y
    halo_forces, halo_centres = (
        extended_2(tractions, (("wide", 0), ("narrow", 1)), side),
        extended_2(centers, (("wide", 0), ("narrow", 1)), side),
    )

    def near_sphere(slot_index, velocity):
        centre = centres[slot_index]
        summed = stokes_tile(jnp.zeros((3,), jnp.float32), node_offsets, forces[slot_index])
        for neighbour_rank in range(NEAR):
            neighbour = neighbours[slot_index, neighbour_rank]
            holder = neighbour // per_device
            within = neighbour % per_device
            halo_row = (
                holder // narrow_count - wide_rank + 1 + wide_count
            ) % wide_count * side + within // side
            column = (
                holder % narrow_count - narrow_rank + 1 + narrow_count
            ) % narrow_count * side + within % side
            summed = summed + stokes_tile(
                nearest_image(centre - halo_centres[halo_row, column]),
                node_offsets,
                halo_forces[halo_row, column],
            )
        return lax.dynamic_update_index_in_dim(velocity, summed, slot_index, 0)

    near_field = lax.fori_loop(
        0, live_count, near_sphere, jnp.zeros((per_device, 3, NODES), jnp.float32)
    )
    buffer = jnp.zeros(
        (3, (1 + reach_x) * pencil_x, (1 + reach_y) * pencil_y, GRID + BLOCK), jnp.float32
    )

    def deposit(slot_index, buffer):
        corner = starts[slot_index]
        location = (zero_index, corner[0] - lower_x, corner[1] - lower_y, corner[2])
        sphere_block = spread_block(
            forces[slot_index], centres[slot_index][:, None] + node_offsets, corner
        )
        current = lax.dynamic_slice(buffer, location, (3, BLOCK, BLOCK, BLOCK))
        return lax.dynamic_update_slice(buffer, current + sphere_block, location)

    buffer = lax.fori_loop(0, live_count, deposit, buffer)
    folded = buffer[..., :GRID]
    folded = lax.dynamic_update_slice_in_dim(folded, folded[..., :BLOCK] + buffer[..., GRID:], 0, 3)
    owned_x = folded[:, :pencil_x]
    for step_x in range(1, reach_x + 1):
        owned_x = owned_x + from_behind(
            folded[:, step_x * pencil_x : (step_x + 1) * pencil_x], "wide", step_x
        )
    mesh = owned_x[:, :, :pencil_y]
    mesh = mesh + from_behind(owned_x[:, :, 1 * pencil_y : 2 * pencil_y], "narrow", 1)
    index_grid = jnp.arange(GRID, dtype=jnp.int32)
    phase = (index_grid[:, None] * index_grid[None, :] % GRID).astype(jnp.float32) * (
        2.0 * jnp.pi / GRID
    )
    cosine = jnp.cos(phase)
    sine = jnp.sin(phase)

    def forward(spectra, dimension):
        real_part, imag_part = spectra
        return (
            along(real_part, cosine, dimension) + along(imag_part, sine, dimension),
            along(imag_part, cosine, dimension) - along(real_part, sine, dimension),
        )

    def backward(spectra, dimension):
        real_part, imag_part = spectra
        return (
            along(real_part, cosine, dimension) - along(imag_part, sine, dimension),
            along(imag_part, cosine, dimension) + along(real_part, sine, dimension),
        )

    spec_real = along(mesh, cosine, 3)
    spec_imag = -along(mesh, sine, 3)
    wide_piece = GRID // wide_count
    narrow_piece = GRID // narrow_count
    spec_real, spec_imag = forward(
        (
            lax.all_to_all(spec_real, "wide", split_axis=3, concat_axis=1, tiled=True),
            lax.all_to_all(spec_imag, "wide", split_axis=3, concat_axis=1, tiled=True),
        ),
        1,
    )
    spec_real, spec_imag = forward(
        (
            lax.all_to_all(spec_real, "narrow", split_axis=1, concat_axis=2, tiled=True),
            lax.all_to_all(spec_imag, "narrow", split_axis=1, concat_axis=2, tiled=True),
        ),
        2,
    )
    wave_x = signed_waves(narrow_rank * narrow_piece + jnp.arange(narrow_piece, dtype=jnp.int32))[
        :, None, None
    ]
    wave_y = signed_waves(index_grid)[None, :, None]
    wave_z = signed_waves(wide_rank * wide_piece + jnp.arange(wide_piece, dtype=jnp.int32))[
        None, None, :
    ]
    spec_real, spec_imag = far_kernel(wave_x, wave_y, wave_z, spec_real, spec_imag)
    spec_real, spec_imag = backward((spec_real, spec_imag), 2)
    spec_real, spec_imag = backward(
        (
            lax.all_to_all(spec_real, "narrow", split_axis=2, concat_axis=1, tiled=True),
            lax.all_to_all(spec_imag, "narrow", split_axis=2, concat_axis=1, tiled=True),
        ),
        1,
    )
    real_part = lax.all_to_all(spec_real, "wide", split_axis=1, concat_axis=3, tiled=True)
    imag_part = lax.all_to_all(spec_imag, "wide", split_axis=1, concat_axis=3, tiled=True)
    velocity_mesh = (along(real_part, cosine, 3) - along(imag_part, sine, 3)) * (1.0 / GRID**3)
    extended_y = jnp.concatenate(
        [velocity_mesh] + [from_behind(velocity_mesh, "narrow", -1)], axis=2
    )
    extended = jnp.concatenate(
        [extended_y]
        + [from_behind(extended_y, "wide", -step_x) for step_x in range(1, reach_x + 1)],
        axis=1,
    )
    extended = jnp.concatenate([extended, extended[..., :BLOCK]], axis=3)

    def sample(slot_index, velocity):
        corner = starts[slot_index]
        location = (zero_index, corner[0] - lower_x, corner[1] - lower_y, corner[2])
        mesh_block = lax.dynamic_slice(extended, location, (3, BLOCK, BLOCK, BLOCK))
        far_part = interp_block(mesh_block, centres[slot_index][:, None] + node_offsets, corner)
        return lax.dynamic_update_index_in_dim(
            velocity, velocity[slot_index] + far_part, slot_index, 0
        )

    node_velocity = lax.fori_loop(0, live_count, sample, near_field)
    hydro = jnp.mean(node_velocity, axis=2)
    first_ids = contact_pairs[0]
    second_ids = contact_pairs[1]
    polar = contact_angles[0]
    azimuth = contact_angles[1]
    normal = jnp.stack(
        [jnp.sin(polar) * jnp.cos(azimuth), jnp.sin(polar) * jnp.sin(azimuth), jnp.cos(polar)],
        axis=1,
    )

    def halo_slot(global_ids):
        holder = global_ids // per_device
        within = global_ids % per_device
        halo_row = (
            holder // narrow_count - wide_rank + 1 + wide_count
        ) % wide_count * side + within // side
        column = (
            holder % narrow_count - narrow_rank + 1 + narrow_count
        ) % narrow_count * side + within % side
        return halo_row * (3 * side) + column

    magnitude = jnp.zeros_like(contact_gap)
    table_side = 3 * side
    first_places = halo_slot(first_ids)
    second_places = halo_slot(second_ids)
    for sweep_index in range(SWEEPS + 1):
        loading = magnitude[:, None] * normal
        table = jax.ops.segment_sum(
            loading, first_places, num_segments=table_side * table_side
        ) - jax.ops.segment_sum(loading, second_places, num_segments=table_side * table_side)
        widened = extended_2(
            table.reshape(table_side, table_side, 3), (("wide", 0), ("narrow", 1)), side
        )
        gathered_sum = jnp.zeros((side, side, 3), jnp.float32)
        for row_block in (0, 2, 4):
            for column_block in (0, 2, 4):
                gathered_sum = (
                    gathered_sum
                    + widened[
                        row_block * side : (row_block + 1) * side,
                        column_block * side : (column_block + 1) * side,
                    ]
                )
        own_totals = gathered_sum.reshape(per_device, 3)
        if sweep_index < SWEEPS:
            velocity_own = (hydro + mobility * own_totals).reshape(side, side, 3)
            surrounding = extended_2(velocity_own, (("wide", 0), ("narrow", 1)), side)
            relax_velocity = surrounding.reshape(table_side * table_side, 3)
            relative = jnp.sum(
                normal * (relax_velocity[first_places] - relax_velocity[second_places]), axis=1
            )
            magnitude = jnp.maximum(
                magnitude
                - relaxation * (contact_gap + time_step * relative) / (2.0 * time_step * mobility),
                0.0,
            )
    moved = centres + time_step * (hydro + mobility * own_totals)
    return (node_velocity.reshape(side, side, 3, NODES), magnitude, moved.reshape(side, side, 3))


def solution(mesh):
    placed = (
        P("wide", "narrow", None, None),
        P("wide", "narrow", None),
        P(),
        P("wide", "narrow"),
        P("wide", "narrow", None),
        P("wide", "narrow", None),
        P(None, ("wide", "narrow")),
        P(("wide", "narrow")),
        P(None, ("wide", "narrow")),
    )
    return jax.shard_map(
        local,
        mesh=mesh,
        in_specs=placed,
        out_specs=(
            P("wide", "narrow", None, None),
            P(("wide", "narrow")),
            P("wide", "narrow", None),
        ),
        check_vma=False,
    )
```

profile of v0, /device:TPU:1, one launch (start us, length us, event | category | flops | bytes accessed | tf_op | source)
XLA Modules:
  0.0 884.1 jit_solution(16848352392138684741)
XLA Ops:
  6.4 30.8 %while.34 = (s32[]{:T(128)}, f32[3,24,64,272]{3,2,1,0:T(8,128)}, s32[]{:T(128)}, s32[4,3]{1,0:T(4,128)}, s32[]{:T(128)}, /*index=5*/s32[]{:T(128)}, f32[4,3,256]...) while((s32[]{:T(128)}, f32[3,24,64,272]{3,2,1,0:T(8,128)}, ...), condition=%wide.region_13.14_spmd, body=%wide.region_12.13_spmd.sunk | while | flops 38073200 | bytes 811841 | solution.py:210
  15.9 20.6 %dynamic_update_slice.24 = f32[3,24,64,272]{3,2,1,0:T(8,128)} dynamic-update-slice(f32[3,24,64,272]{3,2,1,0:T(8,128)} %get-tuple-element.875, f32[3,16,16,16]{3,2,1,0:T(8,128)S(1)} %fusion.416, s32[]{:T(128)} %constant.474.clone.1..sunk.1, s32[]{:T(128)S(6)} %select_n.846, s32[]{:T(128)S(6)} %select_n.847, s32[]{:T(128)S(6)} %select_n.848) | dynamic-update-slice | bytes 98308 | tf_op jit(solution)/shard_map/while/body/dynamic_update_slice | solution.py:208
  37.2 5.2 slice.586
  42.9 11.9 %dynamic_update_slice.17 = f32[3,24,64,256]{3,2,1,0:T(8,128)} dynamic-update-slice(f32[3,24,64,256]{3,2,1,0:T(8,128)} %slice.586, f32[3,24,64,16]{3,2,1,0:T(8,128)S(1)} %slice_add_fusion, s32[]{:T(128)} %constant.474.clone.1, s32[]{:T(128)} %constant.474.clone.1, s32[]{:T(128)} %constant.474.clone.1, s32[]{:T(128)} %constant.474.clone.1) | dynamic-update-slice | bytes 589828 | tf_op jit(solution)/shard_map/dynamic_update_slice | solution.py:212
  59.2 61.9 %collective-permute-start.9 = (f32[3,8,64,256]{3,2,1,0:T(8,128)S(1)}, f32[3,8,64,256]{3,2,1,0:T(8,128)S(1)}, u32[]{:S(2)}, u32[]{:S(2)}) collective-permute-start(f32[3,8,64,256]{3,2,1,0:T(8,128)S(1)} %get-tuple-element.453), channel_id=1, source_target_pairs={{240,0},{248,8},{0,16},{8,24},{16,32},{24,40},{32,48},{40,56},{48,... | collective-permute-start | bytes 4718600 | tf_op jit(solution)/shard_map/ppermute | solution.py:40
  121.1 40.8 %collective-permute-done.8 = f32[3,8,64,256]{3,2,1,0:T(8,128)S(1)} collective-permute-done((f32[3,8,64,256]{3,2,1,0:T(8,128)S(1)}, f32[3,8,64,256]{3,2,1,0:T(8,128)S(1)}, u32[]{:S(2)}, u32[]{:S(2)}) %collective-permute-start.8) | collective-permute-done | bytes 1572896 | tf_op jit(solution)/shard_map/ppermute | solution.py:40
  163.9 26.4 %collective-permute-start.10 = (f32[3,8,32,256]{3,2,1,0:T(8,128)S(1)}, f32[3,8,32,256]{3,2,1,0:T(8,128)S(1)}, u32[]{:S(2)}, u32[]{:S(2)}) collective-permute-start(f32[3,8,32,256]{3,2,1,0:T(8,128)S(1)} %slice.744), channel_id=1, source_target_pairs={{7,0},{0,1},{1,2},{2,3},{3,4},{4,5},{5,6},{6,7},{15,8},{8,9},{9,10... | collective-permute-start | bytes 2359304 | tf_op jit(solution)/shard_map/ppermute | solution.py:40
  190.3 8.9 %collective-permute-done.10 = f32[3,8,32,256]{3,2,1,0:T(8,128)S(1)} collective-permute-done((f32[3,8,32,256]{3,2,1,0:T(8,128)S(1)}, f32[3,8,32,256]{3,2,1,0:T(8,128)S(1)}, u32[]{:S(2)}, u32[]{:S(2)}) %collective-permute-start.10) | collective-permute-done | bytes 786464 | tf_op jit(solution)/shard_map/ppermute | solution.py:40
  207.1 84.9 %all-to-all-start.1 = ((f32[32,1,6144]{2,1,0:T(1,128)}), f32[32,1,6144]{2,1,0:T(1,128)}, u32[]{:S(2)}, u32[]{:S(2)}) async-start(f32[32,1,6144]{2,1,0:T(1,128)} %reshape.1592), calls=%async_computation.1 | async-start | bytes 1572864 | tf_op jit(solution)/shard_map/all_to_all | solution.py:248
  300.5 9.7 %all-to-all-done.1 = f32[32,1,6144]{2,1,0:T(1,128)} async-done(((f32[32,1,6144]{2,1,0:T(1,128)}), f32[32,1,6144]{2,1,0:T(1,128)}, u32[]{:S(2)}, u32[]{:S(2)}) %all-to-all-start.1) | async-done | bytes 786464 | tf_op jit(solution)/shard_map/all_to_all | solution.py:248
  310.1 7.0 all-to-all-start
  317.8 4.5 reduce.5
  335.3 4.5 reduce.4
  354.8 12.3 %all-to-all-start.3 = ((f32[8,1,24576]{2,1,0:T(1,128)}), f32[8,1,24576]{2,1,0:T(1,128)}, u32[]{:S(2)}, u32[]{:S(2)}) async-start(f32[8,1,24576]{2,1,0:T(1,128)} %reshape.1596), calls=%async_computation.3 | async-start | bytes 1572864 | tf_op jit(solution)/shard_map/all_to_all | solution.py:255
  379.5 5.4 all-to-all-start.2
  385.1 4.6 reduce.7
  400.5 4.5 reduce.6
  428.4 5.4 all-to-all-start.4
  446.2 5.0 all-to-all-start.5
  451.1 4.6 reduce.9
  466.6 4.5 reduce.8
  487.2 5.2 all-to-all-start.6
  497.7 4.8 collective-permute-start.1
  514.0 5.8 all-to-all-start.7
  530.7 6.6 collective-permute-done.14
  541.0 4.5 reduce.11
  547.6 4.5 reduce.10
  555.6 7.8 fusion.96
  563.4 5.9 fusion.106
  576.2 5.2 collective-permute-done.7
  581.9 14.3 %while.33 = (s32[]{:T(128)}, f32[4,3,256]{2,1,0:T(4,128)S(1)}, s32[]{:T(128)}, f32[3,256]{1,0:T(4,128)S(1)}, f32[4,3,256]{2,1,0:T(4,128)S(1)}, /*index=5*/f32[4,...) while((s32[]{:T(128)}, f32[4,3,256]{2,1,0:T(4,128)S(1)}, ...), condition=%wide.region_11.12_spmd, body=%wide.region_1.11_spmd.sunk | while | flops 6887653 | bytes 77137 | solution.py:194
  596.2 54.9 %collective-permute-done.12 = f32[3,8,64,256]{3,2,1,0:T(8,128)} collective-permute-done((f32[3,8,64,256]{3,2,1,0:T(8,128)S(1)}, f32[3,8,64,256]{3,2,1,0:T(8,128)}, u32[]{:S(2)}, u32[]{:S(2)}) %collective-permute-start.12) | collective-permute-done | bytes 1572896 | tf_op jit(solution)/shard_map/ppermute | solution.py:40
  651.1 25.3 %collective-permute-done.13 = f32[3,8,64,256]{3,2,1,0:T(8,128)} collective-permute-done((f32[3,8,64,256]{3,2,1,0:T(8,128)S(1)}, f32[3,8,64,256]{3,2,1,0:T(8,128)}, u32[]{:S(2)}, u32[]{:S(2)}) %collective-permute-start.13) | collective-permute-done | bytes 1572896 | tf_op jit(solution)/shard_map/ppermute | solution.py:40
  676.4 5.8 fusion.95
  682.2 11.2 %while.35 = (s32[]{:T(128)}, f32[4,3,256]{2,1,0:T(4,128)S(1)}, s32[]{:T(128)}, f32[4,3]{1,0:T(4,128)S(1)}, f32[3,256]{1,0:T(4,128)S(1)}, /*index=5*/s32[4,3]{1,0...) while((s32[]{:T(128)}, f32[4,3,256]{2,1,0:T(4,128)S(1)}, ...), condition=%wide.region_15.16_spmd, body=%wide.region_14.15_spmd.sunk | while | flops 38192752 | bytes 738113 | solution.py:297
  694.3 4.8 collective-permute-start.19
  700.1 27.3 %collective-permute-done.19 = f32[2,2,3]{2,1,0:T(2,128)S(1)} collective-permute-done((f32[2,2,3]{2,1,0:T(2,128)S(1)}, f32[2,2,3]{2,1,0:T(2,128)S(1)}, u32[]{:S(2)}, u32[]{:S(2)}) %collective-permute-start.19) | collective-permute-done | bytes 80 | tf_op jit(solution)/shard_map/ppermute | solution.py:32
  727.4 12.6 %collective-permute-start.20 = (f32[6,2,3]{2,1,0:T(2,128)S(1)}, f32[6,2,3]{2,1,0:T(2,128)S(1)}, u32[]{:S(2)}, u32[]{:S(2)}) collective-permute-start(f32[6,2,3]{2,1,0:T(2,128)S(1)} %pad_maximum_fusion.18), channel_id=1, source_target_pairs={{0,1},{1,2},{2,3},{3,4},{4,5},{5,6},{6,7},{7,0},{8,9},{9,10},{10,1... | collective-permute-start | bytes 440 | tf_op jit(solution)/shard_map/ppermute | solution.py:29
  756.6 5.1 collective-permute-start.27
  769.8 5.1 collective-permute-start.31
  780.1 5.2 collective-permute-start.35
  793.9 5.1 collective-permute-start.39
  805.4 5.2 collective-permute-start.43
  820.0 5.1 collective-permute-start.47
  831.4 5.2 collective-permute-start.51
  846.0 5.1 collective-permute-start.55
  857.4 5.2 collective-permute-start.59
  872.0 5.1 collective-permute-start.63
  (451 shorter events, 296.2 us)
Async XLA Ops:
  57.0 104.8 %collective-permute-start.8 = (f32[3,8,64,256]{3,2,1,0:T(8,128)S(1)}, f32[3,8,64,256]{3,2,1,0:T(8,128)S(1)}, u32[]{:S(2)}, u32[]{:S(2)}) collective-permute-start(f32[3,8,64,256]{3,2,1,0:T(8,128)S(1)} %get-tuple-element.452), channel_id=1, source_target_pairs={{248,0},{0,8},{8,16},{16,24},{24,32},{32,40},{40,48},{48,56},{56,6... | collective-permute-start | bytes 4718600 | tf_op jit(solution)/shard_map/ppermute | solution.py:40
  59.2 102.7 %collective-permute-start.9 = (f32[3,8,64,256]{3,2,1,0:T(8,128)S(1)}, f32[3,8,64,256]{3,2,1,0:T(8,128)S(1)}, u32[]{:S(2)}, u32[]{:S(2)}) collective-permute-start(f32[3,8,64,256]{3,2,1,0:T(8,128)S(1)} %get-tuple-element.453), channel_id=1, source_target_pairs={{240,0},{248,8},{0,16},{8,24},{16,32},{24,40},{32,48},{40,56},{48,... | collective-permute-start | bytes 4718600 | tf_op jit(solution)/shard_map/ppermute | solution.py:40
  163.9 35.3 %collective-permute-start.10 = (f32[3,8,32,256]{3,2,1,0:T(8,128)S(1)}, f32[3,8,32,256]{3,2,1,0:T(8,128)S(1)}, u32[]{:S(2)}, u32[]{:S(2)}) collective-permute-start(f32[3,8,32,256]{3,2,1,0:T(8,128)S(1)} %slice.744), channel_id=1, source_target_pairs={{7,0},{0,1},{1,2},{2,3},{3,4},{4,5},{5,6},{6,7},{15,8},{8,9},{9,10... | collective-permute-start | bytes 2359304 | tf_op jit(solution)/shard_map/ppermute | solution.py:40
  207.1 103.0 %all-to-all-start.1 = ((f32[32,1,6144]{2,1,0:T(1,128)}), f32[32,1,6144]{2,1,0:T(1,128)}, u32[]{:S(2)}, u32[]{:S(2)}) async-start(f32[32,1,6144]{2,1,0:T(1,128)} %reshape.1592), calls=%async_computation.1 | async-start | bytes 1572864 | tf_op jit(solution)/shard_map/all_to_all | solution.py:248
  310.1 25.2 %all-to-all-start = ((f32[32,1,6144]{2,1,0:T(1,128)}), f32[32,1,6144]{2,1,0:T(1,128)}, u32[]{:S(2)}, u32[]{:S(2)}) async-start(f32[32,1,6144]{2,1,0:T(1,128)} %reshape.1594), calls=%async_computation | async-start | bytes 1572864 | tf_op jit(solution)/shard_map/all_to_all | solution.py:247
  354.8 24.7 %all-to-all-start.3 = ((f32[8,1,24576]{2,1,0:T(1,128)}), f32[8,1,24576]{2,1,0:T(1,128)}, u32[]{:S(2)}, u32[]{:S(2)}) async-start(f32[8,1,24576]{2,1,0:T(1,128)} %reshape.1596), calls=%async_computation.3 | async-start | bytes 1572864 | tf_op jit(solution)/shard_map/all_to_all | solution.py:255
  379.5 21.0 %all-to-all-start.2 = ((f32[8,1,24576]{2,1,0:T(1,128)}), f32[8,1,24576]{2,1,0:T(1,128)}, u32[]{:S(2)}, u32[]{:S(2)}) async-start(f32[8,1,24576]{2,1,0:T(1,128)} %reshape.1598), calls=%async_computation.2 | async-start | bytes 1572864 | tf_op jit(solution)/shard_map/all_to_all | solution.py:254
  428.4 17.8 %all-to-all-start.4 = ((f32[8,1,24576]{2,1,0:T(1,128)}), f32[8,1,24576]{2,1,0:T(1,128)}, u32[]{:S(2)}, u32[]{:S(2)}) async-start(f32[8,1,24576]{2,1,0:T(1,128)} %reshape.1602), calls=%async_computation.4 | async-start | bytes 1572864 | tf_op jit(solution)/shard_map/all_to_all | solution.py:270
  446.2 20.4 %all-to-all-start.5 = ((f32[8,1,24576]{2,1,0:T(1,128)}), f32[8,1,24576]{2,1,0:T(1,128)}, u32[]{:S(2)}, u32[]{:S(2)}) async-start(f32[8,1,24576]{2,1,0:T(1,128)} %reshape.1600), calls=%async_computation.5 | async-start | bytes 1572864 | tf_op jit(solution)/shard_map/all_to_all | solution.py:271
  487.2 26.8 %all-to-all-start.6 = ((f32[32,1,6144]{2,1,0:T(1,128)}), f32[32,1,6144]{2,1,0:T(1,128)}, u32[]{:S(2)}, u32[]{:S(2)}) async-start(f32[32,1,6144]{2,1,0:T(1,128)} %reshape.1606), calls=%async_computation.6 | async-start | bytes 1572864 | tf_op jit(solution)/shard_map/all_to_all | solution.py:275
  492.4 77.0 %collective-permute-start.4 = (f32[2,2,3,256]{3,2,1,0:T(4,128)S(1)}, f32[2,2,3,256]{3,2,1,0:T(4,128)S(1)}, u32[]{:S(2)}, u32[]{:S(2)}) collective-permute-start(f32[2,2,3,256]{3,2,1,0:T(4,128)S(1)} %bitcast.418), channel_id=1, source_target_pairs={{0,8},{8,16},{16,24},{24,32},{32,40},{40,48},{48,56},{56,64},{64,7... | collective-permute-start | bytes 36872 | tf_op jit(solution)/shard_map/ppermute | solution.py:29
  494.1 77.1 %collective-permute-start.5 = (f32[2,2,3,256]{3,2,1,0:T(4,128)S(1)}, f32[2,2,3,256]{3,2,1,0:T(4,128)S(1)}, u32[]{:S(2)}, u32[]{:S(2)}) collective-permute-start(f32[2,2,3,256]{3,2,1,0:T(4,128)S(1)} %bitcast.419), channel_id=1, source_target_pairs={{8,0},{16,8},{24,16},{32,24},{40,32},{48,40},{56,48},{64,56},{72,6... | collective-permute-start | bytes 36872 | tf_op jit(solution)/shard_map/ppermute | solution.py:32
  497.7 25.3 %collective-permute-start = (f32[2,2,3]{2,1,0:T(2,128)S(1)}, f32[2,2,3]{2,1,0:T(2,128)S(1)}, u32[]{:S(2)}, u32[]{:S(2)}) collective-permute-start(f32[2,2,3]{2,1,0:T(2,128)S(1)} %bitcast.458), channel_id=1, source_target_pairs={{0,8},{8,16},{16,24},{24,32},{32,40},{40,48},{48,56},{56,64},{64,7... | collective-permute-start | bytes 152 | tf_op jit(solution)/shard_map/ppermute | solution.py:29
  497.7 29.2 %collective-permute-start.1 = (f32[2,2,3]{2,1,0:T(2,128)S(1)}, f32[2,2,3]{2,1,0:T(2,128)S(1)}, u32[]{:S(2)}, u32[]{:S(2)}) collective-permute-start(f32[2,2,3]{2,1,0:T(2,128)S(1)} %bitcast.459), channel_id=1, source_target_pairs={{8,0},{16,8},{24,16},{32,24},{40,32},{48,40},{56,48},{64,56},{72,6... | collective-permute-start | bytes 152 | tf_op jit(solution)/shard_map/ppermute | solution.py:32
  514.0 33.6 %all-to-all-start.7 = ((f32[32,1,6144]{2,1,0:T(1,128)}), f32[32,1,6144]{2,1,0:T(1,128)}, u32[]{:S(2)}, u32[]{:S(2)}) async-start(f32[32,1,6144]{2,1,0:T(1,128)} %reshape.1604), calls=%async_computation.7 | async-start | bytes 1572864 | tf_op jit(solution)/shard_map/all_to_all | solution.py:276
  521.7 15.6 %collective-permute-start.14 = (f32[2,6,3]{2,1,0:T(8,128)S(1)}, f32[2,6,3]{2,1,0:T(8,128)S(1)}, u32[]{:S(2)}, u32[]{:S(2)}) collective-permute-start(f32[2,6,3]{2,1,0:T(8,128)S(1)} %reshape.1537), channel_id=1, source_target_pairs={{0,8},{8,16},{16,24},{24,32},{32,40},{40,48},{48,56},{56,64},{64,7... | collective-permute-start | bytes 440 | tf_op jit(solution)/shard_map/ppermute | solution.py:29
  523.0 18.0 %collective-permute-start.15 = (f32[2,6,3]{2,1,0:T(8,128)S(1)}, f32[2,6,3]{2,1,0:T(8,128)S(1)}, u32[]{:S(2)}, u32[]{:S(2)}) collective-permute-start(f32[2,6,3]{2,1,0:T(8,128)S(1)} %reshape.1538), channel_id=1, source_target_pairs={{8,0},{16,8},{24,16},{32,24},{40,32},{48,40},{56,48},{64,56},{72,6... | collective-permute-start | bytes 440 | tf_op jit(solution)/shard_map/ppermute | solution.py:32
  526.9 45.6 %collective-permute-start.2 = (f32[6,2,3]{2,1,0:T(2,128)S(1)}, f32[6,2,3]{2,1,0:T(2,128)S(1)}, u32[]{:S(2)}, u32[]{:S(2)}) collective-permute-start(f32[6,2,3]{2,1,0:T(2,128)S(1)} %constant_dynamic-update-slice_fusion), channel_id=1, source_target_pairs={{0,1},{1,2},{2,3},{3,4},{4,5},{5,6},{6,7},{7,0},{8,9},{9,10},{10,1... | collective-permute-start | bytes 440 | tf_op jit(solution)/shard_map/ppermute | solution.py:29
  537.2 35.8 %collective-permute-start.3 = (f32[6,2,3]{2,1,0:T(2,128)S(1)}, f32[6,2,3]{2,1,0:T(2,128)S(1)}, u32[]{:S(2)}, u32[]{:S(2)}) collective-permute-start(f32[6,2,3]{2,1,0:T(2,128)S(1)} %constant_dynamic-update-slice_fusion), channel_id=1, source_target_pairs={{1,0},{2,1},{3,2},{4,3},{5,4},{6,5},{7,6},{0,7},{9,8},{10,9},{11,1... | collective-permute-start | bytes 440 | tf_op jit(solution)/shard_map/ppermute | solution.py:32
  569.4 12.1 %collective-permute-start.11 = (f32[3,8,32,256]{3,2,1,0:T(8,128)S(1)}, f32[3,8,32,256]{3,2,1,0:T(8,128)S(1)}, u32[]{:S(2)}, u32[]{:S(2)}) collective-permute-start(f32[3,8,32,256]{3,2,1,0:T(8,128)S(1)} %fusion.106), channel_id=1, source_target_pairs={{1,0},{2,1},{3,2},{4,3},{5,4},{6,5},{7,6},{0,7},{9,8},{10,9},{11,1... | collective-permute-start | bytes 2359304 | tf_op jit(solution)/shard_map/ppermute | solution.py:40
  569.5 124.1 %collective-permute-start.16 = (f32[10,2,3]{2,1,0:T(2,128)S(1)}, f32[10,2,3]{2,1,0:T(2,128)S(1)}, u32[]{:S(2)}, u32[]{:S(2)}) collective-permute-start(f32[10,2,3]{2,1,0:T(2,128)S(1)} %get-tuple-element.470), channel_id=1, source_target_pairs={{0,1},{1,2},{2,3},{3,4},{4,5},{5,6},{6,7},{7,0},{8,9},{9,10},{10,1... | collective-permute-start | bytes 728 | tf_op jit(solution)/shard_map/ppermute | solution.py:29
  571.2 122.3 %collective-permute-start.17 = (f32[10,2,3]{2,1,0:T(2,128)S(1)}, f32[10,2,3]{2,1,0:T(2,128)}, u32[]{:S(2)}, u32[]{:S(2)}) collective-permute-start(f32[10,2,3]{2,1,0:T(2,128)S(1)} %get-tuple-element.471), channel_id=1, source_target_pairs={{1,0},{2,1},{3,2},{4,3},{5,4},{6,5},{7,6},{0,7},{9,8},{10,9},{11,1... | collective-permute-start | bytes 728 | tf_op jit(solution)/shard_map/ppermute | solution.py:32
  573.0 8.5 collective-permute-start.7
  581.6 69.4 %collective-permute-start.12 = (f32[3,8,64,256]{3,2,1,0:T(8,128)S(1)}, f32[3,8,64,256]{3,2,1,0:T(8,128)}, u32[]{:S(2)}, u32[]{:S(2)}) collective-permute-start(f32[3,8,64,256]{3,2,1,0:T(8,128)S(1)} %pad_maximum_fusion.3), channel_id=1, source_target_pairs={{8,0},{16,8},{24,16},{32,24},{40,32},{48,40},{56,48},{64,56},{72,6... | collective-permute-start | bytes 4718600 | tf_op jit(solution)/shard_map/ppermute | solution.py:40
  581.7 94.6 %collective-permute-start.13 = (f32[3,8,64,256]{3,2,1,0:T(8,128)S(1)}, f32[3,8,64,256]{3,2,1,0:T(8,128)}, u32[]{:S(2)}, u32[]{:S(2)}) collective-permute-start(f32[3,8,64,256]{3,2,1,0:T(8,128)S(1)} %pad_maximum_fusion.3), channel_id=1, source_target_pairs={{16,0},{24,8},{32,16},{40,24},{48,32},{56,40},{64,48},{72,56},{80,... | collective-permute-start | bytes 4718600 | tf_op jit(solution)/shard_map/ppermute | solution.py:40
  694.3 33.1 %collective-permute-start.19 = (f32[2,2,3]{2,1,0:T(2,128)S(1)}, f32[2,2,3]{2,1,0:T(2,128)S(1)}, u32[]{:S(2)}, u32[]{:S(2)}) collective-permute-start(f32[2,2,3]{2,1,0:T(2,128)S(1)} %fusion.239), channel_id=1, source_target_pairs={{8,0},{16,8},{24,16},{32,24},{40,32},{48,40},{56,48},{64,56},{72,6... | collective-permute-start | bytes 152 | tf_op jit(solution)/shard_map/ppermute | solution.py:32
  727.4 13.4 %collective-permute-start.20 = (f32[6,2,3]{2,1,0:T(2,128)S(1)}, f32[6,2,3]{2,1,0:T(2,128)S(1)}, u32[]{:S(2)}, u32[]{:S(2)}) collective-permute-start(f32[6,2,3]{2,1,0:T(2,128)S(1)} %pad_maximum_fusion.18), channel_id=1, source_target_pairs={{0,1},{1,2},{2,3},{3,4},{4,5},{5,6},{6,7},{7,0},{8,9},{9,10},{10,1... | collective-permute-start | bytes 440 | tf_op jit(solution)/shard_map/ppermute | solution.py:29
  746.2 5.9 collective-permute-start.22
  756.5 6.1 collective-permute-start.26
  756.6 6.0 collective-permute-start.27
  769.7 6.1 collective-permute-start.30
  769.8 6.0 collective-permute-start.31
  780.0 6.1 collective-permute-start.34
  780.1 6.1 collective-permute-start.35
  793.7 6.3 collective-permute-start.38
  793.9 6.0 collective-permute-start.39
  805.3 6.2 collective-permute-start.42
  805.4 6.1 collective-permute-start.43
  819.9 6.1 collective-permute-start.46
  820.0 6.0 collective-permute-start.47
  831.3 6.2 collective-permute-start.50
  831.4 6.1 collective-permute-start.51
  845.9 6.1 collective-permute-start.54
  846.0 6.0 collective-permute-start.55
  857.3 6.2 collective-permute-start.58
  857.4 6.1 collective-permute-start.59
  871.9 6.1 collective-permute-start.62
  872.0 6.0 collective-permute-start.63
  (58 other events, 476.9 us)
where the time goes:
time: 898 us; the launch traced here: 884 us
  starting transfers between devices  364 us (41%)
  waiting for transfers between devices  217 us (24%)
  local copies, waits for them, and re-layouts  148 us (16%)
  other arithmetic  67.5 us (8%)
  matrix products  64.7 us (7%)
  loops' own time  20.4 us (2%)
    ppermute x6, waiting for transfers between devices, from_behind(): return lax.ppermute(block, axis, route)  130 us
    ppermute x30, starting transfers between devices, extended_2(): lax.ppermute(lax.slice_in_dim(block, 0, width, axis=dim), axis, backward)  113 us
    ppermute x6, starting transfers between devices, from_behind(): return lax.ppermute(block, axis, route)  90.7 us
    all_to_all x1, starting transfers between devices, local(): lax.all_to_all(spec_imag, 'wide', split_axis=3, concat_axis=1, tiled=True)  84.9 us
    dot_general x20, matrix products, along(): jnp.einsum(letters + ',' + letters[dimension] + 't->' + output, values, t...  60.4 us
    ppermute x30, waiting for transfers between devices, extended_2(): lax.ppermute(lax.slice_in_dim(block, 0, width, axis=dim), axis, backward)  42 us
    unnamed x100, local copies, waits for them, and re-layouts  40.5 us
    ppermute x30, starting transfers between devices, extended_2(): lax.ppermute(lax.slice_in_dim(block, block.shape[dim] - width, None, axis...  29.1 us
  transfers between devices with their start and end apart: 74, of which 48 were waited for; matrix products, arithmetic and copies ran while one was open for 14% of the time, Pallas kernels for 0%

commit v1 on v0

v1 whole, which is shorter than its diff:
```python
import functools

import jax
import jax.numpy as jnp
import ml_dtypes
import numpy as np
from jax import lax
from jax.experimental import pallas as pl
from jax.experimental.pallas import tpu as pltpu
from jax.sharding import PartitionSpec as P

NODES = 256
GRID = 256
BLOCK = 16
NEAR = 2
SWEEPS = 6
SLOTS_DEV = 4

soften = 1.0
screen = 0.0625
near_scale = 0.05
spread_norm = 0.17958712212516656
mobility = 0.2
time_step = 0.5
relaxation = 0.35
ewald_split = 0.5

MESH = pl.DeviceIdType.MESH
F32 = jnp.float32
BF16 = jnp.bfloat16
VMEM_SPEC = pl.BlockSpec(memory_space=pltpu.VMEM)
SMEM_SPEC = pl.BlockSpec(memory_space=pltpu.SMEM)


def params(collective_id=None, limit=40):
    if collective_id is None:
        return pltpu.CompilerParams(vmem_limit_bytes=limit * 2**20)
    return pltpu.CompilerParams(
        vmem_limit_bytes=limit * 2**20, collective_id=collective_id, has_side_effects=True
    )


def trig_table(group):
    cell = np.arange(GRID)
    rows = []
    for first in range(0, GRID // 2, group):
        for half in (0, 1):
            for k in range(first, first + group):
                angle = 2.0 * np.pi / GRID * (k * cell % GRID)
                if half == 0:
                    rows.append(np.cos(angle))
                elif k == 0:
                    rows.append(np.cos(np.pi * cell))
                else:
                    rows.append(np.sin(angle))
    return np.stack(rows)


def halves(table):
    high = table.astype(np.float32).astype(ml_dtypes.bfloat16)
    low = (table - high.astype(np.float64)).astype(np.float32).astype(ml_dtypes.bfloat16)
    return high, low


def split(values):
    high = values.astype(BF16)
    return high, (values - high.astype(F32)).astype(BF16)


def dot(a, b, contract=((1,), (0,))):
    return lax.dot_general(a, b, (contract, ((), ())), preferred_element_type=F32)


def dot3(a, b):
    return dot(a[0], b[0]) + (dot(a[0], b[1]) + dot(a[1], b[0]))


def lanes_of(shape):
    return lax.broadcasted_iota(jnp.int32, shape, len(shape) - 1)


def roll(values, shift):
    return pltpu.roll(values, shift, len(values.shape) - 1)


def pack_lanes(u0, u1, u2, u3):
    lane = lanes_of(u0.shape)
    r1, r2, r3 = roll(u1, 96), roll(u2, 64), roll(u3, 32)
    return (
        jnp.where(lane < 96, u0, r1),
        jnp.where(lane < 64, r1, r2),
        jnp.where(lane < 32, r2, r3),
    )


def unpack_lanes(p0, p1, p2):
    lane = lanes_of(p0.shape)
    return (
        p0,
        roll(jnp.where(lane < 64, p1, p0), 32),
        roll(jnp.where(lane < 32, p2, p1), 64),
        roll(p2, 96),
    )


def greet(wide_count, narrow_count, offsets):
    w, n = lax.axis_index("wide"), lax.axis_index("narrow")
    barrier = pltpu.get_barrier_semaphore()
    for dw, dn in offsets:
        pl.semaphore_signal(
            barrier,
            inc=1,
            device_id=(
                lax.rem(w + dw + wide_count, wide_count),
                lax.rem(n + dn + narrow_count, narrow_count),
            ),
            device_id_type=MESH,
        )
    pl.semaphore_wait(barrier, len(offsets))


GATHER = [(dw, dn) for dw in (-2, -1, 0, 1) for dn in (-1, 0, 1)]


def gather_kernel(wide_count, narrow_count, own_ref, out_ref, held, send_sem, recv_sem):
    w, n = lax.axis_index("wide"), lax.axis_index("narrow")
    reach = [(dw, dn) for dw in (-2, -1, 0, 1, 2) for dn in (-1, 0, 1) if (dw, dn) != (0, 0)]
    greet(wide_count, narrow_count, reach)
    copies = []
    for place, (dw, dn) in enumerate(GATHER):
        if (dw, dn) == (0, 0):
            continue
        copy = pltpu.make_async_remote_copy(
            src_ref=own_ref,
            dst_ref=held.at[place],
            send_sem=send_sem.at[place],
            recv_sem=recv_sem.at[place],
            device_id=(
                lax.rem(w - dw + wide_count, wide_count),
                lax.rem(n - dn + narrow_count, narrow_count),
            ),
            device_id_type=MESH,
        )
        copy.start()
        copies.append((place, copy))
    out_ref[GATHER.index((0, 0))] = own_ref[...]
    for place, copy in copies:
        copy.wait_recv()
        out_ref[place] = held[place]
    for place, copy in copies:
        copy.wait_send()


def near_kernel(wide_count, narrow_count, list_ref, meta_ref, held_ref, off_ref, out_ref, offcol, source, columns):
    w, n = lax.axis_index("wide"), lax.axis_index("narrow")
    own = GATHER.index((0, 0))
    out_ref[...] = jnp.zeros_like(out_ref)
    columns[...] = jnp.zeros_like(columns)
    padded = jnp.concatenate([off_ref[...], jnp.zeros((5, NODES), F32)], axis=0)
    turned = jnp.transpose(padded)
    for c in range(3):
        offcol[c] = jnp.broadcast_to(turned[:, c : c + 1], (NODES, 128))

    for s in range(SLOTS_DEV):

        @pl.when(meta_ref[own, 24 + s] > 0.5)
        def _():
            for j in range(1 + NEAR):
                if j == 0:
                    place, within = own, s
                else:
                    entry = list_ref[s, j - 1]
                    holder = entry // SLOTS_DEV
                    within = entry % SLOTS_DEV
                    row = lax.rem(holder // narrow_count - w + 1 + wide_count, wide_count)
                    column = lax.rem(lax.rem(holder, narrow_count) - n + 1 + narrow_count, narrow_count)
                    place = (row + 1) * 3 + column
                for c in range(3):
                    if j == 0:
                        shift = 0.0
                    else:
                        e = meta_ref[own, 3 * s + c] - meta_ref[place, 3 * within + c]
                        shift = e - jnp.where(e >= 128.0, 256.0, jnp.where(e < -128.0, -256.0, 0.0))
                    source[j, c : c + 1, :] = shift - off_ref[c : c + 1, :]
                    source[j, 3 + c : 4 + c, :] = held_ref[place, pl.ds(within * 3 + c, 1), :]

            def chunk(i, carry):
                rows = pl.ds(pl.multiple_of(i * 8, 8), 8)
                sums = [jnp.zeros((8, 128), F32) for _ in range(3)]
                at = [offcol[c, rows, :] for c in range(3)]
                for j in range(1 + NEAR):
                    for half in (0, 1):
                        lanes = slice(half * 128, half * 128 + 128)
                        d = [at[c] + source[j, c : c + 1, lanes] for c in range(3)]
                        f = [source[j, 3 + c : 4 + c, lanes] for c in range(3)]
                        r2 = d[0] * d[0] + d[1] * d[1] + d[2] * d[2]
                        inverse = lax.rsqrt(r2 + soften)
                        weight = jnp.exp(r2 * (-screen)) * (inverse * inverse * inverse)
                        along = (d[0] * f[0] + d[1] * f[1] + d[2] * f[2]) * weight
                        diagonal = (r2 + 2.0 * soften) * weight
                        for c in range(3):
                            sums[c] = sums[c] + (diagonal * f[c] + d[c] * along)
                for c in range(3):
                    columns[rows, c : c + 1] = jnp.sum(sums[c], axis=1, keepdims=True)
                return carry

            lax.fori_loop(0, NODES // 8, chunk, 0)
            result = jnp.transpose(columns[...])
            out_ref[3 * s : 3 * s + 3, :] = near_scale * result[0:3, :]


def sphere_weights(wide_count, narrow_count, index, meta_ref, off_ref):
    w, n = lax.axis_index("wide"), lax.axis_index("narrow")
    size_x, size_y = GRID // wide_count, GRID // narrow_count
    dw = index // 8 - 2
    dn = (index // 4) % 2 - 1
    s = index % 4
    place = (dw + 2) * 3 + dn + 1
    anchor = [meta_ref[place, 12 + 3 * s + c].astype(jnp.int32) for c in range(3)]
    centre = [meta_ref[place, 3 * s + c] for c in range(3)]
    low_x = anchor[0] - size_x * lax.rem(w + dw + wide_count, wide_count) + size_x * dw
    low_y = anchor[1] - size_y * lax.rem(n + dn + narrow_count, narrow_count) + size_y * dn
    active = (meta_ref[place, 24 + s] > 0.5) & (low_x + BLOCK > 0) & (low_y + BLOCK > 0)

    def weights(c, low, count):
        cell = lax.broadcasted_iota(jnp.int32, (count, NODES), 0)
        position = centre[c] + off_ref[c : c + 1, :]
        distance = position - ((anchor[c] - low) + cell).astype(F32)
        inside = (cell >= low) & (cell < low + BLOCK)
        return jnp.where(inside, jnp.exp(-distance * distance), 0.0)

    return (
        place,
        s,
        active,
        anchor[2],
        lambda: (weights(0, low_x, size_x), weights(1, low_y, size_y), weights(2, anchor[2] % 8, 32)),
    )


def stacked(values, second):
    high, low = split(values)
    return jnp.concatenate([high, low, high] if second else [high, high, low], axis=0)


def spread_kernel(wide_count, narrow_count, meta_ref, held_ref, off_ref, tz_ref, out_ref, a_high, a_low, total, turned):
    total[...] = jnp.zeros_like(total)

    def sphere(index, carry):
        place, s, active, low_z, weights = sphere_weights(wide_count, narrow_count, index, meta_ref, off_ref)

        @pl.when(active)
        def _():
            wx, wy, wz = weights()
            table = tz_ref[pl.ds(pl.multiple_of(low_z // 8 * 8, 8), 32), :]
            along_z = split(
                dot(jnp.transpose(stacked(wz, False).astype(F32)).astype(BF16), stacked(table, True))
            )
            planar = jnp.concatenate(
                [
                    wy * (spread_norm * held_ref[place, pl.ds(s * 3 + c, 1), :])
                    for c in range(3)
                ],
                axis=0,
            )
            for x in range(8):
                high, low = split(planar * wx[x : x + 1, :])
                a_high[x * 96 : x * 96 + 96, :] = high
                a_low[x * 96 : x * 96 + 96, :] = low
            total[...] += dot3((a_high[...], a_low[...]), along_z)

        return carry

    lax.fori_loop(0, 24, sphere, 0)
    for x in range(8):
        block = jnp.concatenate([total[x * 96 : x * 96 + 96, :], jnp.zeros((32, GRID), F32)], axis=0)
        turned[pl.ds(x, GRID, stride=8), :] = jnp.transpose(block)
    values = turned[...].reshape(64, 4, 8, 128)
    packed = pack_lanes(*[values[:, j] for j in range(4)])
    for g in range(3):
        out_ref[:, :, :, g * 128 : g * 128 + 128] = packed[g].reshape(32, 2, 8, 128)


def interp_kernel(wide_count, narrow_count, meta_ref, off_ref, tz_ref, mesh_ref, out_ref, m_high, m_low, turned):
    out_ref[...] = jnp.zeros_like(out_ref)
    groups = [mesh_ref[:, :, :, g * 128 : g * 128 + 128].reshape(64, 8, 128) for g in range(3)]
    unpacked = unpack_lanes(*groups)
    turned[...] = jnp.stack(unpacked, axis=1).reshape(GRID * 8, 128)
    for x in range(8):
        block = jnp.transpose(turned[pl.ds(x, GRID, stride=8), :])
        high, low = split(block[:96])
        m_high[x * 96 : x * 96 + 96, :] = high
        m_low[x * 96 : x * 96 + 96, :] = low

    def sphere(index, carry):
        place, s, active, low_z, weights = sphere_weights(wide_count, narrow_count, index, meta_ref, off_ref)

        @pl.when(active)
        def _():
            wx, wy, wz = weights()
            table = tz_ref[pl.ds(pl.multiple_of(low_z // 8 * 8, 8), 32), :]
            along_z = split(
                dot(jnp.transpose(stacked(table, True).astype(F32)).astype(BF16), stacked(wz, False))
            )
            found = dot3((m_high[...], m_low[...]), along_z)
            summed = found[0:96] * wx[0:1, :]
            for x in range(1, 8):
                summed = summed + found[x * 96 : x * 96 + 96] * wx[x : x + 1, :]
            rows = [
                jnp.sum(summed[c * 32 : c * 32 + 32] * wy, axis=0, keepdims=True) * spread_norm
                for c in range(3)
            ]
            owner = index // 4
            for c in range(3):
                out_ref[owner, pl.ds(s * 3 + c, 1), :] = rows[c]

        return carry

    lax.fori_loop(0, 24, sphere, 0)


def exchange(axis, count, source, target, send_sem, recv_sem, me, other):
    def copy_to(step):
        to = lax.rem(me + step, count)
        device = (to, other) if axis == "wide" else (other, to)
        return pltpu.make_async_remote_copy(
            src_ref=source.at[to],
            dst_ref=target.at[me],
            send_sem=send_sem.at[step],
            recv_sem=recv_sem.at[step],
            device_id=device,
            device_id_type=MESH,
        )

    def begin(step, carry):
        copy_to(step).start()
        return carry

    def end(step, carry):
        copy_to(step).wait()
        return carry

    lax.fori_loop(1, count, begin, 0)
    target[me] = source[me]
    lax.fori_loop(1, count, end, 0)


def transform_kernel(
    wide_count,
    narrow_count,
    mesh_ref,
    tx_high,
    tx_low,
    ix_high,
    ix_low,
    ty_high,
    ty_low,
    iy_high,
    iy_low,
    out_ref,
    wide_in,
    narrow_out,
    narrow_in,
    narrow_back,
    narrow_home,
    wide_back,
    wide_home,
    lines,
    spectrum,
    wide_send,
    wide_recv,
    narrow_send,
    narrow_recv,
):
    w, n = lax.axis_index("wide"), lax.axis_index("narrow")
    greet(
        wide_count,
        narrow_count,
        [(step, 0) for step in range(1, wide_count)] + [(0, step) for step in range(1, narrow_count)],
    )
    exchange("wide", wide_count, mesh_ref, wide_in, wide_send.at[0], wide_recv.at[0], w, n)
    for half in (0, 1):
        block = split(wide_in[:, half].reshape(GRID, 384))
        along = dot3((tx_high[...], tx_low[...]), block)
        narrow_out[:, half] = along.reshape(narrow_count, 32, 384)
    exchange("narrow", narrow_count, narrow_out, narrow_in, narrow_send.at[0], narrow_recv.at[0], n, w)
    for half in (0, 1):
        for source in range(8):
            groups = [narrow_in[source, half, :, g * 128 : g * 128 + 128] for g in range(3)]
            unpacked = unpack_lanes(*groups)
            for j in range(4):
                lines[half * 128 + j * 32 : half * 128 + j * 32 + 32, source * 128 : source * 128 + 128] = unpacked[j]
    for half in (0, 1):
        rows = slice(half * 128, half * 128 + 128)
        spectrum[rows, :] = dot3(split(lines[rows, :]), (ty_high[...], ty_low[...]))

    row = lax.broadcasted_iota(jnp.int32, (32, 1), 0)
    k_x = (n * 16 + row % 16).astype(F32)
    nyquist_x = jnp.where((row >= 16) & (k_x < 0.5), 128.0, 0.0)
    lane = lax.broadcasted_iota(jnp.int32, (1, GRID), 1)
    k_y = (lane % 128).astype(F32)
    nyquist_y = jnp.where((lane >= 128) & (k_y < 0.5), 128.0, 0.0)
    square_xy = k_x * k_x + nyquist_x * nyquist_x + (k_y * k_y + nyquist_y * nyquist_y)
    scale_x = jnp.where(k_x < 0.5, 1.0, 2.0)
    scale_y = jnp.where(k_y < 0.5, 1.0, 2.0)
    scale_xy = scale_x * scale_y
    damping = (ewald_split * np.pi / GRID) ** 2
    constant = GRID * GRID / (4.0 * np.pi * np.pi) / float(GRID) ** 3
    turn_x = jnp.where(row < 16, k_x, -k_x)
    turn_y = jnp.where(lane < 128, k_y, -k_y)

    def derive_x(values):
        return turn_x * jnp.concatenate([values[16:], values[:16]], axis=0)

    def derive_y(values):
        return turn_y * jnp.concatenate([values[:, 128:], values[:, :128]], axis=1)

    def filtered(j, carry):
        k_z = (w * 4 + j).astype(F32)
        bases = [pl.multiple_of(half * 128 + j * 32, 32) for half in (0, 1)]
        fields = [
            [spectrum[pl.ds(bases[half], 32), c * 256 : c * 256 + 256] for c in range(3)]
            for half in (0, 1)
        ]
        flows = []
        nyquists_z = [jnp.zeros_like(k_z), jnp.where(k_z < 0.5, 128.0, 0.0)]
        scale_z = jnp.where(k_z < 0.5, 1.0, 2.0)
        turn_z = (k_z, -k_z)
        for half in (0, 1):
            values = fields[half]
            flows.append(derive_x(values[0]) + derive_y(values[1]) + turn_z[half] * fields[1 - half][2])
        for half in (0, 1):
            values = fields[half]
            nyquist_z = nyquists_z[half]
            square = square_xy + (k_z * k_z + nyquist_z * nyquist_z)
            safe = jnp.maximum(square, 1.0)
            inverse = 1.0 / safe
            factor = jnp.where(square > 0.5, jnp.exp(-damping * square) * inverse, 0.0)
            factor = factor * (scale_xy * (scale_z * constant))
            edge = (nyquist_x * values[0] + nyquist_y * values[1] + nyquist_z * values[2]) * inverse
            flow = [flows[half] * inverse, flows[1 - half] * inverse]
            gradient = [derive_x(flow[0]), derive_y(flow[0]), None]
            other_square = square_xy + (k_z * k_z + nyquists_z[1 - half] * nyquists_z[1 - half])
            gradient[2] = turn_z[half] * (flows[1 - half] * inverse)
            nyquist = (nyquist_x, nyquist_y, nyquist_z)
            for c in range(3):
                spectrum[pl.ds(bases[half], 32), c * 256 : c * 256 + 256] = factor * (
                    values[c] + gradient[c] - nyquist[c] * edge
                )
        return carry

    lax.fori_loop(0, 4, filtered, 0)
    for half in (0, 1):
        rows = slice(half * 128, half * 128 + 128)
        lines[rows, :] = dot3(split(spectrum[rows, :]), (iy_high[...], iy_low[...]))
    for half in (0, 1):
        for target in range(8):
            groups = [
                lines[half * 128 + j * 32 : half * 128 + j * 32 + 32, target * 128 : target * 128 + 128]
                for j in range(4)
            ]
            packed = pack_lanes(*groups)
            for g in range(3):
                narrow_back[target, half, :, g * 128 : g * 128 + 128] = packed[g]
    exchange("narrow", narrow_count, narrow_back, narrow_home, narrow_send.at[1], narrow_recv.at[1], n, w)
    for half in (0, 1):
        block = split(narrow_home[:, half].reshape(GRID, 384))
        along = dot3((ix_high[...], ix_low[...]), block)
        wide_back[:, half] = along.reshape(wide_count, 8, 384)
    exchange("wide", wide_count, wide_back, wide_home, wide_send.at[1], wide_recv.at[1], w, n)
    out_ref[...] = wide_home[...]


AROUND = [(dw, dn) for dw in (-1, 0, 1) for dn in (-1, 0, 1)]
PARTIAL = [(dw, dn) for dw in (-2, -1, 0) for dn in (-1, 0)]


def contact_kernel(
    wide_count,
    narrow_count,
    part_ref,
    near_ref,
    centre_ref,
    edge_ref,
    gap_ref,
    velocity_ref,
    force_ref,
    moved_ref,
    part_in,
    load_out,
    load_in,
    flow_out,
    flow_in,
    part_send,
    part_recv,
    load_send,
    load_recv,
    flow_send,
    flow_recv,
):
    w, n = lax.axis_index("wide"), lax.axis_index("narrow")

    def device(dw, dn):
        return (
            lax.rem(w + dw + wide_count, wide_count),
            lax.rem(n + dn + narrow_count, narrow_count),
        )

    greet(
        wide_count,
        narrow_count,
        [d for d in AROUND if d != (0, 0)] + [(-2, -1), (-2, 0), (2, 1), (2, 0)],
    )
    copies = []
    for place, (dw, dn) in enumerate(PARTIAL):
        if (dw, dn) == (0, 0):
            continue
        copy = pltpu.make_async_remote_copy(
            src_ref=part_ref.at[place],
            dst_ref=part_in.at[place],
            send_sem=part_send.at[place],
            recv_sem=part_recv.at[place],
            device_id=device(dw, dn),
            device_id_type=MESH,
        )
        copy.start()
        copies.append((place, copy))
    velocity = near_ref[...] + part_ref[PARTIAL.index((0, 0))]
    for place, copy in copies:
        copy.wait_recv()
        velocity = velocity + part_in[place]
    velocity_ref[...] = velocity
    hydro = jnp.broadcast_to(
        jnp.sum(velocity, axis=1, keepdims=True) * (1.0 / NODES), (16, 128)
    )

    def flow_copy(turn, place):
        dw, dn = AROUND[place]
        return pltpu.make_async_remote_copy(
            src_ref=flow_out.at[turn],
            dst_ref=flow_in.at[turn, 8 - place],
            send_sem=flow_send.at[turn, place],
            recv_sem=flow_recv.at[turn, 8 - place],
            device_id=device(dw, dn),
            device_id_type=MESH,
        )

    def load_copy(turn, place):
        dw, dn = AROUND[place]
        return pltpu.make_async_remote_copy(
            src_ref=load_out.at[turn, place],
            dst_ref=load_in.at[turn, 8 - place],
            send_sem=load_send.at[turn, place],
            recv_sem=load_recv.at[turn, 8 - place],
            device_id=device(dw, dn),
            device_id_type=MESH,
        )

    others = [place for place in range(9) if place != 4]

    def sweep(turn, carry):
        force, moving = carry
        flow_out[turn] = moving
        for place in others:
            flow_copy(turn, place).start()
        flow_in[turn, 4] = moving
        for place in others:
            flow_copy(turn, place).wait_recv()
        around = flow_in[turn].reshape(144, 128)
        relative = jnp.sum(edge_ref[...] * around, axis=0, keepdims=True)
        force = jnp.maximum(
            force
            - relaxation * (gap_ref[0:1, :] + time_step * relative) / (2.0 * time_step * mobility),
            0.0,
        )
        load = jnp.sum(edge_ref[...] * force, axis=1, keepdims=True)
        load_out[turn] = jnp.broadcast_to(load, (144, 128)).reshape(9, 16, 128)
        for place in others:
            load_copy(turn, place).start()
        summed = load_out[turn, 4]
        for place in others:
            load_copy(turn, place).wait_recv()
            summed = summed + load_in[turn, 8 - place]
        for place in others:
            load_copy(turn, place).wait_send()
            flow_copy(turn, place).wait_send()
        return force, hydro + mobility * summed

    force, moving = lax.fori_loop(0, SWEEPS, sweep, (jnp.zeros((1, 128), F32), hydro))
    force_ref[...] = jnp.broadcast_to(force, (8, 128))
    moved_ref[...] = centre_ref[...] + time_step * moving
    for place, copy in copies:
        copy.wait_send()


def local(
    wide_count,
    narrow_count,
    tractions,
    centers,
    node_offsets,
    occupied,
    anchors,
    near_list,
    contact_pairs,
    contact_gap,
    contact_angles,
):
    w, n = lax.axis_index("wide"), lax.axis_index("narrow")
    sizes = (wide_count, narrow_count)
    shape = jax.ShapeDtypeStruct
    dma = pltpu.SemaphoreType.DMA

    meta = jnp.concatenate(
        [
            centers.reshape(12),
            anchors.reshape(12).astype(F32),
            occupied.reshape(4).astype(F32),
            jnp.zeros((228,), F32),
        ]
    )
    own = jnp.concatenate([tractions.reshape(12, NODES), meta[None], jnp.zeros((3, NODES), F32)])
    held = pl.pallas_call(
        functools.partial(gather_kernel, *sizes),
        out_shape=shape((12, 16, NODES), F32),
        in_specs=[VMEM_SPEC],
        out_specs=VMEM_SPEC,
        scratch_shapes=[pltpu.VMEM((12, 16, NODES), F32), dma((12,)), dma((12,))],
        compiler_params=params(0),
        name="gather",
    )(own)
    metas = held[:, 12, :128]

    table_z = trig_table(4)
    wrapped_z = np.concatenate([table_z, table_z[:, :32]], axis=1).T.astype(np.float32)
    mesh = pl.pallas_call(
        functools.partial(spread_kernel, *sizes),
        out_shape=shape((32, 2, 8, 384), F32),
        in_specs=[SMEM_SPEC, VMEM_SPEC, VMEM_SPEC, VMEM_SPEC],
        out_specs=VMEM_SPEC,
        scratch_shapes=[
            pltpu.VMEM((768, NODES), BF16),
            pltpu.VMEM((768, NODES), BF16),
            pltpu.VMEM((768, GRID), F32),
            pltpu.VMEM((GRID * 8, 128), F32),
        ],
        compiler_params=params(),
        name="spread",
    )(metas, held, node_offsets, wrapped_z)

    table_x = trig_table(16)
    table_y = trig_table(128)
    wide_y = np.zeros((8, 128, 3, GRID))
    for c in range(3):
        wide_y[:, c * 32 : c * 32 + 32, c, :] = table_y.T.reshape(8, 32, GRID)
    wide_y = wide_y.reshape(1024, 768)
    mesh = pl.pallas_call(
        functools.partial(transform_kernel, *sizes),
        out_shape=shape((32, 2, 8, 384), F32),
        in_specs=[VMEM_SPEC] * 9,
        out_specs=VMEM_SPEC,
        scratch_shapes=[
            pltpu.VMEM((32, 2, 8, 384), F32),
            pltpu.VMEM((8, 2, 32, 384), F32),
            pltpu.VMEM((8, 2, 32, 384), F32),
            pltpu.VMEM((8, 2, 32, 384), F32),
            pltpu.VMEM((8, 2, 32, 384), F32),
            pltpu.VMEM((32, 2, 8, 384), F32),
            pltpu.VMEM((32, 2, 8, 384), F32),
            pltpu.VMEM((256, 1024), F32),
            pltpu.VMEM((256, 768), F32),
            dma((2, 32)),
            dma((2, 32)),
            dma((2, 8)),
            dma((2, 8)),
        ],
        compiler_params=params(1),
        name="transform",
    )(
        mesh,
        *halves(table_x),
        *halves(np.ascontiguousarray(table_x.T)),
        *halves(wide_y),
        *halves(np.ascontiguousarray(wide_y.T)),
    )

    part = pl.pallas_call(
        functools.partial(interp_kernel, *sizes),
        out_shape=shape((6, 16, NODES), F32),
        in_specs=[SMEM_SPEC, VMEM_SPEC, VMEM_SPEC, VMEM_SPEC],
        out_specs=VMEM_SPEC,
        scratch_shapes=[
            pltpu.VMEM((768, GRID), BF16),
            pltpu.VMEM((768, GRID), BF16),
            pltpu.VMEM((GRID * 8, 128), F32),
        ],
        compiler_params=params(),
        name="interpolate",
    )(metas, node_offsets, wrapped_z, mesh)

    near = pl.pallas_call(
        functools.partial(near_kernel, *sizes),
        out_shape=shape((16, NODES), F32),
        in_specs=[SMEM_SPEC, SMEM_SPEC, VMEM_SPEC, VMEM_SPEC],
        out_specs=VMEM_SPEC,
        scratch_shapes=[
            pltpu.VMEM((3, NODES, 128), F32),
            pltpu.VMEM((3, 8, NODES), F32),
            pltpu.VMEM((NODES, 8), F32),
        ],
        compiler_params=params(),
        name="near",
    )(near_list.reshape(4, NEAR), metas, held, node_offsets)

    polar, azimuth = contact_angles[0], contact_angles[1]
    normal = jnp.stack(
        [jnp.sin(polar) * jnp.cos(azimuth), jnp.sin(polar) * jnp.sin(azimuth), jnp.cos(polar)]
    )
    holder, within = contact_pairs // 4, contact_pairs % 4
    row_w = (holder // narrow_count - w + 1 + wide_count) % wide_count
    row_n = (holder % narrow_count - n + 1 + narrow_count) % narrow_count
    first_row = (row_w * 3 + row_n) * 16 + within * 3
    index = jnp.arange(144, dtype=jnp.int32)
    component = index % 16 % 3
    base = (index - component)[:, None]
    used = (index % 16 < 12)[:, None]
    sign = jnp.where(base == first_row[0][None, :], 1.0, 0.0) - jnp.where(
        base == first_row[1][None, :], 1.0, 0.0
    )
    spread_normal = jnp.where(
        (component == 0)[:, None],
        normal[0][None],
        jnp.where((component == 1)[:, None], normal[1][None], normal[2][None]),
    )
    edge = jnp.pad(jnp.where(used, sign * spread_normal, 0.0), ((0, 0), (0, 96)))
    gap = jnp.pad(jnp.broadcast_to(contact_gap[None], (8, 32)), ((0, 0), (0, 96)))
    centre_rows = jnp.broadcast_to(jnp.pad(centers.reshape(12, 1), ((0, 4), (0, 0))), (16, 128))
    velocity, force, moved = pl.pallas_call(
        functools.partial(contact_kernel, *sizes),
        out_shape=(shape((16, NODES), F32), shape((8, 128), F32), shape((16, 128), F32)),
        in_specs=[VMEM_SPEC] * 5,
        out_specs=(VMEM_SPEC,) * 3,
        scratch_shapes=[
            pltpu.VMEM((6, 16, NODES), F32),
            pltpu.VMEM((SWEEPS, 9, 16, 128), F32),
            pltpu.VMEM((SWEEPS, 9, 16, 128), F32),
            pltpu.VMEM((SWEEPS, 16, 128), F32),
            pltpu.VMEM((SWEEPS, 9, 16, 128), F32),
            dma((6,)),
            dma((6,)),
            dma((SWEEPS, 9)),
            dma((SWEEPS, 9)),
            dma((SWEEPS, 9)),
            dma((SWEEPS, 9)),
        ],
        compiler_params=params(2),
        name="contacts",
    )(part, near, centre_rows, edge, gap)
    return (
        velocity[:12].reshape(2, 2, 3, NODES),
        force[0, :32],
        moved[:12, 0].reshape(2, 2, 3),
    )


def solution(mesh):
    placed = (
        P("wide", "narrow", None, None),
        P("wide", "narrow", None),
        P(),
        P("wide", "narrow"),
        P("wide", "narrow", None),
        P("wide", "narrow", None),
        P(None, ("wide", "narrow")),
        P(("wide", "narrow")),
        P(None, ("wide", "narrow")),
    )
    return jax.shard_map(
        functools.partial(local, mesh.shape["wide"], mesh.shape["narrow"]),
        mesh=mesh,
        in_specs=placed,
        out_specs=(
            P("wide", "narrow", None, None),
            P(("wide", "narrow")),
            P("wide", "narrow", None),
        ),
        check_vma=False,
    )
```

time: 898 us -> 214 us (0.24); the launches traced: 884 us -> 213 us
  starting transfers between devices: 364 us -> 0 us
  waiting for transfers between devices: 217 us -> 0 us
  Pallas kernels: 0 us -> 194 us
  local copies, waits for them, and re-layouts: 148 us -> 15.4 us
  matrix products: 64.7 us -> 0 us
  other arithmetic: 67.5 us -> 3.33 us
  loops' own time: 20.4 us -> 0 us
    ppermute x66 -> x0, starting transfers between devices: 233 us -> none  [the longest x30 113 us: extended_2(): lax.ppermute(lax.slice_in_dim(block, 0, width, axis=dim), axis, backward)]
    ppermute x66 -> x0, waiting for transfers between devices: 198 us -> none  [the longest x6 130 us: from_behind(): return lax.ppermute(block, axis, route)]
    pallas_call x0 -> x6, Pallas kernels: none -> 194 us  [the longest x1 76.9 us: local(): pl.pallas_call(functools.partial(transform_kernel, *sizes), out_shape=sha...]
    all_to_all x8 -> x0, starting transfers between devices: 131 us -> none  [the longest x1 84.9 us: local(): lax.all_to_all(spec_imag, 'wide', split_axis=3, concat_axis=1, tiled=True)]
    dot_general x22 -> x0, matrix products: 64.7 us -> none  [the longest x20 60.4 us: along(): jnp.einsum(letters + ',' + letters[dimension] + 't->' + output, values, t...]
    all_to_all x8 -> x0, other arithmetic: 36.2 us -> none  [the longest x1 4.56 us: local(): lax.all_to_all(spec_imag, 'narrow', split_axis=1, concat_axis=2, tiled=True)]
    all_to_all x13 -> x0, local copies, waits for them, and re-layouts: 34.3 us -> none  [the longest x2 6.18 us: local(): lax.all_to_all(spec_real, 'narrow', split_axis=1, concat_axis=2, tiled=True)]
    dynamic_update_slice x2 -> x0, local copies, waits for them, and re-layouts: 32.6 us -> none  [the longest x1 20.6 us: deposit(): return lax.dynamic_update_slice(buffer, current + sphere_block, location)]
  transfers between devices with their start and end apart: 74 -> 0, of which waited for: 48 -> 0; matrix products, arithmetic and copies ran while one was open for 14% -> 0% of each run, Pallas kernels for 0% -> 0%
where the time goes in v1:
time: 214 us; the launch traced here: 213 us
  Pallas kernels  194 us (91%)
  local copies, waits for them, and re-layouts  15.4 us (7%)
  other arithmetic  3.33 us (2%)
    pallas_call x1, Pallas kernels, local(): pl.pallas_call(functools.partial(transform_kernel, *sizes), out_shape=sha...  76.9 us
    pallas_call x1, Pallas kernels, local(): pl.pallas_call(functools.partial(contact_kernel, *sizes), out_shape=(shap...  72.3 us
    pallas_call x1, Pallas kernels, local(): pl.pallas_call(functools.partial(gather_kernel, *sizes), out_shape=shape(...  15.4 us
    pallas_call x1, Pallas kernels, local(): pl.pallas_call(functools.partial(near_kernel, *sizes), out_shape=shape((1...  12 us
    unnamed x25, local copies, waits for them, and re-layouts  11.5 us
    pallas_call x1, Pallas kernels, local(): pl.pallas_call(functools.partial(spread_kernel, *sizes), out_shape=shape(...  8.69 us
    pallas_call x1, Pallas kernels, local(): pl.pallas_call(functools.partial(interp_kernel, *sizes), out_shape=shape(...  8.58 us

profile of v1, /device:TPU:1, one launch (start us, length us, event | category | flops | bytes accessed | tf_op | source)
XLA Modules:
  0.0 213.2 jit_solution(5056977893489482540)
XLA Ops:
  0.6 0.0 copy-start
  0.6 0.8 fusion.4
  1.5 0.7 pad.16
  2.1 0.8 reshape.56
  2.9 0.8 reshape.54
  3.7 0.1 pad.20.clone
  3.8 0.7 convert_element_type.20
  4.5 0.1 convert_element_type.21
  4.6 0.8 multiply_bitcast_fusion.1
  5.4 0.7 convert_element_type.18
  6.1 0.1 convert_element_type.19
  6.1 0.1 pad_maximum_fusion
  6.2 0.1 broadcast_in_dim.94.centre_ref
  6.3 0.7 copy.26
  7.0 0.1 maximum_maximum_fusion.own_ref
  7.1 0.1 multiply_select_fusion
  7.3 15.4 %gather.1.held_ref = f32[12,16,256]{2,1,0:T(8,128)S(1)} custom-call(f32[16,256]{1,0:T(8,128)S(1)} %maximum_maximum_fusion.own_ref), custom_call_target="tpu_custom_call" | custom-call | tf_op jit(solution)/shard_map/gather/pallas_call | solution.py:623
  22.7 0.0 copy-start.9
  22.7 0.7 copy-done.9
  23.4 0.0 copy-start.10
  23.4 0.7 copy-done.10
  24.0 12.0 %near.1.near_ref = f32[16,256]{1,0:T(8,128)S(1)} custom-call(s32[4,2]{1,0:T(4,128)S(1)} %bitcast.24, f32[12,128]{1,0:T(8,128)S(1)} %bitcast.20, f32[12,16,256]{2,1,0:T(8,128)S(1)} %gather.1.held_ref, f32[3,256]{1,0:T(4,128)S(1)} %copy-done.9), custom_call_target="tpu_custom_call" | custom-call | tf_op jit(solution)/shard_map/near/pallas_call | solution.py:701
  36.0 0.0 copy-start.4
  36.0 1.0 copy-done.4
  37.0 8.7 %spread.1.mesh_ref = f32[32,2,8,384]{3,2,1,0:T(8,128)S(1)} custom-call(f32[12,128]{1,0:T(8,128)S(1)} %bitcast.21, f32[12,16,256]{2,1,0:T(8,128)S(1)} %gather.1.held_ref, f32[3,256]{1,0:T(4,128)S(1)} %copy-done.9, f32[288,256]{1,0:T(8,128)S(1)} %copy-done.4), custom_call_target="tpu_custom_call" | custom-call | tf_op jit(solution)/shard_map/spread/pallas_call | solution.py:636
  45.7 0.0 copy-done
  45.7 0.0 copy-start.1
  45.7 1.4 copy-done.1
  47.1 0.0 copy-start.2
  47.1 1.4 copy-done.2
  48.5 0.0 copy-start.3
  48.5 1.4 copy-done.3
  49.9 0.0 copy-start.5
  49.9 0.9 copy-done.5
  50.8 0.0 copy-start.6
  50.8 0.9 copy-done.6
  51.7 0.0 copy-start.7
  51.7 0.9 copy-done.7
  52.6 0.0 copy-start.8
  52.6 0.9 copy-done.8
  53.6 76.9 %transform.1.mesh_ref = f32[32,2,8,384]{3,2,1,0:T(8,128)S(1)} custom-call(f32[32,2,8,384]{3,2,1,0:T(8,128)S(1)} %spread.1.mesh_ref, bf16[256,256]{1,0:T(8,128)(2,1)S(1)} %copy-done.8, bf16[256,256]{1,0:T(8,128)(2,1)S(1)} %copy-done.7, bf16[256,256]{1,0:T(8,128)(2,1)S(1)} %copy-done.6, bf16[256,256]{1,0:T(8,128)(2,1)S(1)} %copy-done.5, ...), custom_call_target="tpu_custom_call" | custom-call | tf_op jit(solution)/shard_map/transform/pallas_call | solution.py:657
  130.5 8.6 %interpolate.1.part_ref = f32[6,16,256]{2,1,0:T(8,128)S(1)} custom-call(f32[12,128]{1,0:T(8,128)S(1)} %bitcast.22, f32[3,256]{1,0:T(4,128)S(1)} %copy-done.9, f32[288,256]{1,0:T(8,128)S(1)} %copy-done.4, f32[32,2,8,384]{3,2,1,0:T(8,128)S(1)} %transform.1.mesh_ref), custom_call_target="tpu_custom_call" | custom-call | tf_op jit(solution)/shard_map/interpolate/pallas_call | solution.py:687
  139.1 72.3 %contacts.1 = (f32[16,256]{1,0:T(8,128)S(1)}, f32[8,128]{1,0:T(8,128)S(1)}, f32[16,128]{1,0:T(8,128)S(1)}) custom-call(f32[6,16,256]{2,1,0:T(8,128)S(1)} %interpolate.1.part_ref, f32[16,256]{1,0:T(8,128)S(1)} %near.1.near_ref, f32[16,128]{1,0:T(8,128)S(1)} %broadcast_in_dim.94.centre_ref, f32[144,128]{1,0:T(8,128)S(1)} %pad.15.edge_ref, ...), custom_call_target="tpu_custom_call" | custom-call | tf_op jit(solution)/shard_map/contacts/pallas_call | solution.py:738
  211.4 0.6 copy.30
  212.0 0.5 slice_bitcast_fusion
  212.5 0.1 slice_reduce_fusion
  212.6 0.7 reshape_squeeze.3
  (13 shorter events, 0.1 us)
Async XLA Ops:
  0.6 45.1 %copy-start = (bf16[768,1024]{1,0:T(8,128)(2,1)S(1)}, bf16[768,1024]{1,0:T(8,128)(2,1)}, u32[]{:S(2)}) copy-start(bf16[768,1024]{1,0:T(8,128)(2,1)} %constant.144.clone.iy_low) | copy-start | bytes 4718596
  22.7 0.7 copy-start.9
  23.4 0.7 copy-start.10
  36.0 1.0 copy-start.4
  45.7 1.4 copy-start.1
  47.1 1.4 copy-start.2
  48.5 1.4 copy-start.3
  49.9 0.9 copy-start.5
  50.8 0.9 copy-start.6
  51.7 0.9 copy-start.7
  52.6 0.9 copy-start.8

commit v2 on v1

--- a/solution.py
+++ b/solution.py
@@ -15,6 +15,8 @@
 NEAR = 2
 SWEEPS = 6
 SLOTS_DEV = 4
+ROWS_DEV = 3 * SLOTS_DEV
+CONT_DEV = 32
 
 soften = 1.0
 screen = 0.0625
@@ -29,6 +31,7 @@
 F32 = jnp.float32
 BF16 = jnp.bfloat16
 VMEM_SPEC = pl.BlockSpec(memory_space=pltpu.VMEM)
+HBM_SPEC = pl.BlockSpec(memory_space=pltpu.HBM)
 SMEM_SPEC = pl.BlockSpec(memory_space=pltpu.SMEM)
 
 
@@ -122,9 +125,33 @@
 GATHER = [(dw, dn) for dw in (-2, -1, 0, 1) for dn in (-1, 0, 1)]
 
 
-def gather_kernel(wide_count, narrow_count, own_ref, out_ref, held, send_sem, recv_sem):
+def gather_kernel(
+    wide_count,
+    narrow_count,
+    tractions_ref,
+    centres_ref,
+    anchors_ref,
+    occupied_ref,
+    out_ref,
+    meta_ref,
+    own_ref,
+    held,
+    send_sem,
+    recv_sem,
+):
     w, n = lax.axis_index("wide"), lax.axis_index("narrow")
     reach = [(dw, dn) for dw in (-2, -1, 0, 1, 2) for dn in (-1, 0, 1) if (dw, dn) != (0, 0)]
+    slots = [(a, b) for a in (0, 1) for b in (0, 1)]
+    numbers = [centres_ref[a, b, c] for a, b in slots for c in range(3)]
+    numbers += [anchors_ref[a, b, c].astype(F32) for a, b in slots for c in range(3)]
+    numbers += [occupied_ref[a, b].astype(F32) for a, b in slots]
+    lane = lanes_of((1, NODES))
+    line = jnp.zeros((1, NODES), F32)
+    for place, number in enumerate(numbers):
+        line = jnp.where(lane == place, number, line)
+    for s, (a, b) in enumerate(slots):
+        own_ref[3 * s : 3 * s + 3, :] = tractions_ref[a, b]
+    own_ref[12:16, :] = jnp.broadcast_to(line, (4, NODES))
     greet(wide_count, narrow_count, reach)
     copies = []
     for place, (dw, dn) in enumerate(GATHER):
@@ -143,15 +170,19 @@
         )
         copy.start()
         copies.append((place, copy))
-    out_ref[GATHER.index((0, 0))] = own_ref[...]
+    own = GATHER.index((0, 0))
+    out_ref[own] = own_ref[...]
+    meta_ref[own : own + 1, :] = own_ref[12:13, 0:128]
     for place, copy in copies:
         copy.wait_recv()
         out_ref[place] = held[place]
+        meta_ref[place : place + 1, :] = held[place, 12:13, 0:128]
     for place, copy in copies:
         copy.wait_send()
 
 
-def near_kernel(wide_count, narrow_count, list_ref, meta_ref, held_ref, off_ref, out_ref, offcol, source, columns):
+def near_field(sizes, list_ref, meta_ref, held_ref, off_ref, out_ref, offcol, source, columns):
+    wide_count, narrow_count = sizes
     w, n = lax.axis_index("wide"), lax.axis_index("narrow")
     own = GATHER.index((0, 0))
     out_ref[...] = jnp.zeros_like(out_ref)
@@ -162,30 +193,28 @@
         offcol[c] = jnp.broadcast_to(turned[:, c : c + 1], (NODES, 128))
 
     for s in range(SLOTS_DEV):
-
-        @pl.when(meta_ref[own, 24 + s] > 0.5)
-        def _():
-            for j in range(1 + NEAR):
+        for j in range(1 + NEAR):
+            if j == 0:
+                place, within = own, s
+            else:
+                entry = list_ref[s, j - 1]
+                holder = entry // SLOTS_DEV
+                within = entry % SLOTS_DEV
+                row = lax.rem(holder // narrow_count - w + 1 + wide_count, wide_count)
+                column = lax.rem(lax.rem(holder, narrow_count) - n + 1 + narrow_count, narrow_count)
+                place = (jnp.minimum(row, 2) + 1) * 3 + jnp.minimum(column, 2)
+            for c in range(3):
                 if j == 0:
-                    place, within = own, s
+                    shift = 0.0
                 else:
-                    entry = list_ref[s, j - 1]
-                    holder = entry // SLOTS_DEV
-                    within = entry % SLOTS_DEV
-                    row = lax.rem(holder // narrow_count - w + 1 + wide_count, wide_count)
-                    column = lax.rem(lax.rem(holder, narrow_count) - n + 1 + narrow_count, narrow_count)
-                    place = (row + 1) * 3 + column
-                for c in range(3):
-                    if j == 0:
-                        shift = 0.0
-                    else:
-                        e = meta_ref[own, 3 * s + c] - meta_ref[place, 3 * within + c]
-                        shift = e - jnp.where(e >= 128.0, 256.0, jnp.where(e < -128.0, -256.0, 0.0))
-                    source[j, c : c + 1, :] = shift - off_ref[c : c + 1, :]
-                    source[j, 3 + c : 4 + c, :] = held_ref[place, pl.ds(within * 3 + c, 1), :]
-
-            def chunk(i, carry):
-                rows = pl.ds(pl.multiple_of(i * 8, 8), 8)
+                    e = meta_ref[own, 3 * s + c] - meta_ref[place, 3 * within + c]
+                    shift = e - jnp.where(e >= 128.0, 256.0, jnp.where(e < -128.0, -256.0, 0.0))
+                source[j, c : c + 1, :] = shift - off_ref[c : c + 1, :]
+                source[j, 3 + c : 4 + c, :] = held_ref[place, pl.ds(within * 3 + c, 1), :]
+
+        def chunk(i, carry):
+            for part in (0, 1):
+                rows = pl.ds(pl.multiple_of(i * 16 + part * 8, 8), 8)
                 sums = [jnp.zeros((8, 128), F32) for _ in range(3)]
                 at = [offcol[c, rows, :] for c in range(3)]
                 for j in range(1 + NEAR):
@@ -202,11 +231,12 @@
                             sums[c] = sums[c] + (diagonal * f[c] + d[c] * along)
                 for c in range(3):
                     columns[rows, c : c + 1] = jnp.sum(sums[c], axis=1, keepdims=True)
-                return carry
-
-            lax.fori_loop(0, NODES // 8, chunk, 0)
-            result = jnp.transpose(columns[...])
-            out_ref[3 * s : 3 * s + 3, :] = near_scale * result[0:3, :]
+            return carry
+
+        lax.fori_loop(0, NODES // 16, chunk, 0)
+        result = jnp.transpose(columns[...])
+        alive = jnp.where(meta_ref[own, 24 + s] > 0.5, near_scale, 0.0)
+        out_ref[3 * s : 3 * s + 3, :] = alive * result[0:3, :]
 
 
 def sphere_weights(wide_count, narrow_count, index, meta_ref, off_ref):
@@ -319,45 +349,59 @@
     lax.fori_loop(0, 24, sphere, 0)
 
 
-def exchange(axis, count, source, target, send_sem, recv_sem, me, other):
-    def copy_to(step):
-        to = lax.rem(me + step, count)
-        device = (to, other) if axis == "wide" else (other, to)
+class Exchange:
+    def __init__(self, axis, count, source, target, half, send_sem, recv_sem, me, other):
+        self.__dict__.update(locals())
+
+    def copy_to(self, step):
+        to = lax.rem(self.me + step, self.count)
         return pltpu.make_async_remote_copy(
-            src_ref=source.at[to],
-            dst_ref=target.at[me],
-            send_sem=send_sem.at[step],
-            recv_sem=recv_sem.at[step],
-            device_id=device,
+            src_ref=self.source.at[to, self.half],
+            dst_ref=self.target.at[self.me, self.half],
+            send_sem=self.send_sem.at[step],
+            recv_sem=self.recv_sem.at[step],
+            device_id=(to, self.other) if self.axis == "wide" else (self.other, to),
             device_id_type=MESH,
         )
 
-    def begin(step, carry):
-        copy_to(step).start()
-        return carry
-
-    def end(step, carry):
-        copy_to(step).wait()
-        return carry
-
-    lax.fori_loop(1, count, begin, 0)
-    target[me] = source[me]
-    lax.fori_loop(1, count, end, 0)
+    def begin(self):
+        def step(index, carry):
+            self.copy_to(index).start()
+            return carry
+
+        lax.fori_loop(1, self.count, step, 0)
+        self.target[self.me, self.half] = self.source[self.me, self.half]
+
+    def arrive(self):
+        def step(index, carry):
+            self.copy_to(index).wait_recv()
+            return carry
+
+        lax.fori_loop(1, self.count, step, 0)
+
+    def sent(self):
+        def step(index, carry):
+            self.copy_to(index).wait_send()
+            return carry
+
+        lax.fori_loop(1, self.count, step, 0)
 
 
 def transform_kernel(
     wide_count,
     narrow_count,
     mesh_ref,
-    tx_high,
-    tx_low,
-    ix_high,
-    ix_low,
-    ty_high,
-    ty_low,
-    iy_high,
-    iy_low,
+    list_ref,
+    meta_ref,
+    held_ref,
+    off_ref,
+    pairs_ref,
+    gap_ref,
+    angles_ref,
+    tables,
     out_ref,
+    near_ref,
+    contacts_ref,
     wide_in,
     narrow_out,
     narrow_in,
@@ -367,32 +411,140 @@
     wide_home,
     lines,
     spectrum,
+    t_x,
+    t_yf,
+    t_yi,
+    offcol,
+    source,
+    columns,
+    own_line,
+    lines_in,
+    column_out,
+    column_in,
     wide_send,
     wide_recv,
     narrow_send,
     narrow_recv,
+    table_sem,
+    line_send,
+    line_recv,
+    column_send,
+    column_recv,
 ):
     w, n = lax.axis_index("wide"), lax.axis_index("narrow")
+    load = pltpu.make_async_copy(tables, t_x, table_sem)
+    load.start()
     greet(
         wide_count,
         narrow_count,
         [(step, 0) for step in range(1, wide_count)] + [(0, step) for step in range(1, narrow_count)],
     )
-    exchange("wide", wide_count, mesh_ref, wide_in, wide_send.at[0], wide_recv.at[0], w, n)
+
+    def exchanges(axis, source, target, way):
+        if axis == "wide":
+            fixed = (wide_count, w, n, wide_send, wide_recv)
+        else:
+            fixed = (narrow_count, n, w, narrow_send, narrow_recv)
+        count, me, other, send_sem, recv_sem = fixed
+        return [
+            Exchange(
+                axis, count, source, target, half, send_sem.at[way, half], recv_sem.at[way, half], me, other
+            )
+            for half in (0, 1)
+        ]
+
+    wide_go = exchanges("wide", mesh_ref, wide_in, 0)
+    narrow_go = exchanges("narrow", narrow_out, narrow_in, 0)
+    narrow_return = exchanges("narrow", narrow_back, narrow_home, 1)
+    wide_return = exchanges("wide", wide_back, wide_home, 1)
     for half in (0, 1):
+        wide_go[half].begin()
+
+    ids = pairs_ref[...]
+    within = (ids % SLOTS_DEV).astype(F32)
+    holder = ids // SLOTS_DEV
+    row_w = lax.rem(holder // narrow_count - w + 1 + wide_count, wide_count)
+    row_n = lax.rem(lax.rem(holder, narrow_count) - n + 1 + narrow_count, narrow_count)
+    seconds = ((row_w * 3 + row_n) * SLOTS_DEV).astype(F32) + within
+    polar, azimuth = angles_ref[0:1, :], angles_ref[1:2, :]
+    across = jnp.sin(polar)
+    fields = [
+        within[0:1],
+        seconds[1:2],
+        across * jnp.cos(azimuth),
+        across * jnp.sin(azimuth),
+        jnp.cos(polar),
+        gap_ref[...].reshape(1, CONT_DEV),
+    ]
+    line = jnp.concatenate(fields + [jnp.zeros((1, 64), F32)], axis=1)
+    own_line[...] = jnp.where(lax.broadcasted_iota(jnp.int32, (8, NODES), 0) == n, line, 0.0)
+
+    def line_copy(step):
+        return pltpu.make_async_remote_copy(
+            src_ref=own_line,
+            dst_ref=lines_in.at[step],
+            send_sem=line_send.at[step],
+            recv_sem=line_recv.at[step],
+            device_id=(w, lax.rem(n + step, narrow_count)),
+            device_id_type=MESH,
+        )
+
+    def column_copy(step):
+        return pltpu.make_async_remote_copy(
+            src_ref=column_out,
+            dst_ref=column_in.at[w],
+            send_sem=column_send.at[step],
+            recv_sem=column_recv.at[step],
+            device_id=(lax.rem(w + step, wide_count), n),
+            device_id_type=MESH,
+        )
+
+    for step in range(1, narrow_count):
+        line_copy(step).start()
+    near_field(
+        (wide_count, narrow_count), list_ref, meta_ref, held_ref, off_ref, near_ref, offcol, source, columns
+    )
+    load.wait()
+    t_yf[...] = jnp.zeros_like(t_yf)
+    for part in (0, 1):
+        for piece in range(8):
+            for c in range(3):
+                t_yf[part, piece * 128 + c * 32 : piece * 128 + c * 32 + 32, c * 256 : c * 256 + 256] = t_x[
+                    4 + part, piece * 32 : piece * 32 + 32, :
+                ]
+        for piece in range(8):
+            for c in range(3):
+                block = t_yf[part, piece * 128 : piece * 128 + 128, c * 256 : c * 256 + 256]
+                t_yi[part, c * 256 : c * 256 + 256, piece * 128 : piece * 128 + 128] = jnp.transpose(
+                    block.astype(F32)
+                ).astype(BF16)
+    for half in (0, 1):
+        wide_go[half].arrive()
         block = split(wide_in[:, half].reshape(GRID, 384))
-        along = dot3((tx_high[...], tx_low[...]), block)
+        along = dot3((t_x[0], t_x[1]), block)
         narrow_out[:, half] = along.reshape(narrow_count, 32, 384)
-    exchange("narrow", narrow_count, narrow_out, narrow_in, narrow_send.at[0], narrow_recv.at[0], n, w)
+        narrow_go[half].begin()
+    column = own_line[...]
+    for step in range(1, narrow_count):
+        line_copy(step).wait_recv()
+        column = column + lines_in[step]
+    column_out[...] = column
+    column_in[w] = column
+
+    def begin_column(step, carry):
+        column_copy(step).start()
+        return carry
+
+    lax.fori_loop(1, wide_count, begin_column, 0)
     for half in (0, 1):
-        for source in range(8):
-            groups = [narrow_in[source, half, :, g * 128 : g * 128 + 128] for g in range(3)]
+        narrow_go[half].arrive()
+        for piece in range(8):
+            groups = [narrow_in[piece, half, :, g * 128 : g * 128 + 128] for g in range(3)]
             unpacked = unpack_lanes(*groups)
             for j in range(4):
-                lines[half * 128 + j * 32 : half * 128 + j * 32 + 32, source * 128 : source * 128 + 128] = unpacked[j]
-    for half in (0, 1):
+                lines[half * 128 + j * 32 : half * 128 + j * 32 + 32, piece * 128 : piece * 128 + 128] = unpacked[j]
         rows = slice(half * 128, half * 128 + 128)
-        spectrum[rows, :] = dot3(split(lines[rows, :]), (ty_high[...], ty_low[...]))
+        spectrum[rows, :] = dot3(split(lines[rows, :]), (t_yf[0], t_yf[1]))
 
     row = lax.broadcasted_iota(jnp.int32, (32, 1), 0)
     k_x = (n * 16 + row % 16).astype(F32)
@@ -440,7 +592,6 @@
             edge = (nyquist_x * values[0] + nyquist_y * values[1] + nyquist_z * values[2]) * inverse
             flow = [flows[half] * inverse, flows[1 - half] * inverse]
             gradient = [derive_x(flow[0]), derive_y(flow[0]), None]
-            other_square = square_xy + (k_z * k_z + nyquists_z[1 - half] * nyquists_z[1 - half])
             gradient[2] = turn_z[half] * (flows[1 - half] * inverse)
             nyquist = (nyquist_x, nyquist_y, nyquist_z)
             for c in range(3):
@@ -452,8 +603,7 @@
     lax.fori_loop(0, 4, filtered, 0)
     for half in (0, 1):
         rows = slice(half * 128, half * 128 + 128)
-        lines[rows, :] = dot3(split(spectrum[rows, :]), (iy_high[...], iy_low[...]))
-    for half in (0, 1):
+        lines[rows, :] = dot3(split(spectrum[rows, :]), (t_yi[0], t_yi[1]))
         for target in range(8):
             groups = [
                 lines[half * 128 + j * 32 : half * 128 + j * 32 + 32, target * 128 : target * 128 + 128]
@@ -462,17 +612,52 @@
             packed = pack_lanes(*groups)
             for g in range(3):
                 narrow_back[target, half, :, g * 128 : g * 128 + 128] = packed[g]
-    exchange("narrow", narrow_count, narrow_back, narrow_home, narrow_send.at[1], narrow_recv.at[1], n, w)
+        narrow_return[half].begin()
     for half in (0, 1):
+        narrow_return[half].arrive()
         block = split(narrow_home[:, half].reshape(GRID, 384))
-        along = dot3((ix_high[...], ix_low[...]), block)
+        along = dot3((t_x[2], t_x[3]), block)
         wide_back[:, half] = along.reshape(wide_count, 8, 384)
-    exchange("wide", wide_count, wide_back, wide_home, wide_send.at[1], wide_recv.at[1], w, n)
-    out_ref[...] = wide_home[...]
+        wide_return[half].begin()
+    def end_column(step, carry):
+        column_copy(step).wait()
+        return carry
+
+    lax.fori_loop(1, wide_count, end_column, 0)
+    for step in range(1, narrow_count):
+        line_copy(step).wait_send()
+    contacts_ref[...] = column_in[...].reshape(wide_count * narrow_count, NODES)
+    for group in (wide_go, narrow_go, narrow_return):
+        for half in (0, 1):
+            group[half].sent()
+    for half in (0, 1):
+        wide_return[half].arrive()
+        out_ref[:, half] = wide_home[:, half]
+    for half in (0, 1):
+        wide_return[half].sent()
 
 
 AROUND = [(dw, dn) for dw in (-1, 0, 1) for dn in (-1, 0, 1)]
 PARTIAL = [(dw, dn) for dw in (-2, -1, 0) for dn in (-1, 0)]
+
+
+def shift_narrow(values, dn, narrow_count):
+    if dn == 0:
+        return values
+    place = lanes_of(values.shape) % narrow_count
+    edge = 0 if dn == 1 else narrow_count - 1
+    total = values.shape[-1]
+    return jnp.where(
+        place == edge,
+        roll(values, (dn - dn * narrow_count) % total),
+        roll(values, dn % total),
+    )
+
+
+def shift_wide(values, dw, narrow_count):
+    if dw == 0:
+        return values
+    return roll(values, (dw * narrow_count) % values.shape[-1])
 
 
 def contact_kernel(
@@ -480,25 +665,28 @@
     narrow_count,
     part_ref,
     near_ref,
+    static_ref,
     centre_ref,
-    edge_ref,
-    gap_ref,
     velocity_ref,
     force_ref,
     moved_ref,
     part_in,
-    load_out,
-    load_in,
-    flow_out,
-    flow_in,
+    tile_out,
+    tile_in,
+    table_out,
+    table_in,
+    edges,
+    around,
+    loads,
     part_send,
     part_recv,
-    load_send,
-    load_recv,
-    flow_send,
-    flow_recv,
+    narrow_send,
+    narrow_recv,
+    wide_send,
+    wide_recv,
 ):
     w, n = lax.axis_index("wide"), lax.axis_index("narrow")
+    devices = wide_count * narrow_count
 
     def device(dw, dn):
         return (
@@ -509,8 +697,41 @@
     greet(
         wide_count,
         narrow_count,
-        [d for d in AROUND if d != (0, 0)] + [(-2, -1), (-2, 0), (2, 1), (2, 0)],
-    )
+        [(step, 0) for step in range(1, wide_count)]
+        + [(0, step) for step in range(1, narrow_count)]
+        + [(-2, -1), (-1, -1), (2, 1), (1, 1)],
+    )
+    own = PARTIAL.index((0, 0))
+    pieces = [part_ref[p] + near_ref[...] if p == own else part_ref[p] for p in range(6)]
+    means = [jnp.sum(piece, axis=1, keepdims=True) * (1.0 / NODES) for piece in pieces]
+    column = jnp.concatenate(means + [jnp.zeros((32, 1), F32)], axis=0)
+    line = jnp.transpose(jnp.broadcast_to(column, (128, 128)))[:8]
+    tile_out[...] = jnp.where(lax.broadcasted_iota(jnp.int32, (8, 128), 0) == n, line, 0.0)
+
+    def narrow_copy(step):
+        to = lax.rem(n + step, narrow_count)
+        return pltpu.make_async_remote_copy(
+            src_ref=tile_out,
+            dst_ref=tile_in.at[step],
+            send_sem=narrow_send.at[step],
+            recv_sem=narrow_recv.at[step],
+            device_id=(w, to),
+            device_id_type=MESH,
+        )
+
+    def wide_copy(step):
+        to = lax.rem(w + step, wide_count)
+        return pltpu.make_async_remote_copy(
+            src_ref=table_out,
+            dst_ref=table_in.at[w],
+            send_sem=wide_send.at[step],
+            recv_sem=wide_recv.at[step],
+            device_id=(to, n),
+            device_id_type=MESH,
+        )
+
+    for step in range(1, narrow_count):
+        narrow_copy(step).start()
     copies = []
     for place, (dw, dn) in enumerate(PARTIAL):
         if (dw, dn) == (0, 0):
@@ -525,72 +746,99 @@
         )
         copy.start()
         copies.append((place, copy))
-    velocity = near_ref[...] + part_ref[PARTIAL.index((0, 0))]
+    tile = tile_out[...]
+    for step in range(1, narrow_count):
+        narrow_copy(step).wait_recv()
+        tile = tile + tile_in[step]
+    table_out[...] = tile
+    table_in[w] = tile
+
+    def begin(step, carry):
+        wide_copy(step).start()
+        return carry
+
+    lax.fori_loop(1, wide_count, begin, 0)
+
+    fields = jnp.transpose(static_ref[...])
+    first, second, gap = fields[0:32], fields[32:64], fields[160:192]
+    normal = [fields[64 + 32 * c : 96 + 32 * c] for c in range(3)]
+    for place in range(9):
+        for s in range(SLOTS_DEV):
+            mark = jnp.where(second == float(place * SLOTS_DEV + s), -1.0, 0.0)
+            if place == 4:
+                mark = mark + jnp.where(first == float(s), 1.0, 0.0)
+            for c in range(3):
+                edges[place, 3 * s + c] = mark * normal[c]
+
+    velocity = pieces[own]
     for place, copy in copies:
         copy.wait_recv()
         velocity = velocity + part_in[place]
     velocity_ref[...] = velocity
-    hydro = jnp.broadcast_to(
-        jnp.sum(velocity, axis=1, keepdims=True) * (1.0 / NODES), (16, 128)
-    )
-
-    def flow_copy(turn, place):
-        dw, dn = AROUND[place]
-        return pltpu.make_async_remote_copy(
-            src_ref=flow_out.at[turn],
-            dst_ref=flow_in.at[turn, 8 - place],
-            send_sem=flow_send.at[turn, place],
-            recv_sem=flow_recv.at[turn, 8 - place],
-            device_id=device(dw, dn),
-            device_id_type=MESH,
-        )
-
-    def load_copy(turn, place):
-        dw, dn = AROUND[place]
-        return pltpu.make_async_remote_copy(
-            src_ref=load_out.at[turn, place],
-            dst_ref=load_in.at[turn, 8 - place],
-            send_sem=load_send.at[turn, place],
-            recv_sem=load_recv.at[turn, 8 - place],
-            device_id=device(dw, dn),
-            device_id_type=MESH,
-        )
-
-    others = [place for place in range(9) if place != 4]
+
+    def end(step, carry):
+        wide_copy(step).wait_recv()
+        return carry
+
+    lax.fori_loop(1, wide_count, end, 0)
+    spread_means = jnp.transpose(table_in[...].reshape(devices, 128))
+    hydro = jnp.zeros((16, devices), F32)
+    for p, (dw, dn) in enumerate(PARTIAL):
+        moved_means = shift_wide(spread_means[p * 16 : p * 16 + 16], dw, narrow_count)
+        hydro = hydro + shift_narrow(moved_means, dn, narrow_count)
+
+    def totals(force):
+        def one_place(place, carry):
+            for k in range(ROWS_DEV):
+                loads[place, k : k + 1, :] = jnp.sum(edges[place, k] * force, axis=0, keepdims=True)
+            return carry
+
+        lax.fori_loop(0, 9, one_place, 0)
+        result = jnp.zeros((16, devices), F32)
+        for dn in (-1, 0, 1):
+            inner = jnp.zeros((16, devices), F32)
+            for dw in (-1, 0, 1):
+                inner = inner + shift_wide(loads[AROUND.index((dw, dn))], dw, narrow_count)
+            result = result + shift_narrow(inner, dn, narrow_count)
+        return result
 
     def sweep(turn, carry):
         force, moving = carry
-        flow_out[turn] = moving
-        for place in others:
-            flow_copy(turn, place).start()
-        flow_in[turn, 4] = moving
-        for place in others:
-            flow_copy(turn, place).wait_recv()
-        around = flow_in[turn].reshape(144, 128)
-        relative = jnp.sum(edge_ref[...] * around, axis=0, keepdims=True)
+        for dn in (-1, 0, 1):
+            beside = shift_narrow(moving, -dn, narrow_count)
+            for dw in (-1, 0, 1):
+                around[AROUND.index((dw, dn))] = shift_wide(beside, -dw, narrow_count)
+
+        def one_place(place, relative):
+            for k in range(ROWS_DEV):
+                relative = relative + edges[place, k] * around[place, k : k + 1, :]
+            return relative
+
+        relative = lax.fori_loop(0, 9, one_place, jnp.zeros((CONT_DEV, devices), F32))
         force = jnp.maximum(
-            force
-            - relaxation * (gap_ref[0:1, :] + time_step * relative) / (2.0 * time_step * mobility),
-            0.0,
+            force - relaxation * (gap + time_step * relative) / (2.0 * time_step * mobility), 0.0
         )
-        load = jnp.sum(edge_ref[...] * force, axis=1, keepdims=True)
-        load_out[turn] = jnp.broadcast_to(load, (144, 128)).reshape(9, 16, 128)
-        for place in others:
-            load_copy(turn, place).start()
-        summed = load_out[turn, 4]
-        for place in others:
-            load_copy(turn, place).wait_recv()
-            summed = summed + load_in[turn, 8 - place]
-        for place in others:
-            load_copy(turn, place).wait_send()
-            flow_copy(turn, place).wait_send()
-        return force, hydro + mobility * summed
-
-    force, moving = lax.fori_loop(0, SWEEPS, sweep, (jnp.zeros((1, 128), F32), hydro))
-    force_ref[...] = jnp.broadcast_to(force, (8, 128))
-    moved_ref[...] = centre_ref[...] + time_step * moving
+        return force, hydro + mobility * totals(force)
+
+    loads[...] = jnp.zeros_like(loads)
+    force, moving = lax.fori_loop(
+        0, SWEEPS, sweep, (jnp.zeros((CONT_DEV, devices), F32), hydro)
+    )
+    mine = lanes_of((1, devices)) == w * narrow_count + n
+    own_force = jnp.sum(jnp.where(mine, force, 0.0), axis=1, keepdims=True)
+    force_ref[...] = jnp.broadcast_to(own_force, (CONT_DEV, 128))
+    own_moving = jnp.sum(jnp.where(mine, moving, 0.0), axis=1, keepdims=True)
+    moved_ref[...] = centre_ref[...] + time_step * own_moving
     for place, copy in copies:
         copy.wait_send()
+    for step in range(1, narrow_count):
+        narrow_copy(step).wait_send()
+
+    def finish(step, carry):
+        wide_copy(step).wait_send()
+        return carry
+
+    lax.fori_loop(1, wide_count, finish, 0)
 
 
 def local(
@@ -611,25 +859,20 @@
     shape = jax.ShapeDtypeStruct
     dma = pltpu.SemaphoreType.DMA
 
-    meta = jnp.concatenate(
-        [
-            centers.reshape(12),
-            anchors.reshape(12).astype(F32),
-            occupied.reshape(4).astype(F32),
-            jnp.zeros((228,), F32),
-        ]
-    )
-    own = jnp.concatenate([tractions.reshape(12, NODES), meta[None], jnp.zeros((3, NODES), F32)])
-    held = pl.pallas_call(
+    held, metas = pl.pallas_call(
         functools.partial(gather_kernel, *sizes),
-        out_shape=shape((12, 16, NODES), F32),
-        in_specs=[VMEM_SPEC],
-        out_specs=VMEM_SPEC,
-        scratch_shapes=[pltpu.VMEM((12, 16, NODES), F32), dma((12,)), dma((12,))],
+        out_shape=(shape((12, 16, NODES), F32), shape((12, 128), F32)),
+        in_specs=[VMEM_SPEC, SMEM_SPEC, SMEM_SPEC, SMEM_SPEC],
+        out_specs=(VMEM_SPEC, VMEM_SPEC),
+        scratch_shapes=[
+            pltpu.VMEM((16, NODES), F32),
+            pltpu.VMEM((12, 16, NODES), F32),
+            dma((12,)),
+            dma((12,)),
+        ],
         compiler_params=params(0),
         name="gather",
-    )(own)
-    metas = held[:, 12, :128]
+    )(tractions, centers, anchors, occupied)
 
     table_z = trig_table(4)
     wrapped_z = np.concatenate([table_z, table_z[:, :32]], axis=1).T.astype(np.float32)
@@ -650,15 +893,18 @@
 
     table_x = trig_table(16)
     table_y = trig_table(128)
-    wide_y = np.zeros((8, 128, 3, GRID))
-    for c in range(3):
-        wide_y[:, c * 32 : c * 32 + 32, c, :] = table_y.T.reshape(8, 32, GRID)
-    wide_y = wide_y.reshape(1024, 768)
-    mesh = pl.pallas_call(
+    turned_x = np.ascontiguousarray(table_x.T)
+    turned_y = np.ascontiguousarray(table_y.T)
+    tables = np.stack([*halves(table_x), *halves(turned_x), *halves(turned_y)])
+    mesh, near, contacts = pl.pallas_call(
         functools.partial(transform_kernel, *sizes),
-        out_shape=shape((32, 2, 8, 384), F32),
-        in_specs=[VMEM_SPEC] * 9,
-        out_specs=VMEM_SPEC,
+        out_shape=(
+            shape((32, 2, 8, 384), F32),
+            shape((16, NODES), F32),
+            shape((wide_count * narrow_count, NODES), F32),
+        ),
+        in_specs=[VMEM_SPEC, SMEM_SPEC, SMEM_SPEC] + [VMEM_SPEC] * 5 + [HBM_SPEC],
+        out_specs=(VMEM_SPEC,) * 3,
         scratch_shapes=[
             pltpu.VMEM((32, 2, 8, 384), F32),
             pltpu.VMEM((8, 2, 32, 384), F32),
@@ -669,19 +915,38 @@
             pltpu.VMEM((32, 2, 8, 384), F32),
             pltpu.VMEM((256, 1024), F32),
             pltpu.VMEM((256, 768), F32),
-            dma((2, 32)),
-            dma((2, 32)),
-            dma((2, 8)),
-            dma((2, 8)),
+            pltpu.VMEM((6, 256, 256), BF16),
+            pltpu.VMEM((2, 1024, 768), BF16),
+            pltpu.VMEM((2, 768, 1024), BF16),
+            pltpu.VMEM((3, NODES, 128), F32),
+            pltpu.VMEM((3, 8, NODES), F32),
+            pltpu.VMEM((NODES, 8), F32),
+            pltpu.VMEM((8, NODES), F32),
+            pltpu.VMEM((8, 8, NODES), F32),
+            pltpu.VMEM((8, NODES), F32),
+            pltpu.VMEM((32, 8, NODES), F32),
+            dma((2, 2, 32)),
+            dma((2, 2, 32)),
+            dma((2, 2, 8)),
+            dma((2, 2, 8)),
+            dma,
+            dma((8,)),
+            dma((8,)),
+            dma((32,)),
+            dma((32,)),
         ],
         compiler_params=params(1),
         name="transform",
     )(
         mesh,
-        *halves(table_x),
-        *halves(np.ascontiguousarray(table_x.T)),
-        *halves(wide_y),
-        *halves(np.ascontiguousarray(wide_y.T)),
+        near_list.reshape(4, NEAR),
+        metas,
+        held,
+        node_offsets,
+        contact_pairs,
+        contact_gap,
+        contact_angles,
+        tables,
     )
 
     part = pl.pallas_call(
@@ -698,67 +963,35 @@
         name="interpolate",
     )(metas, node_offsets, wrapped_z, mesh)
 
-    near = pl.pallas_call(
-        functools.partial(near_kernel, *sizes),
-        out_shape=shape((16, NODES), F32),
-        in_specs=[SMEM_SPEC, SMEM_SPEC, VMEM_SPEC, VMEM_SPEC],
-        out_specs=VMEM_SPEC,
-        scratch_shapes=[
-            pltpu.VMEM((3, NODES, 128), F32),
-            pltpu.VMEM((3, 8, NODES), F32),
-            pltpu.VMEM((NODES, 8), F32),
-        ],
-        compiler_params=params(),
-        name="near",
-    )(near_list.reshape(4, NEAR), metas, held, node_offsets)
-
-    polar, azimuth = contact_angles[0], contact_angles[1]
-    normal = jnp.stack(
-        [jnp.sin(polar) * jnp.cos(azimuth), jnp.sin(polar) * jnp.sin(azimuth), jnp.cos(polar)]
-    )
-    holder, within = contact_pairs // 4, contact_pairs % 4
-    row_w = (holder // narrow_count - w + 1 + wide_count) % wide_count
-    row_n = (holder % narrow_count - n + 1 + narrow_count) % narrow_count
-    first_row = (row_w * 3 + row_n) * 16 + within * 3
-    index = jnp.arange(144, dtype=jnp.int32)
-    component = index % 16 % 3
-    base = (index - component)[:, None]
-    used = (index % 16 < 12)[:, None]
-    sign = jnp.where(base == first_row[0][None, :], 1.0, 0.0) - jnp.where(
-        base == first_row[1][None, :], 1.0, 0.0
-    )
-    spread_normal = jnp.where(
-        (component == 0)[:, None],
-        normal[0][None],
-        jnp.where((component == 1)[:, None], normal[1][None], normal[2][None]),
-    )
-    edge = jnp.pad(jnp.where(used, sign * spread_normal, 0.0), ((0, 0), (0, 96)))
-    gap = jnp.pad(jnp.broadcast_to(contact_gap[None], (8, 32)), ((0, 0), (0, 96)))
     centre_rows = jnp.broadcast_to(jnp.pad(centers.reshape(12, 1), ((0, 4), (0, 0))), (16, 128))
+    devices = wide_count * narrow_count
     velocity, force, moved = pl.pallas_call(
         functools.partial(contact_kernel, *sizes),
-        out_shape=(shape((16, NODES), F32), shape((8, 128), F32), shape((16, 128), F32)),
-        in_specs=[VMEM_SPEC] * 5,
+        out_shape=(shape((16, NODES), F32), shape((CONT_DEV, 128), F32), shape((16, 128), F32)),
+        in_specs=[VMEM_SPEC] * 4,
         out_specs=(VMEM_SPEC,) * 3,
         scratch_shapes=[
             pltpu.VMEM((6, 16, NODES), F32),
-            pltpu.VMEM((SWEEPS, 9, 16, 128), F32),
-            pltpu.VMEM((SWEEPS, 9, 16, 128), F32),
-            pltpu.VMEM((SWEEPS, 16, 128), F32),
-            pltpu.VMEM((SWEEPS, 9, 16, 128), F32),
+            pltpu.VMEM((8, 128), F32),
+            pltpu.VMEM((8, 8, 128), F32),
+            pltpu.VMEM((8, 128), F32),
+            pltpu.VMEM((32, 8, 128), F32),
+            pltpu.VMEM((9, ROWS_DEV, CONT_DEV, devices), F32),
+            pltpu.VMEM((9, 16, devices), F32),
+            pltpu.VMEM((9, 16, devices), F32),
             dma((6,)),
             dma((6,)),
-            dma((SWEEPS, 9)),
-            dma((SWEEPS, 9)),
-            dma((SWEEPS, 9)),
-            dma((SWEEPS, 9)),
+            dma((8,)),
+            dma((8,)),
+            dma((32,)),
+            dma((32,)),
         ],
         compiler_params=params(2),
         name="contacts",
-    )(part, near, centre_rows, edge, gap)
+    )(part, near, contacts, centre_rows)
     return (
         velocity[:12].reshape(2, 2, 3, NODES),
-        force[0, :32],
+        force[:, 0],
         moved[:12, 0].reshape(2, 2, 3),
     )
 

time: 214 us -> 136 us (0.64)
  Pallas kernels: 194 us -> 130 us
  local copies, waits for them, and re-layouts: 15.4 us -> 4.54 us
  other arithmetic: 3.33 us -> 0 us
    pallas_call x1, Pallas kernels: 72.3 us -> 23.1 us  [local(): pl.pallas_call(functools.partial(contact_kernel, *sizes), out_shape=(shap...]
    pallas_call x3 -> x2, Pallas kernels: 104 us -> 87.9 us  [the longest x1 71.9 us: local(): pl.pallas_call(functools.partial(transform_kernel, *sizes), out_shape=(sh...]
    unnamed x25 -> x24, local copies, waits for them, and re-layouts: 11.5 us -> 2.97 us
where the time goes in v2:
time: 136 us; the launch traced here: 135 us
  Pallas kernels  130 us (96%)
  local copies, waits for them, and re-layouts  4.54 us (3%)
    pallas_call x1, Pallas kernels, local(): pl.pallas_call(functools.partial(transform_kernel, *sizes), out_shape=(sh...  71.9 us
    pallas_call x1, Pallas kernels, local(): pl.pallas_call(functools.partial(contact_kernel, *sizes), out_shape=(shap...  23.1 us
    pallas_call x1, Pallas kernels, local(): pl.pallas_call(functools.partial(gather_kernel, *sizes), out_shape=(shape...  16 us
    pallas_call x1, Pallas kernels, local(): pl.pallas_call(functools.partial(spread_kernel, *sizes), out_shape=shape(...  9.45 us
    pallas_call x1, Pallas kernels, local(): pl.pallas_call(functools.partial(interp_kernel, *sizes), out_shape=shape(...  9.32 us
    unnamed x24, local copies, waits for them, and re-layouts  2.97 us

profile of v2, /device:TPU:1, one launch (start us, length us, event | category | flops | bytes accessed | tf_op | source)
XLA Modules:
  0.0 135.1 jit_solution(9580560480733983738)
XLA Ops:
  0.6 0.0 copy-start.4
  0.6 0.0 copy-start.9
  0.7 0.0 copy-start.5
  0.7 0.7 copy.18.tractions_ref
  1.4 0.0 copy-done.4
  1.4 0.0 copy-done.9
  1.4 0.0 copy-done.5
  1.4 0.0 copy-start.3
  1.4 16.0 %gather.1 = (f32[12,16,256]{2,1,0:T(8,128)S(1)}, f32[12,128]{1,0:T(8,128)S(1)}) custom-call(f32[2,2,3,256]{3,2,1,0:T(4,128)S(1)} %copy.18.tractions_ref, f32[2,2,3]{2,1,0:T(2,128)S(1)} %copy-done.4, s32[2,2,3]{2,1,0:T(2,128)S(1)} %copy-done.5, s32[2,2]{1,0:T(2,128)S(1)} %copy-done.9), custom_call_target="tpu_custom_call" | custom-call | tf_op jit(solution)/shard_map/gather/pallas_call | solution.py:862
  17.4 0.0 copy-done.3
  17.4 0.0 copy-start
  17.4 1.0 copy-done
  18.4 0.0 copy-start.2
  18.4 0.0 copy-start.6
  18.4 0.0 copy-start.8
  18.4 9.4 %spread.1.mesh_ref = f32[32,2,8,384]{3,2,1,0:T(8,128)S(1)} custom-call(f32[12,128]{1,0:T(8,128)S(1)} %get-tuple-element.11.meta_ref, f32[12,16,256]{2,1,0:T(8,128)S(1)} %get-tuple-element.12.held_ref, f32[3,256]{1,0:T(4,128)S(1)} %copy-done.3, f32[288,256]{1,0:T(8,128)S(1)} %copy-done), custom_call_target="tpu_custom_call" | custom-call | tf_op jit(solution)/shard_map/spread/pallas_call | solution.py:879
  27.9 0.0 copy-start.7
  27.9 0.0 copy-start.10
  27.9 0.0 copy-done.2
  27.9 0.0 copy-done.6
  27.9 0.0 copy-done.8
  27.9 0.6 copy-done.7
  28.5 0.0 copy-done.10
  28.5 0.0 copy-start.1
  28.5 71.9 %transform.1 = (f32[32,2,8,384]{3,2,1,0:T(8,128)S(1)}, f32[16,256]{1,0:T(8,128)S(1)}, f32[256,256]{1,0:T(8,128)S(1)}) custom-call(f32[32,2,8,384]{3,2,1,0:T(8,128)S(1)} %spread.1.mesh_ref, s32[4,2]{1,0:T(4,128)S(1)} %bitcast.5, f32[12,128]{1,0:T(8,128)S(1)} %get-tuple-element.11.meta_ref, f32[12,16,256]{2,1,0:T(8,128)S(1)} %get-tuple-element.12.held_ref, ...), custom_call_target="tpu_custom_call" | custom-call | tf_op jit(solution)/shard_map/transform/pallas_call | solution.py:899
  100.5 0.0 copy-done.1
  100.5 9.3 %interpolate.1.part_ref = f32[6,16,256]{2,1,0:T(8,128)S(1)} custom-call(f32[12,128]{1,0:T(8,128)S(1)} %get-tuple-element.11.meta_ref, f32[3,256]{1,0:T(4,128)S(1)} %copy-done.3, f32[288,256]{1,0:T(8,128)S(1)} %copy-done.1, f32[32,2,8,384]{3,2,1,0:T(8,128)S(1)} %get-tuple-element.13.mesh_ref), custom_call_target="tpu_custom_call" | custom-call | tf_op jit(solution)/shard_map/interpolate/pallas_call | solution.py:952
  109.8 0.1 reshape.16
  109.9 0.1 broadcast_in_dim.8.centre_ref
  110.0 23.1 %contacts.1 = (f32[16,256]{1,0:T(8,128)S(1)}, f32[32,128]{1,0:T(8,128)S(1)}, f32[16,128]{1,0:T(8,128)S(1)}) custom-call(f32[6,16,256]{2,1,0:T(8,128)S(1)} %interpolate.1.part_ref, f32[16,256]{1,0:T(8,128)S(1)} %get-tuple-element.14.near_ref, f32[256,256]{1,0:T(8,128)S(1)} %get-tuple-element.15.static_ref, f32[16,128]{1,0:T(8,128)S(1)} %broadcast_in_dim.8.centre_ref), custom_call_target="tpu_custom_call" | custom-call | tf_op jit(solution)/shard_map/contacts/pallas_call | solution.py:968
  133.1 0.6 copy.21
  133.7 0.1 slice_reduce_fusion.1
  133.8 0.7 reshape_squeeze.3
  134.5 0.6 slice_reduce_fusion
  (2 shorter events, 0.0 us)
Async XLA Ops:
  0.6 0.8 copy-start.4
  0.6 0.8 copy-start.9
  0.7 0.8 copy-start.5
  1.4 16.0 %copy-start.3 = (f32[3,256]{1,0:T(4,128)S(1)}, f32[3,256]{1,0:T(4,128)}, u32[]{:S(2)}) copy-start(f32[3,256]{1,0:T(4,128)} %off_ref.5) | copy-start | bytes 9220
  17.4 1.0 copy-start
  18.4 9.5 %copy-start.2 = (bf16[6,256,256]{2,1,0:T(8,128)(2,1)S(1)}, bf16[6,256,256]{2,1,0:T(8,128)(2,1)}, u32[]{:S(2)}) copy-start(bf16[6,256,256]{2,1,0:T(8,128)(2,1)} %constant.8.clone.tables) | copy-start | bytes 2359300
  18.4 9.5 %copy-start.6 = (s32[2,2,2]{2,1,0:T(2,128)S(1)}, s32[2,2,2]{2,1,0:T(2,128)}, u32[]{:S(2)}) copy-start(s32[2,2,2]{2,1,0:T(2,128)} %param.16) | copy-start | bytes 100
  18.4 9.5 %copy-start.8 = (f32[2,32]{1,0:T(2,128)S(1)}, f32[2,32]{1,0:T(2,128)}, u32[]{:S(2)}) copy-start(f32[2,32]{1,0:T(2,128)} %angles_ref.1) | copy-start | bytes 772
  27.9 0.7 copy-start.7
  27.9 0.7 copy-start.10
  28.5 71.9 %copy-start.1 = (f32[288,256]{1,0:T(8,128)S(1)}, f32[288,256]{1,0:T(8,128)}, u32[]{:S(2)}) copy-start(f32[288,256]{1,0:T(8,128)} %constant.7.clone.tz_ref) | copy-start | bytes 884740

commit v3 on v2

--- a/solution.py
+++ b/solution.py
@@ -75,7 +75,9 @@
 
 
 def dot3(a, b):
-    return dot(a[0], b[0]) + (dot(a[0], b[1]) + dot(a[1], b[0]))
+    return dot(
+        jnp.concatenate([a[0], a[0], a[1]], axis=1), jnp.concatenate([b[0], b[1], b[0]], axis=0)
+    )
 
 
 def lanes_of(shape):
@@ -106,12 +108,11 @@
     )
 
 
-def greet(wide_count, narrow_count, offsets):
+def hail(wide_count, narrow_count, offsets):
     w, n = lax.axis_index("wide"), lax.axis_index("narrow")
-    barrier = pltpu.get_barrier_semaphore()
     for dw, dn in offsets:
         pl.semaphore_signal(
-            barrier,
+            pltpu.get_barrier_semaphore(),
             inc=1,
             device_id=(
                 lax.rem(w + dw + wide_count, wide_count),
@@ -119,7 +120,10 @@
             ),
             device_id_type=MESH,
         )
-    pl.semaphore_wait(barrier, len(offsets))
+
+
+def hear(offsets):
+    pl.semaphore_wait(pltpu.get_barrier_semaphore(), len(offsets))
 
 
 GATHER = [(dw, dn) for dw in (-2, -1, 0, 1) for dn in (-1, 0, 1)]
@@ -134,6 +138,7 @@
     occupied_ref,
     out_ref,
     meta_ref,
+    cells_ref,
     own_ref,
     held,
     send_sem,
@@ -141,6 +146,7 @@
 ):
     w, n = lax.axis_index("wide"), lax.axis_index("narrow")
     reach = [(dw, dn) for dw in (-2, -1, 0, 1, 2) for dn in (-1, 0, 1) if (dw, dn) != (0, 0)]
+    hail(wide_count, narrow_count, reach)
     slots = [(a, b) for a in (0, 1) for b in (0, 1)]
     numbers = [centres_ref[a, b, c] for a, b in slots for c in range(3)]
     numbers += [anchors_ref[a, b, c].astype(F32) for a, b in slots for c in range(3)]
@@ -152,7 +158,7 @@
     for s, (a, b) in enumerate(slots):
         own_ref[3 * s : 3 * s + 3, :] = tractions_ref[a, b]
     own_ref[12:16, :] = jnp.broadcast_to(line, (4, NODES))
-    greet(wide_count, narrow_count, reach)
+    hear(reach)
     copies = []
     for place, (dw, dn) in enumerate(GATHER):
         if (dw, dn) == (0, 0):
@@ -173,10 +179,12 @@
     own = GATHER.index((0, 0))
     out_ref[own] = own_ref[...]
     meta_ref[own : own + 1, :] = own_ref[12:13, 0:128]
+    cells_ref[own : own + 1, :] = own_ref[12:13, 0:128].astype(jnp.int32)
     for place, copy in copies:
         copy.wait_recv()
         out_ref[place] = held[place]
         meta_ref[place : place + 1, :] = held[place, 12:13, 0:128]
+        cells_ref[place : place + 1, :] = held[place, 12:13, 0:128].astype(jnp.int32)
     for place, copy in copies:
         copy.wait_send()
 
@@ -187,11 +195,6 @@
     own = GATHER.index((0, 0))
     out_ref[...] = jnp.zeros_like(out_ref)
     columns[...] = jnp.zeros_like(columns)
-    padded = jnp.concatenate([off_ref[...], jnp.zeros((5, NODES), F32)], axis=0)
-    turned = jnp.transpose(padded)
-    for c in range(3):
-        offcol[c] = jnp.broadcast_to(turned[:, c : c + 1], (NODES, 128))
-
     for s in range(SLOTS_DEV):
         for j in range(1 + NEAR):
             if j == 0:
@@ -239,69 +242,82 @@
         out_ref[3 * s : 3 * s + 3, :] = alive * result[0:3, :]
 
 
-def sphere_weights(wide_count, narrow_count, index, meta_ref, off_ref):
+def columns_of(off_ref, offcol):
+    padded = jnp.concatenate([off_ref[...], jnp.zeros((5, NODES), F32)], axis=0)
+    turned = jnp.transpose(padded)
+    for c in range(3):
+        offcol[c] = jnp.broadcast_to(turned[:, c : c + 1], (NODES, 128))
+
+
+def sphere_weights(sizes, dw, dn, s, meta_ref, cells_ref, off_ref, offcol, tz_ref):
+    wide_count, narrow_count = sizes
     w, n = lax.axis_index("wide"), lax.axis_index("narrow")
     size_x, size_y = GRID // wide_count, GRID // narrow_count
-    dw = index // 8 - 2
-    dn = (index // 4) % 2 - 1
-    s = index % 4
     place = (dw + 2) * 3 + dn + 1
-    anchor = [meta_ref[place, 12 + 3 * s + c].astype(jnp.int32) for c in range(3)]
+    anchor = [cells_ref[place, 12 + 3 * s + c] for c in range(3)]
     centre = [meta_ref[place, 3 * s + c] for c in range(3)]
+    alive = jnp.where(meta_ref[place, 24 + s] > 0.5, spread_norm, 0.0)
     low_x = anchor[0] - size_x * lax.rem(w + dw + wide_count, wide_count) + size_x * dw
     low_y = anchor[1] - size_y * lax.rem(n + dn + narrow_count, narrow_count) + size_y * dn
-    active = (meta_ref[place, 24 + s] > 0.5) & (low_x + BLOCK > 0) & (low_y + BLOCK > 0)
-
-    def weights(c, low, count):
+    low_z = anchor[2] % 8
+
+    def weights(cell, position, base, low, factor):
+        distance = position - (base + cell).astype(F32)
+        inside = (cell >= low) & (cell < low + BLOCK)
+        return jnp.where(inside, jnp.exp(-distance * distance) * factor, 0.0)
+
+    def rows(c, low, count, factor):
         cell = lax.broadcasted_iota(jnp.int32, (count, NODES), 0)
-        position = centre[c] + off_ref[c : c + 1, :]
-        distance = position - ((anchor[c] - low) + cell).astype(F32)
-        inside = (cell >= low) & (cell < low + BLOCK)
-        return jnp.where(inside, jnp.exp(-distance * distance), 0.0)
-
-    return (
-        place,
-        s,
-        active,
-        anchor[2],
-        lambda: (weights(0, low_x, size_x), weights(1, low_y, size_y), weights(2, anchor[2] % 8, 32)),
-    )
-
-
-def stacked(values, second):
-    high, low = split(values)
-    return jnp.concatenate([high, low, high] if second else [high, high, low], axis=0)
-
-
-def spread_kernel(wide_count, narrow_count, meta_ref, held_ref, off_ref, tz_ref, out_ref, a_high, a_low, total, turned):
+        return weights(cell, centre[c] + off_ref[c : c + 1, :], anchor[c] - low, low, factor)
+
+    lane = lanes_of((NODES, 128))
+    wz = weights(lane % 32, centre[2] + offcol[2], anchor[2] - low_z, low_z, 1.0)
+    high = wz.astype(BF16).astype(F32)
+    left = jnp.where(lane < 64, high, jnp.where(lane < 96, wz - high, 0.0)).astype(BF16)
+    tile = anchor[2] // 8
+    t_high, t_low = split(jnp.concatenate([tz_ref[tile + t] for t in range(4)], axis=0))
+    right = jnp.concatenate([t_high, t_low, t_high, jnp.zeros((32, GRID), BF16)], axis=0)
+    along_z = split(dot(left, right))
+    return place, rows(0, low_x, size_x, alive), rows(1, low_y, 16 if dn else size_y, 1.0), along_z
+
+
+def pair_loop(body, unroll=1):
+    for dn in (-1, 0):
+
+        def step(index, carry):
+            body(index // 2 - 2, dn, index % 2)
+            return carry
+
+        lax.fori_loop(0, 6, step, 0, unroll=unroll)
+
+
+def spread(sizes, meta_ref, cells_ref, held_ref, off_ref, tz_ref, out_ref, offcol, a_high, a_low, total, turned):
     total[...] = jnp.zeros_like(total)
 
-    def sphere(index, carry):
-        place, s, active, low_z, weights = sphere_weights(wide_count, narrow_count, index, meta_ref, off_ref)
-
-        @pl.when(active)
-        def _():
-            wx, wy, wz = weights()
-            table = tz_ref[pl.ds(pl.multiple_of(low_z // 8 * 8, 8), 32), :]
-            along_z = split(
-                dot(jnp.transpose(stacked(wz, False).astype(F32)).astype(BF16), stacked(table, True))
+    def pair(dw, dn, which):
+        span = 16 if dn else 32
+        sums = []
+        for member in (0, 1):
+            s = 2 * which + member
+            place, wx, wy, along_z = sphere_weights(sizes, dw, dn, s, meta_ref, cells_ref, off_ref, offcol, tz_ref)
+            planar = jnp.concatenate(
+                [wy * held_ref[place, pl.ds(s * 3 + c, 1), :] for c in range(3)], axis=0
             )
-            planar = jnp.concatenate(
-                [
-                    wy * (spread_norm * held_ref[place, pl.ds(s * 3 + c, 1), :])
-                    for c in range(3)
-                ],
-                axis=0,
-            )
+            size = 3 * span
             for x in range(8):
                 high, low = split(planar * wx[x : x + 1, :])
-                a_high[x * 96 : x * 96 + 96, :] = high
-                a_low[x * 96 : x * 96 + 96, :] = low
-            total[...] += dot3((a_high[...], a_low[...]), along_z)
-
-        return carry
-
-    lax.fori_loop(0, 24, sphere, 0)
+                a_high[member, x * size : x * size + size, :] = high
+                a_low[member, x * size : x * size + size, :] = low
+            rows = slice(0, 8 * size)
+            sums.append(dot3((a_high[member, rows, :], a_low[member, rows, :]), along_z))
+        both = sums[0] + sums[1]
+        if dn == 0:
+            total[...] += both
+        else:
+            for block in range(24):
+                total[block * 32 : block * 32 + 16, :] += both[block * 16 : block * 16 + 16]
+
+    pair_loop(pair)
     for x in range(8):
         block = jnp.concatenate([total[x * 96 : x * 96 + 96, :], jnp.zeros((32, GRID), F32)], axis=0)
         turned[pl.ds(x, GRID, stride=8), :] = jnp.transpose(block)
@@ -311,7 +327,7 @@
         out_ref[:, :, :, g * 128 : g * 128 + 128] = packed[g].reshape(32, 2, 8, 128)
 
 
-def interp_kernel(wide_count, narrow_count, meta_ref, off_ref, tz_ref, mesh_ref, out_ref, m_high, m_low, turned):
+def interpolate(sizes, meta_ref, cells_ref, off_ref, tz_ref, mesh_ref, out_ref, offcol, m_high, m_low, h_high, h_low, turned):
     out_ref[...] = jnp.zeros_like(out_ref)
     groups = [mesh_ref[:, :, :, g * 128 : g * 128 + 128].reshape(64, 8, 128) for g in range(3)]
     unpacked = unpack_lanes(*groups)
@@ -321,32 +337,34 @@
         high, low = split(block[:96])
         m_high[x * 96 : x * 96 + 96, :] = high
         m_low[x * 96 : x * 96 + 96, :] = low
-
-    def sphere(index, carry):
-        place, s, active, low_z, weights = sphere_weights(wide_count, narrow_count, index, meta_ref, off_ref)
-
-        @pl.when(active)
-        def _():
-            wx, wy, wz = weights()
-            table = tz_ref[pl.ds(pl.multiple_of(low_z // 8 * 8, 8), 32), :]
-            along_z = split(
-                dot(jnp.transpose(stacked(table, True).astype(F32)).astype(BF16), stacked(wz, False))
+        for c in range(3):
+            target = slice(x * 48 + c * 16, x * 48 + c * 16 + 16)
+            h_high[target, :] = high[c * 32 : c * 32 + 16]
+            h_low[target, :] = low[c * 32 : c * 32 + 16]
+
+    def pair(dw, dn, which):
+        span = 16 if dn else 32
+        size = 3 * span
+        for member in (0, 1):
+            s = 2 * which + member
+            place, wx, wy, along_z = sphere_weights(sizes, dw, dn, s, meta_ref, cells_ref, off_ref, offcol, tz_ref)
+            left = (h_high[...], h_low[...]) if dn else (m_high[...], m_low[...])
+            turn = ((1,), (1,))
+            found = dot(
+                jnp.concatenate([left[0], left[0], left[1]], axis=1),
+                jnp.concatenate([along_z[0], along_z[1], along_z[0]], axis=1),
+                turn,
             )
-            found = dot3((m_high[...], m_low[...]), along_z)
-            summed = found[0:96] * wx[0:1, :]
+            summed = found[0:size] * wx[0:1, :]
             for x in range(1, 8):
-                summed = summed + found[x * 96 : x * 96 + 96] * wx[x : x + 1, :]
-            rows = [
-                jnp.sum(summed[c * 32 : c * 32 + 32] * wy, axis=0, keepdims=True) * spread_norm
-                for c in range(3)
-            ]
-            owner = index // 4
+                summed = summed + found[x * size : x * size + size] * wx[x : x + 1, :]
+            owner = (dw + 2) * 2 + dn + 1
             for c in range(3):
-                out_ref[owner, pl.ds(s * 3 + c, 1), :] = rows[c]
-
-        return carry
-
-    lax.fori_loop(0, 24, sphere, 0)
+                out_ref[owner, pl.ds(s * 3 + c, 1), :] = jnp.sum(
+                    summed[c * span : c * span + span] * wy, axis=0, keepdims=True
+                )
+
+    pair_loop(pair, 2)
 
 
 class Exchange:
@@ -390,11 +408,12 @@
 def transform_kernel(
     wide_count,
     narrow_count,
-    mesh_ref,
     list_ref,
     meta_ref,
+    cells_ref,
     held_ref,
     off_ref,
+    tz_ref,
     pairs_ref,
     gap_ref,
     angles_ref,
@@ -402,6 +421,11 @@
     out_ref,
     near_ref,
     contacts_ref,
+    a_high,
+    a_low,
+    total,
+    turned,
+    mesh_ref,
     wide_in,
     narrow_out,
     narrow_in,
@@ -434,11 +458,12 @@
     w, n = lax.axis_index("wide"), lax.axis_index("narrow")
     load = pltpu.make_async_copy(tables, t_x, table_sem)
     load.start()
-    greet(
-        wide_count,
-        narrow_count,
-        [(step, 0) for step in range(1, wide_count)] + [(0, step) for step in range(1, narrow_count)],
-    )
+    reach = [(step, 0) for step in range(1, wide_count)] + [(0, step) for step in range(1, narrow_count)]
+    sizes = (wide_count, narrow_count)
+    hail(*sizes, reach)
+    columns_of(off_ref, offcol)
+    spread(sizes, meta_ref, cells_ref, held_ref, off_ref, tz_ref, mesh_ref, offcol, a_high, a_low, total, turned)
+    hear(reach)
 
     def exchanges(axis, source, target, way):
         if axis == "wide":
@@ -536,16 +561,6 @@
         return carry
 
     lax.fori_loop(1, wide_count, begin_column, 0)
-    for half in (0, 1):
-        narrow_go[half].arrive()
-        for piece in range(8):
-            groups = [narrow_in[piece, half, :, g * 128 : g * 128 + 128] for g in range(3)]
-            unpacked = unpack_lanes(*groups)
-            for j in range(4):
-                lines[half * 128 + j * 32 : half * 128 + j * 32 + 32, piece * 128 : piece * 128 + 128] = unpacked[j]
-        rows = slice(half * 128, half * 128 + 128)
-        spectrum[rows, :] = dot3(split(lines[rows, :]), (t_yf[0], t_yf[1]))
-
     row = lax.broadcasted_iota(jnp.int32, (32, 1), 0)
     k_x = (n * 16 + row % 16).astype(F32)
     nyquist_x = jnp.where((row >= 16) & (k_x < 0.5), 128.0, 0.0)
@@ -567,9 +582,9 @@
     def derive_y(values):
         return turn_y * jnp.concatenate([values[:, 128:], values[:, :128]], axis=1)
 
-    def filtered(j, carry):
-        k_z = (w * 4 + j).astype(F32)
-        bases = [pl.multiple_of(half * 128 + j * 32, 32) for half in (0, 1)]
+    def filtered(index, group):
+        k_z = (w * 4 + group * 2 + index).astype(F32)
+        bases = [pl.multiple_of(group * 128 + half * 64 + index * 32, 32) for half in (0, 1)]
         fields = [
             [spectrum[pl.ds(bases[half], 32), c * 256 : c * 256 + 256] for c in range(3)]
             for half in (0, 1)
@@ -598,11 +613,18 @@
                 spectrum[pl.ds(bases[half], 32), c * 256 : c * 256 + 256] = factor * (
                     values[c] + gradient[c] - nyquist[c] * edge
                 )
-        return carry
-
-    lax.fori_loop(0, 4, filtered, 0)
+        return group
+
     for half in (0, 1):
+        narrow_go[half].arrive()
+        for piece in range(8):
+            groups = [narrow_in[piece, half, :, g * 128 : g * 128 + 128] for g in range(3)]
+            unpacked = unpack_lanes(*groups)
+            for j in range(4):
+                lines[half * 128 + j * 32 : half * 128 + j * 32 + 32, piece * 128 : piece * 128 + 128] = unpacked[j]
         rows = slice(half * 128, half * 128 + 128)
+        spectrum[rows, :] = dot3(split(lines[rows, :]), (t_yf[0], t_yf[1]))
+        lax.fori_loop(0, 2, filtered, half)
         lines[rows, :] = dot3(split(spectrum[rows, :]), (t_yi[0], t_yi[1]))
         for target in range(8):
             groups = [
@@ -663,13 +685,24 @@
 def contact_kernel(
     wide_count,
     narrow_count,
-    part_ref,
+    meta_ref,
+    cells_ref,
+    off_ref,
+    tz_ref,
+    mesh_ref,
     near_ref,
     static_ref,
     centre_ref,
     velocity_ref,
     force_ref,
     moved_ref,
+    offcol,
+    m_high,
+    m_low,
+    h_high,
+    h_low,
+    turned,
+    part_ref,
     part_in,
     tile_out,
     tile_in,
@@ -694,13 +727,18 @@
             lax.rem(n + dn + narrow_count, narrow_count),
         )
 
-    greet(
-        wide_count,
-        narrow_count,
+    reach = (
         [(step, 0) for step in range(1, wide_count)]
         + [(0, step) for step in range(1, narrow_count)]
-        + [(-2, -1), (-1, -1), (2, 1), (1, 1)],
-    )
+        + [(-2, -1), (-1, -1), (2, 1), (1, 1)]
+    )
+    sizes = (wide_count, narrow_count)
+    hail(*sizes, reach)
+    columns_of(off_ref, offcol)
+    interpolate(
+        sizes, meta_ref, cells_ref, off_ref, tz_ref, mesh_ref, part_ref, offcol, m_high, m_low, h_high, h_low, turned
+    )
+    hear(reach)
     own = PARTIAL.index((0, 0))
     pieces = [part_ref[p] + near_ref[...] if p == own else part_ref[p] for p in range(6)]
     means = [jnp.sum(piece, axis=1, keepdims=True) * (1.0 / NODES) for piece in pieces]
@@ -859,11 +897,11 @@
     shape = jax.ShapeDtypeStruct
     dma = pltpu.SemaphoreType.DMA
 
-    held, metas = pl.pallas_call(
+    held, metas, cells = pl.pallas_call(
         functools.partial(gather_kernel, *sizes),
-        out_shape=(shape((12, 16, NODES), F32), shape((12, 128), F32)),
+        out_shape=(shape((12, 16, NODES), F32), shape((12, 128), F32), shape((12, 128), jnp.int32)),
         in_specs=[VMEM_SPEC, SMEM_SPEC, SMEM_SPEC, SMEM_SPEC],
-        out_specs=(VMEM_SPEC, VMEM_SPEC),
+        out_specs=(VMEM_SPEC,) * 3,
         scratch_shapes=[
             pltpu.VMEM((16, NODES), F32),
             pltpu.VMEM((12, 16, NODES), F32),
@@ -874,23 +912,8 @@
         name="gather",
     )(tractions, centers, anchors, occupied)
 
-    table_z = trig_table(4)
-    wrapped_z = np.concatenate([table_z, table_z[:, :32]], axis=1).T.astype(np.float32)
-    mesh = pl.pallas_call(
-        functools.partial(spread_kernel, *sizes),
-        out_shape=shape((32, 2, 8, 384), F32),
-        in_specs=[SMEM_SPEC, VMEM_SPEC, VMEM_SPEC, VMEM_SPEC],
-        out_specs=VMEM_SPEC,
-        scratch_shapes=[
-            pltpu.VMEM((768, NODES), BF16),
-            pltpu.VMEM((768, NODES), BF16),
-            pltpu.VMEM((768, GRID), F32),
-            pltpu.VMEM((GRID * 8, 128), F32),
-        ],
-        compiler_params=params(),
-        name="spread",
-    )(metas, held, node_offsets, wrapped_z)
-
+    table_z = trig_table(2)
+    wrapped_z = np.concatenate([table_z, table_z[:, :32]], axis=1).T.astype(np.float32).reshape(36, 8, GRID)
     table_x = trig_table(16)
     table_y = trig_table(128)
     turned_x = np.ascontiguousarray(table_x.T)
@@ -903,9 +926,14 @@
             shape((16, NODES), F32),
             shape((wide_count * narrow_count, NODES), F32),
         ),
-        in_specs=[VMEM_SPEC, SMEM_SPEC, SMEM_SPEC] + [VMEM_SPEC] * 5 + [HBM_SPEC],
+        in_specs=[SMEM_SPEC] * 3 + [VMEM_SPEC] * 6 + [HBM_SPEC],
         out_specs=(VMEM_SPEC,) * 3,
         scratch_shapes=[
+            pltpu.VMEM((2, 768, NODES), BF16),
+            pltpu.VMEM((2, 768, NODES), BF16),
+            pltpu.VMEM((768, GRID), F32),
+            pltpu.VMEM((GRID * 8, 128), F32),
+            pltpu.VMEM((32, 2, 8, 384), F32),
             pltpu.VMEM((32, 2, 8, 384), F32),
             pltpu.VMEM((8, 2, 32, 384), F32),
             pltpu.VMEM((8, 2, 32, 384), F32),
@@ -938,39 +966,33 @@
         compiler_params=params(1),
         name="transform",
     )(
-        mesh,
         near_list.reshape(4, NEAR),
         metas,
+        cells,
         held,
         node_offsets,
+        wrapped_z,
         contact_pairs,
         contact_gap,
         contact_angles,
         tables,
     )
-
-    part = pl.pallas_call(
-        functools.partial(interp_kernel, *sizes),
-        out_shape=shape((6, 16, NODES), F32),
-        in_specs=[SMEM_SPEC, VMEM_SPEC, VMEM_SPEC, VMEM_SPEC],
-        out_specs=VMEM_SPEC,
-        scratch_shapes=[
-            pltpu.VMEM((768, GRID), BF16),
-            pltpu.VMEM((768, GRID), BF16),
-            pltpu.VMEM((GRID * 8, 128), F32),
-        ],
-        compiler_params=params(),
-        name="interpolate",
-    )(metas, node_offsets, wrapped_z, mesh)
 
     centre_rows = jnp.broadcast_to(jnp.pad(centers.reshape(12, 1), ((0, 4), (0, 0))), (16, 128))
     devices = wide_count * narrow_count
     velocity, force, moved = pl.pallas_call(
         functools.partial(contact_kernel, *sizes),
         out_shape=(shape((16, NODES), F32), shape((CONT_DEV, 128), F32), shape((16, 128), F32)),
-        in_specs=[VMEM_SPEC] * 4,
+        in_specs=[SMEM_SPEC] * 2 + [VMEM_SPEC] * 6,
         out_specs=(VMEM_SPEC,) * 3,
         scratch_shapes=[
+            pltpu.VMEM((3, NODES, 128), F32),
+            pltpu.VMEM((768, GRID), BF16),
+            pltpu.VMEM((768, GRID), BF16),
+            pltpu.VMEM((384, GRID), BF16),
+            pltpu.VMEM((384, GRID), BF16),
+            pltpu.VMEM((GRID * 8, 128), F32),
+            pltpu.VMEM((6, 16, NODES), F32),
             pltpu.VMEM((6, 16, NODES), F32),
             pltpu.VMEM((8, 128), F32),
             pltpu.VMEM((8, 8, 128), F32),
@@ -988,7 +1010,7 @@
         ],
         compiler_params=params(2),
         name="contacts",
-    )(part, near, contacts, centre_rows)
+    )(metas, cells, node_offsets, wrapped_z, mesh, near, contacts, centre_rows)
     return (
         velocity[:12].reshape(2, 2, 3, NODES),
         force[:, 0],

time: 136 us -> 126 us (0.926)
  Pallas kernels: 130 us -> 120 us
    pallas_call x2 -> x0, Pallas kernels: 18.8 us -> none  [the longest x1 9.45 us: local(): pl.pallas_call(functools.partial(spread_kernel, *sizes), out_shape=shape(...]
    pallas_call x1, Pallas kernels: 23.1 us -> 35 us  [local(): pl.pallas_call(functools.partial(contact_kernel, *sizes), out_shape=(shap...]
    pallas_call x1, Pallas kernels: 71.9 us -> 68.6 us  [local(): pl.pallas_call(functools.partial(transform_kernel, *sizes), out_shape=(sh...]
where the time goes in v3:
time: 126 us
  Pallas kernels  120 us (95%)
  local copies, waits for them, and re-layouts  5.7 us (5%)
    pallas_call x1, Pallas kernels, local(): pl.pallas_call(functools.partial(transform_kernel, *sizes), out_shape=(sh...  68.6 us
    pallas_call x1, Pallas kernels, local(): pl.pallas_call(functools.partial(contact_kernel, *sizes), out_shape=(shap...  35 us
    pallas_call x1, Pallas kernels, local(): pl.pallas_call(functools.partial(gather_kernel, *sizes), out_shape=(shape...  16 us
    unnamed x24, local copies, waits for them, and re-layouts  4.13 us

profile of v3, /device:TPU:1, one launch (start us, length us, event | category | flops | bytes accessed | tf_op | source)
XLA Modules:
  0.0 126.1 jit_solution(8887391984749148294)
XLA Ops:
  0.6 0.0 copy-start.4
  0.6 0.0 copy-start.9
  0.7 0.0 copy-start.6
  0.7 0.7 copy.18.tractions_ref
  1.4 0.0 copy-done.4
  1.4 0.0 copy-done.9
  1.4 0.0 copy-done.6
  1.4 0.0 copy-start.8
  1.4 16.0 %gather.1 = (f32[12,16,256]{2,1,0:T(8,128)S(1)}, f32[12,128]{1,0:T(8,128)S(1)}, s32[12,128]{1,0:T(8,128)S(1)}) custom-call(f32[2,2,3,256]{3,2,1,0:T(4,128)S(1)} %copy.18.tractions_ref, f32[2,2,3]{2,1,0:T(2,128)S(1)} %copy-done.4, s32[2,2,3]{2,1,0:T(2,128)S(1)} %copy-done.6, s32[2,2]{1,0:T(2,128)S(1)} %copy-done.9), custom_call_target="tpu_custom_call" | custom-call | tf_op jit(solution)/shard_map/gather/pallas_call | solution.py:900
  17.4 0.0 copy-start.3
  17.4 0.0 copy-start.5
  17.5 0.0 copy-start.7
  17.5 0.0 copy-start.10
  17.5 0.0 copy-done.8
  17.5 0.6 copy-done.3
  18.1 0.0 copy-done.5
  18.1 0.0 copy-done.7
  18.1 0.0 copy-done.10
  18.1 0.0 copy-start
  18.1 1.0 copy-done
  19.1 0.0 copy-start.2
  19.1 1.1 copy-done.2
  20.2 0.0 copy-start.1
  20.2 68.6 %transform.1 = (f32[32,2,8,384]{3,2,1,0:T(8,128)S(1)}, f32[16,256]{1,0:T(8,128)S(1)}, f32[256,256]{1,0:T(8,128)S(1)}) custom-call(s32[4,2]{1,0:T(4,128)S(1)} %bitcast.5, f32[12,128]{1,0:T(8,128)S(1)} %get-tuple-element.12.meta_ref, s32[12,128]{1,0:T(8,128)S(1)} %get-tuple-element.13.cells_ref, f32[12,16,256]{2,1,0:T(8,128)S(1)} %get-tuple-element.14.held_ref, ...), custom_call_target="tpu_custom_call" | custom-call | tf_op jit(solution)/shard_map/transform/pallas_call | solution.py:922
  88.9 0.1 reshape.16
  89.0 0.1 broadcast_in_dim.8.centre_ref
  89.0 0.0 copy-done.1
  89.1 35.0 %contacts.1 = (f32[16,256]{1,0:T(8,128)S(1)}, f32[32,128]{1,0:T(8,128)S(1)}, f32[16,128]{1,0:T(8,128)S(1)}) custom-call(f32[12,128]{1,0:T(8,128)S(1)} %get-tuple-element.12.meta_ref, s32[12,128]{1,0:T(8,128)S(1)} %get-tuple-element.13.cells_ref, f32[3,256]{1,0:T(4,128)S(1)} %copy-done.3, f32[36,8,256]{2,1,0:T(8,128)S(1)} %copy-done.1, ...), custom_call_target="tpu_custom_call" | custom-call | tf_op jit(solution)/shard_map/contacts/pallas_call | solution.py:983
  124.1 0.6 copy.21
  124.7 0.1 slice_reduce_fusion.1
  124.8 0.7 reshape_squeeze.3
  125.5 0.6 slice_reduce_fusion
  (2 shorter events, 0.0 us)
Async XLA Ops:
  0.6 0.8 copy-start.4
  0.6 0.8 copy-start.9
  0.7 0.8 copy-start.6
  1.4 16.1 %copy-start.8 = (f32[2,32]{1,0:T(2,128)S(1)}, f32[2,32]{1,0:T(2,128)}, u32[]{:S(2)}) copy-start(f32[2,32]{1,0:T(2,128)} %angles_ref.1) | copy-start | bytes 772
  17.4 0.7 copy-start.3
  17.4 0.7 copy-start.5
  17.5 0.7 copy-start.7
  17.5 0.7 copy-start.10
  18.1 1.0 copy-start
  19.1 1.1 copy-start.2
  20.2 68.8 %copy-start.1 = (f32[36,8,256]{2,1,0:T(8,128)S(1)}, f32[36,8,256]{2,1,0:T(8,128)}, u32[]{:S(2)}) copy-start(f32[36,8,256]{2,1,0:T(8,128)} %constant.7.clone.tz_ref) | copy-start | bytes 884740

commit v4 on v3

--- a/solution.py
+++ b/solution.py
@@ -281,14 +281,12 @@
     return place, rows(0, low_x, size_x, alive), rows(1, low_y, 16 if dn else size_y, 1.0), along_z
 
 
-def pair_loop(body, unroll=1):
-    for dn in (-1, 0):
-
-        def step(index, carry):
-            body(index // 2 - 2, dn, index % 2)
-            return carry
-
-        lax.fori_loop(0, 6, step, 0, unroll=unroll)
+def pair_loop(body, dn, unroll=1):
+    def step(index, carry):
+        body(index // 2 - 2, dn, index % 2)
+        return carry
+
+    lax.fori_loop(0, 6, step, 0, unroll=unroll)
 
 
 def spread(sizes, meta_ref, cells_ref, held_ref, off_ref, tz_ref, out_ref, offcol, a_high, a_low, total, turned):
@@ -317,7 +315,8 @@
             for block in range(24):
                 total[block * 32 : block * 32 + 16, :] += both[block * 16 : block * 16 + 16]
 
-    pair_loop(pair)
+    pair_loop(pair, -1)
+    pair_loop(pair, 0)
     for x in range(8):
         block = jnp.concatenate([total[x * 96 : x * 96 + 96, :], jnp.zeros((32, GRID), F32)], axis=0)
         turned[pl.ds(x, GRID, stride=8), :] = jnp.transpose(block)
@@ -327,14 +326,53 @@
         out_ref[:, :, :, g * 128 : g * 128 + 128] = packed[g].reshape(32, 2, 8, 128)
 
 
-def interpolate(sizes, meta_ref, cells_ref, off_ref, tz_ref, mesh_ref, out_ref, offcol, m_high, m_low, h_high, h_low, turned):
-    out_ref[...] = jnp.zeros_like(out_ref)
+def mean_weights(sizes, meta_ref, cells_ref, off_ref, tz_ref, offcol, full, half):
+    def pair(dw, dn, which):
+        span = 16 if dn else 32
+        for member in (0, 1):
+            s = 2 * which + member
+            place, wx, wy, along_z = sphere_weights(
+                sizes, dw, dn, s, meta_ref, cells_ref, off_ref, offcol, tz_ref
+            )
+            wy = wy * (1.0 / NODES)
+            left = split(jnp.concatenate([wy * wx[x : x + 1, :] for x in range(8)], axis=0))
+            target = half if dn else full
+            target[(dw + 2) * 4 + s] = dot3(left, along_z)
+
+    pair_loop(pair, -1)
+    pair_loop(pair, 0)
+
+
+def mean_velocities(values, full, half, rows_ref):
+    rows_ref[...] = jnp.zeros_like(rows_ref)
+    for dn in (-1, 0):
+        span = 16 if dn else 32
+
+        def sphere(index, carry):
+            source = half if dn else full
+            tiles = [jnp.zeros((8, GRID), F32) for _ in range(3)]
+            for x in range(8):
+                for y in range(0, span, 8):
+                    weight = source[index, x * span + y : x * span + y + 8, :]
+                    for c in range(3):
+                        at = x * 96 + c * 32 + y
+                        tiles[c] = tiles[c] + values[at : at + 8, :] * weight
+            piece = (index // 4) * 2 + dn + 1
+            for c in range(3):
+                rows_ref[piece, pl.ds((index % 4) * 3 + c, 1), :] = jnp.sum(tiles[c], axis=0, keepdims=True)
+            return carry
+
+        lax.fori_loop(0, 12, sphere, 0)
+
+
+def unpack_mesh(mesh_ref, values, m_high, m_low, h_high, h_low, turned):
     groups = [mesh_ref[:, :, :, g * 128 : g * 128 + 128].reshape(64, 8, 128) for g in range(3)]
     unpacked = unpack_lanes(*groups)
     turned[...] = jnp.stack(unpacked, axis=1).reshape(GRID * 8, 128)
     for x in range(8):
-        block = jnp.transpose(turned[pl.ds(x, GRID, stride=8), :])
-        high, low = split(block[:96])
+        block = jnp.transpose(turned[pl.ds(x, GRID, stride=8), :])[:96]
+        values[x * 96 : x * 96 + 96, :] = block
+        high, low = split(block)
         m_high[x * 96 : x * 96 + 96, :] = high
         m_low[x * 96 : x * 96 + 96, :] = low
         for c in range(3):
@@ -342,6 +380,10 @@
             h_high[target, :] = high[c * 32 : c * 32 + 16]
             h_low[target, :] = low[c * 32 : c * 32 + 16]
 
+
+def interpolate(
+    sizes, lower, meta_ref, cells_ref, off_ref, tz_ref, out_ref, offcol, m_high, m_low, h_high, h_low
+):
     def pair(dw, dn, which):
         span = 16 if dn else 32
         size = 3 * span
@@ -364,7 +406,30 @@
                     summed[c * span : c * span + span] * wy, axis=0, keepdims=True
                 )
 
-    pair_loop(pair, 2)
+    pair_loop(pair, lower, 2)
+
+
+AROUND = [(dw, dn) for dw in (-1, 0, 1) for dn in (-1, 0, 1)]
+PARTIAL = [(dw, dn) for dw in (-2, -1, 0) for dn in (-1, 0)]
+
+
+def shift_narrow(values, dn, narrow_count):
+    if dn == 0:
+        return values
+    place = lanes_of(values.shape) % narrow_count
+    edge = 0 if dn == 1 else narrow_count - 1
+    total = values.shape[-1]
+    return jnp.where(
+        place == edge,
+        roll(values, (dn - dn * narrow_count) % total),
+        roll(values, dn % total),
+    )
+
+
+def shift_wide(values, dw, narrow_count):
+    if dw == 0:
+        return values
+    return roll(values, (dw * narrow_count) % values.shape[-1])
 
 
 class Exchange:
@@ -405,7 +470,7 @@
         lax.fori_loop(1, self.count, step, 0)
 
 
-def transform_kernel(
+def flow_kernel(
     wide_count,
     narrow_count,
     list_ref,
@@ -418,9 +483,32 @@
     gap_ref,
     angles_ref,
     tables,
-    out_ref,
+    velocity_ref,
+    force_ref,
+    moved_ref,
     near_ref,
-    contacts_ref,
+    m_high,
+    m_low,
+    h_high,
+    h_low,
+    full_means,
+    half_means,
+    mean_rows,
+    part_ref,
+    part_in,
+    tile_out,
+    tile_in,
+    table_out,
+    table_in,
+    edges,
+    around,
+    loads,
+    part_send,
+    part_recv,
+    tile_send,
+    tile_recv,
+    spread_send,
+    spread_recv,
     a_high,
     a_low,
     total,
@@ -458,7 +546,11 @@
     w, n = lax.axis_index("wide"), lax.axis_index("narrow")
     load = pltpu.make_async_copy(tables, t_x, table_sem)
     load.start()
-    reach = [(step, 0) for step in range(1, wide_count)] + [(0, step) for step in range(1, narrow_count)]
+    reach = (
+        [(step, 0) for step in range(1, wide_count)]
+        + [(0, step) for step in range(1, narrow_count)]
+        + [(-2, -1), (-1, -1), (2, 1), (1, 1)]
+    )
     sizes = (wide_count, narrow_count)
     hail(*sizes, reach)
     columns_of(off_ref, offcol)
@@ -529,6 +621,7 @@
     near_field(
         (wide_count, narrow_count), list_ref, meta_ref, held_ref, off_ref, near_ref, offcol, source, columns
     )
+    mean_weights(sizes, meta_ref, cells_ref, off_ref, tz_ref, offcol, full_means, half_means)
     load.wait()
     t_yf[...] = jnp.zeros_like(t_yf)
     for part in (0, 1):
@@ -648,78 +741,23 @@
     lax.fori_loop(1, wide_count, end_column, 0)
     for step in range(1, narrow_count):
         line_copy(step).wait_send()
-    contacts_ref[...] = column_in[...].reshape(wide_count * narrow_count, NODES)
+    fields = jnp.transpose(column_in[...].reshape(wide_count * narrow_count, NODES))
+    first, second, gap = fields[0:32], fields[32:64], fields[160:192]
+    normal = [fields[64 + 32 * c : 96 + 32 * c] for c in range(3)]
+    for place in range(9):
+        for s in range(SLOTS_DEV):
+            mark = jnp.where(second == float(place * SLOTS_DEV + s), -1.0, 0.0)
+            if place == 4:
+                mark = mark + jnp.where(first == float(s), 1.0, 0.0)
+            for c in range(3):
+                edges[place, 3 * s + c] = mark * normal[c]
     for group in (wide_go, narrow_go, narrow_return):
         for half in (0, 1):
             group[half].sent()
     for half in (0, 1):
         wide_return[half].arrive()
-        out_ref[:, half] = wide_home[:, half]
-    for half in (0, 1):
-        wide_return[half].sent()
-
-
-AROUND = [(dw, dn) for dw in (-1, 0, 1) for dn in (-1, 0, 1)]
-PARTIAL = [(dw, dn) for dw in (-2, -1, 0) for dn in (-1, 0)]
-
-
-def shift_narrow(values, dn, narrow_count):
-    if dn == 0:
-        return values
-    place = lanes_of(values.shape) % narrow_count
-    edge = 0 if dn == 1 else narrow_count - 1
-    total = values.shape[-1]
-    return jnp.where(
-        place == edge,
-        roll(values, (dn - dn * narrow_count) % total),
-        roll(values, dn % total),
-    )
-
-
-def shift_wide(values, dw, narrow_count):
-    if dw == 0:
-        return values
-    return roll(values, (dw * narrow_count) % values.shape[-1])
-
-
-def contact_kernel(
-    wide_count,
-    narrow_count,
-    meta_ref,
-    cells_ref,
-    off_ref,
-    tz_ref,
-    mesh_ref,
-    near_ref,
-    static_ref,
-    centre_ref,
-    velocity_ref,
-    force_ref,
-    moved_ref,
-    offcol,
-    m_high,
-    m_low,
-    h_high,
-    h_low,
-    turned,
-    part_ref,
-    part_in,
-    tile_out,
-    tile_in,
-    table_out,
-    table_in,
-    edges,
-    around,
-    loads,
-    part_send,
-    part_recv,
-    narrow_send,
-    narrow_recv,
-    wide_send,
-    wide_recv,
-):
-    w, n = lax.axis_index("wide"), lax.axis_index("narrow")
-    devices = wide_count * narrow_count
+    unpack_mesh(wide_home, total, m_high, m_low, h_high, h_low, turned)
+    mean_velocities(total, full_means, half_means, mean_rows)
 
     def device(dw, dn):
         return (
@@ -727,21 +765,10 @@
             lax.rem(n + dn + narrow_count, narrow_count),
         )
 
-    reach = (
-        [(step, 0) for step in range(1, wide_count)]
-        + [(0, step) for step in range(1, narrow_count)]
-        + [(-2, -1), (-1, -1), (2, 1), (1, 1)]
-    )
-    sizes = (wide_count, narrow_count)
-    hail(*sizes, reach)
-    columns_of(off_ref, offcol)
-    interpolate(
-        sizes, meta_ref, cells_ref, off_ref, tz_ref, mesh_ref, part_ref, offcol, m_high, m_low, h_high, h_low, turned
-    )
-    hear(reach)
+    devices = wide_count * narrow_count
     own = PARTIAL.index((0, 0))
-    pieces = [part_ref[p] + near_ref[...] if p == own else part_ref[p] for p in range(6)]
-    means = [jnp.sum(piece, axis=1, keepdims=True) * (1.0 / NODES) for piece in pieces]
+    means = [jnp.sum(mean_rows[p], axis=1, keepdims=True) for p in range(6)]
+    means[own] = means[own] + jnp.sum(near_ref[...], axis=1, keepdims=True) * (1.0 / NODES)
     column = jnp.concatenate(means + [jnp.zeros((32, 1), F32)], axis=0)
     line = jnp.transpose(jnp.broadcast_to(column, (128, 128)))[:8]
     tile_out[...] = jnp.where(lax.broadcasted_iota(jnp.int32, (8, 128), 0) == n, line, 0.0)
@@ -751,8 +778,8 @@
         return pltpu.make_async_remote_copy(
             src_ref=tile_out,
             dst_ref=tile_in.at[step],
-            send_sem=narrow_send.at[step],
-            recv_sem=narrow_recv.at[step],
+            send_sem=tile_send.at[step],
+            recv_sem=tile_recv.at[step],
             device_id=(w, to),
             device_id_type=MESH,
         )
@@ -762,14 +789,31 @@
         return pltpu.make_async_remote_copy(
             src_ref=table_out,
             dst_ref=table_in.at[w],
-            send_sem=wide_send.at[step],
-            recv_sem=wide_recv.at[step],
+            send_sem=spread_send.at[step],
+            recv_sem=spread_recv.at[step],
             device_id=(to, n),
             device_id_type=MESH,
         )
 
     for step in range(1, narrow_count):
         narrow_copy(step).start()
+    part_ref[...] = jnp.zeros_like(part_ref)
+    fixed = (meta_ref, cells_ref, off_ref, tz_ref, part_ref, offcol, m_high, m_low, h_high, h_low)
+    interpolate(sizes, -1, *fixed)
+    tile = tile_out[...]
+    for step in range(1, narrow_count):
+        narrow_copy(step).wait_recv()
+        tile = tile + tile_in[step]
+    table_out[...] = tile
+    table_in[w] = tile
+
+    def begin(step, carry):
+        wide_copy(step).start()
+        return carry
+
+    lax.fori_loop(1, wide_count, begin, 0)
+
+    interpolate(sizes, 0, *fixed)
     copies = []
     for place, (dw, dn) in enumerate(PARTIAL):
         if (dw, dn) == (0, 0):
@@ -784,36 +828,6 @@
         )
         copy.start()
         copies.append((place, copy))
-    tile = tile_out[...]
-    for step in range(1, narrow_count):
-        narrow_copy(step).wait_recv()
-        tile = tile + tile_in[step]
-    table_out[...] = tile
-    table_in[w] = tile
-
-    def begin(step, carry):
-        wide_copy(step).start()
-        return carry
-
-    lax.fori_loop(1, wide_count, begin, 0)
-
-    fields = jnp.transpose(static_ref[...])
-    first, second, gap = fields[0:32], fields[32:64], fields[160:192]
-    normal = [fields[64 + 32 * c : 96 + 32 * c] for c in range(3)]
-    for place in range(9):
-        for s in range(SLOTS_DEV):
-            mark = jnp.where(second == float(place * SLOTS_DEV + s), -1.0, 0.0)
-            if place == 4:
-                mark = mark + jnp.where(first == float(s), 1.0, 0.0)
-            for c in range(3):
-                edges[place, 3 * s + c] = mark * normal[c]
-
-    velocity = pieces[own]
-    for place, copy in copies:
-        copy.wait_recv()
-        velocity = velocity + part_in[place]
-    velocity_ref[...] = velocity
-
     def end(step, carry):
         wide_copy(step).wait_recv()
         return carry
@@ -866,9 +880,20 @@
     own_force = jnp.sum(jnp.where(mine, force, 0.0), axis=1, keepdims=True)
     force_ref[...] = jnp.broadcast_to(own_force, (CONT_DEV, 128))
     own_moving = jnp.sum(jnp.where(mine, moving, 0.0), axis=1, keepdims=True)
-    moved_ref[...] = centre_ref[...] + time_step * own_moving
+    row = lax.broadcasted_iota(jnp.int32, (16, 128), 0)
+    centre = jnp.zeros((16, 128), F32)
+    for k in range(ROWS_DEV):
+        centre = jnp.where(row == k, meta_ref[GATHER.index((0, 0)), k], centre)
+    moved_ref[...] = centre + time_step * own_moving
+    velocity = part_ref[own] + near_ref[...]
+    for place, copy in copies:
+        copy.wait_recv()
+        velocity = velocity + part_in[place]
+    velocity_ref[...] = velocity
     for place, copy in copies:
         copy.wait_send()
+    for half in (0, 1):
+        wide_return[half].sent()
     for step in range(1, narrow_count):
         narrow_copy(step).wait_send()
 
@@ -919,16 +944,36 @@
     turned_x = np.ascontiguousarray(table_x.T)
     turned_y = np.ascontiguousarray(table_y.T)
     tables = np.stack([*halves(table_x), *halves(turned_x), *halves(turned_y)])
-    mesh, near, contacts = pl.pallas_call(
-        functools.partial(transform_kernel, *sizes),
-        out_shape=(
-            shape((32, 2, 8, 384), F32),
-            shape((16, NODES), F32),
-            shape((wide_count * narrow_count, NODES), F32),
-        ),
+    devices = wide_count * narrow_count
+    velocity, force, moved = pl.pallas_call(
+        functools.partial(flow_kernel, *sizes),
+        out_shape=(shape((16, NODES), F32), shape((CONT_DEV, 128), F32), shape((16, 128), F32)),
         in_specs=[SMEM_SPEC] * 3 + [VMEM_SPEC] * 6 + [HBM_SPEC],
         out_specs=(VMEM_SPEC,) * 3,
         scratch_shapes=[
+            pltpu.VMEM((16, NODES), F32),
+            pltpu.VMEM((768, GRID), BF16),
+            pltpu.VMEM((768, GRID), BF16),
+            pltpu.VMEM((384, GRID), BF16),
+            pltpu.VMEM((384, GRID), BF16),
+            pltpu.VMEM((12, 256, GRID), F32),
+            pltpu.VMEM((12, 128, GRID), F32),
+            pltpu.VMEM((6, 16, NODES), F32),
+            pltpu.VMEM((6, 16, NODES), F32),
+            pltpu.VMEM((6, 16, NODES), F32),
+            pltpu.VMEM((8, 128), F32),
+            pltpu.VMEM((8, 8, 128), F32),
+            pltpu.VMEM((8, 128), F32),
+            pltpu.VMEM((32, 8, 128), F32),
+            pltpu.VMEM((9, ROWS_DEV, CONT_DEV, devices), F32),
+            pltpu.VMEM((9, 16, devices), F32),
+            pltpu.VMEM((9, 16, devices), F32),
+            dma((6,)),
+            dma((6,)),
+            dma((8,)),
+            dma((8,)),
+            dma((32,)),
+            dma((32,)),
             pltpu.VMEM((2, 768, NODES), BF16),
             pltpu.VMEM((2, 768, NODES), BF16),
             pltpu.VMEM((768, GRID), F32),
@@ -963,8 +1008,8 @@
             dma((32,)),
             dma((32,)),
         ],
-        compiler_params=params(1),
-        name="transform",
+        compiler_params=params(1, 56),
+        name="flow",
     )(
         near_list.reshape(4, NEAR),
         metas,
@@ -977,40 +1022,6 @@
         contact_angles,
         tables,
     )
-
-    centre_rows = jnp.broadcast_to(jnp.pad(centers.reshape(12, 1), ((0, 4), (0, 0))), (16, 128))
-    devices = wide_count * narrow_count
-    velocity, force, moved = pl.pallas_call(
-        functools.partial(contact_kernel, *sizes),
-        out_shape=(shape((16, NODES), F32), shape((CONT_DEV, 128), F32), shape((16, 128), F32)),
-        in_specs=[SMEM_SPEC] * 2 + [VMEM_SPEC] * 6,
-        out_specs=(VMEM_SPEC,) * 3,
-        scratch_shapes=[
-            pltpu.VMEM((3, NODES, 128), F32),
-            pltpu.VMEM((768, GRID), BF16),
-            pltpu.VMEM((768, GRID), BF16),
-            pltpu.VMEM((384, GRID), BF16),
-            pltpu.VMEM((384, GRID), BF16),
-            pltpu.VMEM((GRID * 8, 128), F32),
-            pltpu.VMEM((6, 16, NODES), F32),
-            pltpu.VMEM((6, 16, NODES), F32),
-            pltpu.VMEM((8, 128), F32),
-            pltpu.VMEM((8, 8, 128), F32),
-            pltpu.VMEM((8, 128), F32),
-            pltpu.VMEM((32, 8, 128), F32),
-            pltpu.VMEM((9, ROWS_DEV, CONT_DEV, devices), F32),
-            pltpu.VMEM((9, 16, devices), F32),
-            pltpu.VMEM((9, 16, devices), F32),
-            dma((6,)),
-            dma((6,)),
-            dma((8,)),
-            dma((8,)),
-            dma((32,)),
-            dma((32,)),
-        ],
-        compiler_params=params(2),
-        name="contacts",
-    )(metas, cells, node_offsets, wrapped_z, mesh, near, contacts, centre_rows)
     return (
         velocity[:12].reshape(2, 2, 3, NODES),
         force[:, 0],

time: 126 us -> 120 us (0.952)
  Pallas kernels: 120 us -> 113 us
    pallas_call x2 -> x1, Pallas kernels: 104 us -> 97.3 us  [local(): pl.pallas_call(functools.partial(flow_kernel, *sizes), out_shape=(shape((...]
    unnamed x24 -> x18, local copies, waits for them, and re-layouts: 4.13 us -> 3.39 us
where the time goes in v4:
time: 120 us
  Pallas kernels  113 us (94%)
  local copies, waits for them, and re-layouts  5.52 us (5%)
    pallas_call x1, Pallas kernels, local(): pl.pallas_call(functools.partial(flow_kernel, *sizes), out_shape=(shape((...  97.3 us
    pallas_call x1, Pallas kernels, local(): pl.pallas_call(functools.partial(gather_kernel, *sizes), out_shape=(shape...  16 us
    unnamed x18, local copies, waits for them, and re-layouts  3.39 us

profile of v4, /device:TPU:1, one launch (start us, length us, event | category | flops | bytes accessed | tf_op | source)
XLA Modules:
  0.0 119.6 jit_solution(4535325001686918121)
XLA Ops:
  0.6 0.0 copy-start.3
  0.6 0.0 copy-start.4
  0.7 0.0 copy-start.5
  0.7 0.7 copy.19.tractions_ref
  1.4 0.0 copy-done.3
  1.4 0.0 copy-done.4
  1.4 0.0 copy-done.5
  1.4 16.0 %gather.1 = (f32[12,16,256]{2,1,0:T(8,128)S(1)}, f32[12,128]{1,0:T(8,128)S(1)}, s32[12,128]{1,0:T(8,128)S(1)}) custom-call(f32[2,2,3,256]{3,2,1,0:T(4,128)S(1)} %copy.19.tractions_ref, f32[2,2,3]{2,1,0:T(2,128)S(1)} %copy-done.3, s32[2,2,3]{2,1,0:T(2,128)S(1)} %copy-done.4, s32[2,2]{1,0:T(2,128)S(1)} %copy-done.5), custom_call_target="tpu_custom_call" | custom-call | tf_op jit(solution)/shard_map/gather/pallas_call | solution.py:925
  17.4 0.0 copy-start
  17.4 0.7 copy-done
  18.1 0.0 copy-start.1
  18.1 0.6 copy-done.1
  18.7 0.0 copy-start.2
  18.7 0.6 copy-done.2
  19.3 97.3 %flow.1 = (f32[16,256]{1,0:T(8,128)}, f32[32,128]{1,0:T(8,128)}, f32[16,128]{1,0:T(8,128)}) custom-call(s32[4,2]{1,0:T(4,128)} %bitcast.3, f32[12,128]{1,0:T(8,128)} %copy-done.1, s32[12,128]{1,0:T(8,128)} %copy-done.2, f32[12,16,256]{2,1,0:T(8,128)} %copy-done, f32[3,256]{1,0:T(4,128)} %off_ref.1, f32[36,8,256]{2,1,0:T(8,128)} %constant.4.clone.tz_ref, ...), custom_call_target="tpu_custom_call" | custom-call | tf_op jit(solution)/shard_map/flow/pallas_call | solution.py:948
  116.6 0.7 reshape.13
  117.4 0.0 copy-start.6
  117.4 0.6 copy.21
  118.0 0.1 copy-done.6
  118.1 0.0 copy-start.7
  118.1 0.6 slice_reduce_fusion
  118.7 0.1 copy-done.7
  118.8 0.1 slice_reduce_fusion.1
  118.9 0.7 reshape_squeeze.3
Async XLA Ops:
  0.6 0.8 copy-start.3
  0.6 0.8 copy-start.4
  0.7 0.8 copy-start.5
  17.4 0.7 copy-start
  18.1 0.6 copy-start.1
  18.7 0.6 copy-start.2
  117.4 0.7 copy-start.6
  118.1 0.7 copy-start.7

commit v5 on v4

--- a/solution.py
+++ b/solution.py
@@ -17,6 +17,7 @@
 SLOTS_DEV = 4
 ROWS_DEV = 3 * SLOTS_DEV
 CONT_DEV = 32
+EDGE_ROWS = 112
 
 soften = 1.0
 screen = 0.0625
@@ -200,7 +201,7 @@
             if j == 0:
                 place, within = own, s
             else:
-                entry = list_ref[s, j - 1]
+                entry = list_ref[s // 2, s % 2, j - 1]
                 holder = entry // SLOTS_DEV
                 within = entry % SLOTS_DEV
                 row = lax.rem(holder // narrow_count - w + 1 + wide_count, wide_count)
@@ -501,8 +502,11 @@
     table_out,
     table_in,
     edges,
+    fields,
     around,
     loads,
+    relatives,
+    forces,
     part_send,
     part_recv,
     tile_send,
@@ -585,7 +589,7 @@
     seconds = ((row_w * 3 + row_n) * SLOTS_DEV).astype(F32) + within
     polar, azimuth = angles_ref[0:1, :], angles_ref[1:2, :]
     across = jnp.sin(polar)
-    fields = [
+    parts = [
         within[0:1],
         seconds[1:2],
         across * jnp.cos(azimuth),
@@ -593,7 +597,7 @@
         jnp.cos(polar),
         gap_ref[...].reshape(1, CONT_DEV),
     ]
-    line = jnp.concatenate(fields + [jnp.zeros((1, 64), F32)], axis=1)
+    line = jnp.concatenate(parts + [jnp.zeros((1, 64), F32)], axis=1)
     own_line[...] = jnp.where(lax.broadcasted_iota(jnp.int32, (8, NODES), 0) == n, line, 0.0)
 
     def line_copy(step):
@@ -618,9 +622,6 @@
 
     for step in range(1, narrow_count):
         line_copy(step).start()
-    near_field(
-        (wide_count, narrow_count), list_ref, meta_ref, held_ref, off_ref, near_ref, offcol, source, columns
-    )
     mean_weights(sizes, meta_ref, cells_ref, off_ref, tz_ref, offcol, full_means, half_means)
     load.wait()
     t_yf[...] = jnp.zeros_like(t_yf)
@@ -734,6 +735,9 @@
         along = dot3((t_x[2], t_x[3]), block)
         wide_back[:, half] = along.reshape(wide_count, 8, 384)
         wide_return[half].begin()
+    near_field(
+        (wide_count, narrow_count), list_ref, meta_ref, held_ref, off_ref, near_ref, offcol, source, columns
+    )
     def end_column(step, carry):
         column_copy(step).wait()
         return carry
@@ -741,16 +745,20 @@
     lax.fori_loop(1, wide_count, end_column, 0)
     for step in range(1, narrow_count):
         line_copy(step).wait_send()
-    fields = jnp.transpose(column_in[...].reshape(wide_count * narrow_count, NODES))
-    first, second, gap = fields[0:32], fields[32:64], fields[160:192]
-    normal = [fields[64 + 32 * c : 96 + 32 * c] for c in range(3)]
-    for place in range(9):
-        for s in range(SLOTS_DEV):
-            mark = jnp.where(second == float(place * SLOTS_DEV + s), -1.0, 0.0)
-            if place == 4:
-                mark = mark + jnp.where(first == float(s), 1.0, 0.0)
-            for c in range(3):
-                edges[place, 3 * s + c] = mark * normal[c]
+    fields[...] = jnp.transpose(column_in[...].reshape(wide_count * narrow_count, NODES))
+    sphere = lax.broadcasted_iota(jnp.int32, (EDGE_ROWS, 1), 0)
+    component = sphere % 3
+    sphere = (sphere // 3).astype(F32)
+
+    def incidence(i, carry):
+        first, second = fields[pl.ds(i, 1), :] + 4.0 * SLOTS_DEV, fields[pl.ds(32 + i, 1), :]
+        normal = [fields[pl.ds(64 + 32 * c + i, 1), :] for c in range(3)]
+        along = jnp.where(component == 0, normal[0], jnp.where(component == 1, normal[1], normal[2]))
+        sign = jnp.where(sphere == first, 1.0, 0.0) - jnp.where(sphere == second, 1.0, 0.0)
+        edges[i] = sign * along
+        return carry
+
+    lax.fori_loop(0, CONT_DEV, incidence, 0)
     for group in (wide_go, narrow_go, narrow_return):
         for half in (0, 1):
             group[half].sent()
@@ -839,43 +847,51 @@
         moved_means = shift_wide(spread_means[p * 16 : p * 16 + 16], dw, narrow_count)
         hydro = hydro + shift_narrow(moved_means, dn, narrow_count)
 
-    def totals(force):
-        def one_place(place, carry):
-            for k in range(ROWS_DEV):
-                loads[place, k : k + 1, :] = jnp.sum(edges[place, k] * force, axis=0, keepdims=True)
-            return carry
-
-        lax.fori_loop(0, 9, one_place, 0)
-        result = jnp.zeros((16, devices), F32)
+    gap = fields[160:192, :]
+
+    def totals():
+        def one_contact(i, sums):
+            return sums + edges[i] * forces[pl.ds(i, 1), :]
+
+        loads[...] = lax.fori_loop(
+            0, CONT_DEV, one_contact, jnp.zeros((EDGE_ROWS, devices), F32), unroll=4
+        )
+        result = jnp.zeros((ROWS_DEV, devices), F32)
         for dn in (-1, 0, 1):
-            inner = jnp.zeros((16, devices), F32)
+            inner = jnp.zeros((ROWS_DEV, devices), F32)
             for dw in (-1, 0, 1):
-                inner = inner + shift_wide(loads[AROUND.index((dw, dn))], dw, narrow_count)
+                start = AROUND.index((dw, dn)) * ROWS_DEV
+                inner = inner + shift_wide(loads[start : start + ROWS_DEV, :], dw, narrow_count)
             result = result + shift_narrow(inner, dn, narrow_count)
-        return result
-
-    def sweep(turn, carry):
-        force, moving = carry
+        return jnp.concatenate([result, jnp.zeros((16 - ROWS_DEV, devices), F32)], axis=0)
+
+    def sweep(turn, moving):
         for dn in (-1, 0, 1):
             beside = shift_narrow(moving, -dn, narrow_count)
             for dw in (-1, 0, 1):
-                around[AROUND.index((dw, dn))] = shift_wide(beside, -dw, narrow_count)
-
-        def one_place(place, relative):
-            for k in range(ROWS_DEV):
-                relative = relative + edges[place, k] * around[place, k : k + 1, :]
-            return relative
-
-        relative = lax.fori_loop(0, 9, one_place, jnp.zeros((CONT_DEV, devices), F32))
-        force = jnp.maximum(
-            force - relaxation * (gap + time_step * relative) / (2.0 * time_step * mobility), 0.0
+                start = AROUND.index((dw, dn)) * ROWS_DEV
+                around[start : start + ROWS_DEV, :] = shift_wide(beside, -dw, narrow_count)[:ROWS_DEV]
+
+        def eight_contacts(block, carry):
+            rows = [
+                jnp.sum(edges[block * 8 + i] * around[...], axis=0, keepdims=True) for i in range(8)
+            ]
+            at = pl.ds(pl.multiple_of(block * 8, 8), 8)
+            relatives[at, :] = jnp.concatenate(rows, axis=0)
+            return carry
+
+        lax.fori_loop(0, CONT_DEV // 8, eight_contacts, 0)
+        forces[...] = jnp.maximum(
+            forces[...]
+            - relaxation * (gap + time_step * relatives[...]) / (2.0 * time_step * mobility),
+            0.0,
         )
-        return force, hydro + mobility * totals(force)
-
-    loads[...] = jnp.zeros_like(loads)
-    force, moving = lax.fori_loop(
-        0, SWEEPS, sweep, (jnp.zeros((CONT_DEV, devices), F32), hydro)
-    )
+        return hydro + mobility * totals()
+
+    around[...] = jnp.zeros_like(around)
+    forces[...] = jnp.zeros_like(forces)
+    moving = lax.fori_loop(0, SWEEPS, sweep, hydro)
+    force = forces[...]
     mine = lanes_of((1, devices)) == w * narrow_count + n
     own_force = jnp.sum(jnp.where(mine, force, 0.0), axis=1, keepdims=True)
     force_ref[...] = jnp.broadcast_to(own_force, (CONT_DEV, 128))
@@ -965,9 +981,12 @@
             pltpu.VMEM((8, 8, 128), F32),
             pltpu.VMEM((8, 128), F32),
             pltpu.VMEM((32, 8, 128), F32),
-            pltpu.VMEM((9, ROWS_DEV, CONT_DEV, devices), F32),
-            pltpu.VMEM((9, 16, devices), F32),
-            pltpu.VMEM((9, 16, devices), F32),
+            pltpu.VMEM((CONT_DEV, EDGE_ROWS, devices), F32),
+            pltpu.VMEM((NODES, devices), F32),
+            pltpu.VMEM((EDGE_ROWS, devices), F32),
+            pltpu.VMEM((EDGE_ROWS, devices), F32),
+            pltpu.VMEM((CONT_DEV, devices), F32),
+            pltpu.VMEM((CONT_DEV, devices), F32),
             dma((6,)),
             dma((6,)),
             dma((8,)),
@@ -1011,7 +1030,7 @@
         compiler_params=params(1, 56),
         name="flow",
     )(
-        near_list.reshape(4, NEAR),
+        near_list,
         metas,
         cells,
         held,

time: 120 us -> 118 us (0.983)
  Pallas kernels: 113 us -> 111 us
    pallas_call x1, Pallas kernels: 97.3 us -> 95 us  [local(): pl.pallas_call(functools.partial(flow_kernel, *sizes), out_shape=(shape((...]
where the time goes in v5:
time: 118 us; the launch traced here: 117 us
  Pallas kernels  111 us (94%)
  local copies, waits for them, and re-layouts  5.52 us (5%)
    pallas_call x1, Pallas kernels, local(): pl.pallas_call(functools.partial(flow_kernel, *sizes), out_shape=(shape((...  95 us
    pallas_call x1, Pallas kernels, local(): pl.pallas_call(functools.partial(gather_kernel, *sizes), out_shape=(shape...  16 us
    unnamed x18, local copies, waits for them, and re-layouts  3.39 us

profile of v5, /device:TPU:1, one launch (start us, length us, event | category | flops | bytes accessed | tf_op | source)
XLA Modules:
  0.0 117.2 jit_solution(5421736886387972718)
XLA Ops:
  0.6 0.0 copy-start.4
  0.6 0.0 copy-start.5
  0.7 0.0 copy-start.3
  0.7 0.7 copy.16.tractions_ref
  1.4 0.0 copy-done.4
  1.4 0.0 copy-done.5
  1.4 0.0 copy-done.3
  1.4 16.0 %gather.1 = (f32[12,16,256]{2,1,0:T(8,128)S(1)}, f32[12,128]{1,0:T(8,128)S(1)}, s32[12,128]{1,0:T(8,128)S(1)}) custom-call(f32[2,2,3,256]{3,2,1,0:T(4,128)S(1)} %copy.16.tractions_ref, f32[2,2,3]{2,1,0:T(2,128)S(1)} %copy-done.3, s32[2,2,3]{2,1,0:T(2,128)S(1)} %copy-done.4, s32[2,2]{1,0:T(2,128)S(1)} %copy-done.5), custom_call_target="tpu_custom_call" | custom-call | tf_op jit(solution)/shard_map/gather/pallas_call | solution.py:941
  17.4 0.0 copy-start
  17.4 0.7 copy-done
  18.1 0.0 copy-start.1
  18.1 0.6 copy-done.1
  18.7 0.0 copy-start.2
  18.7 0.6 copy-done.2
  19.3 95.0 %flow.1 = (f32[16,256]{1,0:T(8,128)}, f32[32,128]{1,0:T(8,128)}, f32[16,128]{1,0:T(8,128)}) custom-call(s32[2,2,2]{2,1,0:T(2,128)} %list_ref.1, f32[12,128]{1,0:T(8,128)} %copy-done.1, s32[12,128]{1,0:T(8,128)} %copy-done.2, f32[12,16,256]{2,1,0:T(8,128)} %copy-done, f32[3,256]{1,0:T(4,128)} %off_ref.1, f32[36,8,256]{2,1,0:T(8,128)} %constant.4.clone.tz_ref, ...), custom_call_target="tpu_custom_call" | custom-call | tf_op jit(solution)/shard_map/flow/pallas_call | solution.py:964
  114.3 0.7 reshape.9
  115.0 0.0 copy-start.6
  115.0 0.6 copy.17
  115.6 0.1 copy-done.6
  115.7 0.0 copy-start.7
  115.7 0.6 slice_reduce_fusion
  116.4 0.1 copy-done.7
  116.4 0.1 slice_reduce_fusion.1
  116.5 0.7 reshape_squeeze.3
Async XLA Ops:
  0.6 0.8 copy-start.4
  0.6 0.8 copy-start.5
  0.7 0.8 copy-start.3
  17.4 0.7 copy-start
  18.1 0.6 copy-start.1
  18.7 0.6 copy-start.2
  115.0 0.7 copy-start.6
  115.7 0.7 copy-start.7

commit v6 on v5

--- a/solution.py
+++ b/solution.py
@@ -190,13 +190,12 @@
         copy.wait_send()
 
 
-def near_field(sizes, list_ref, meta_ref, held_ref, off_ref, out_ref, offcol, source, columns):
+def near_field(slots, sizes, list_ref, meta_ref, held_ref, off_ref, out_ref, offcol, source, columns):
     wide_count, narrow_count = sizes
     w, n = lax.axis_index("wide"), lax.axis_index("narrow")
     own = GATHER.index((0, 0))
-    out_ref[...] = jnp.zeros_like(out_ref)
     columns[...] = jnp.zeros_like(columns)
-    for s in range(SLOTS_DEV):
+    for s in slots:
         for j in range(1 + NEAR):
             if j == 0:
                 place, within = own, s
@@ -622,6 +621,10 @@
 
     for step in range(1, narrow_count):
         line_copy(step).start()
+    near_ref[...] = jnp.zeros_like(near_ref)
+    near_field(
+        (0, 1), sizes, list_ref, meta_ref, held_ref, off_ref, near_ref, offcol, source, columns
+    )
     mean_weights(sizes, meta_ref, cells_ref, off_ref, tz_ref, offcol, full_means, half_means)
     load.wait()
     t_yf[...] = jnp.zeros_like(t_yf)
@@ -736,7 +739,7 @@
         wide_back[:, half] = along.reshape(wide_count, 8, 384)
         wide_return[half].begin()
     near_field(
-        (wide_count, narrow_count), list_ref, meta_ref, held_ref, off_ref, near_ref, offcol, source, columns
+        (2, 3), sizes, list_ref, meta_ref, held_ref, off_ref, near_ref, offcol, source, columns
     )
     def end_column(step, carry):
         column_copy(step).wait()

time: 118 us -> 118 us (level)
  no operation moved by 1% of the time
where the time goes in v6:
time: 118 us; the launch traced here: 117 us
  Pallas kernels  111 us (94%)
  local copies, waits for them, and re-layouts  5.52 us (5%)
    pallas_call x1, Pallas kernels, local(): pl.pallas_call(functools.partial(flow_kernel, *sizes), out_shape=(shape((...  95 us
    pallas_call x1, Pallas kernels, local(): pl.pallas_call(functools.partial(gather_kernel, *sizes), out_shape=(shape...  16 us
    unnamed x18, local copies, waits for them, and re-layouts  3.39 us

profile of v6, /device:TPU:1, one launch (start us, length us, event | category | flops | bytes accessed | tf_op | source)
XLA Modules:
  0.0 117.2 jit_solution(6579430267309223858)
XLA Ops:
  0.6 0.0 copy-start.4
  0.6 0.0 copy-start.5
  0.7 0.0 copy-start.3
  0.7 0.7 copy.16.tractions_ref
  1.4 0.0 copy-done.4
  1.4 0.0 copy-done.5
  1.4 0.0 copy-done.3
  1.4 16.0 %gather.1 = (f32[12,16,256]{2,1,0:T(8,128)S(1)}, f32[12,128]{1,0:T(8,128)S(1)}, s32[12,128]{1,0:T(8,128)S(1)}) custom-call(f32[2,2,3,256]{3,2,1,0:T(4,128)S(1)} %copy.16.tractions_ref, f32[2,2,3]{2,1,0:T(2,128)S(1)} %copy-done.3, s32[2,2,3]{2,1,0:T(2,128)S(1)} %copy-done.4, s32[2,2]{1,0:T(2,128)S(1)} %copy-done.5), custom_call_target="tpu_custom_call" | custom-call | tf_op jit(solution)/shard_map/gather/pallas_call | solution.py:944
  17.4 0.0 copy-start
  17.4 0.7 copy-done
  18.1 0.0 copy-start.1
  18.1 0.6 copy-done.1
  18.7 0.0 copy-start.2
  18.7 0.6 copy-done.2
  19.3 95.0 %flow.1 = (f32[16,256]{1,0:T(8,128)}, f32[32,128]{1,0:T(8,128)}, f32[16,128]{1,0:T(8,128)}) custom-call(s32[2,2,2]{2,1,0:T(2,128)} %list_ref.1, f32[12,128]{1,0:T(8,128)} %copy-done.1, s32[12,128]{1,0:T(8,128)} %copy-done.2, f32[12,16,256]{2,1,0:T(8,128)} %copy-done, f32[3,256]{1,0:T(4,128)} %off_ref.1, f32[36,8,256]{2,1,0:T(8,128)} %constant.4.clone.tz_ref, ...), custom_call_target="tpu_custom_call" | custom-call | tf_op jit(solution)/shard_map/flow/pallas_call | solution.py:967
  114.3 0.7 reshape.9
  115.0 0.0 copy-start.6
  115.0 0.6 copy.17
  115.6 0.1 copy-done.6
  115.7 0.0 copy-start.7
  115.7 0.6 slice_reduce_fusion
  116.3 0.1 copy-done.7
  116.4 0.1 slice_reduce_fusion.1
  116.5 0.7 reshape_squeeze.3
Async XLA Ops:
  0.6 0.8 copy-start.4
  0.6 0.8 copy-start.5
  0.7 0.8 copy-start.3
  17.4 0.7 copy-start
  18.1 0.6 copy-start.1
  18.7 0.6 copy-start.2
  115.0 0.7 copy-start.6
  115.7 0.7 copy-start.7

commit v7 on v5

--- a/solution.py
+++ b/solution.py
@@ -1027,7 +1027,7 @@
             dma((32,)),
             dma((32,)),
         ],
-        compiler_params=params(1, 56),
+        compiler_params=params(1, 40),
         name="flow",
     )(
         near_list,

time: 118 us -> 117 us (level)
    unnamed x18 -> x22, local copies, waits for them, and re-layouts: 3.39 us -> 4.11 us
where the time goes in v7:
time: 117 us
  Pallas kernels  110 us (94%)
  local copies, waits for them, and re-layouts  5.53 us (5%)
    pallas_call x1, Pallas kernels, local(): pl.pallas_call(functools.partial(flow_kernel, *sizes), out_shape=(shape((...  94.3 us
    pallas_call x1, Pallas kernels, local(): pl.pallas_call(functools.partial(gather_kernel, *sizes), out_shape=(shape...  16 us
    unnamed x22, local copies, waits for them, and re-layouts  4.11 us

profile of v7, /device:TPU:1, one launch (start us, length us, event | category | flops | bytes accessed | tf_op | source)
XLA Modules:
  0.0 116.6 jit_solution(649219875880953680)
XLA Ops:
  0.6 0.0 copy-start.5
  0.6 0.0 copy-start.8
  0.7 0.0 copy-start.4
  0.7 0.7 copy.16.tractions_ref
  1.4 0.0 copy-done.5
  1.4 0.0 copy-done.8
  1.4 0.0 copy-done.4
  1.4 0.0 copy-start.3
  1.4 0.0 copy-start.7
  1.4 16.0 %gather.1 = (f32[12,16,256]{2,1,0:T(8,128)S(1)}, f32[12,128]{1,0:T(8,128)S(1)}, s32[12,128]{1,0:T(8,128)S(1)}) custom-call(f32[2,2,3,256]{3,2,1,0:T(4,128)S(1)} %copy.16.tractions_ref, f32[2,2,3]{2,1,0:T(2,128)S(1)} %copy-done.4, s32[2,2,3]{2,1,0:T(2,128)S(1)} %copy-done.5, s32[2,2]{1,0:T(2,128)S(1)} %copy-done.8), custom_call_target="tpu_custom_call" | custom-call | tf_op jit(solution)/shard_map/gather/pallas_call | solution.py:941
  17.4 0.0 copy-start.2
  17.5 0.0 copy-start.6
  17.5 0.0 copy-start.9
  17.5 0.0 copy-done.3
  17.5 0.0 copy-done.7
  17.5 0.6 copy-done.2
  18.1 0.0 copy-done.6
  18.1 0.0 copy-done.9
  18.1 0.0 copy-start
  18.1 1.1 copy-done
  19.3 0.0 copy-start.1
  19.3 1.0 copy-done.1
  20.2 94.3 %flow.1 = (f32[16,256]{1,0:T(8,128)S(1)}, f32[32,128]{1,0:T(8,128)S(1)}, f32[16,128]{1,0:T(8,128)S(1)}) custom-call(s32[2,2,2]{2,1,0:T(2,128)S(1)} %copy-done.3, f32[12,128]{1,0:T(8,128)S(1)} %get-tuple-element.9.meta_ref, s32[12,128]{1,0:T(8,128)S(1)} %get-tuple-element.10.cells_ref, f32[12,16,256]{2,1,0:T(8,128)S(1)} %get-tuple-element.11.held_ref, ...), custom_call_target="tpu_custom_call" | custom-call | tf_op jit(solution)/shard_map/flow/pallas_call | solution.py:964
  114.6 0.6 copy.17
  115.2 0.6 slice_reduce_fusion
  115.8 0.1 slice_reduce_fusion.1
  115.9 0.7 reshape_squeeze.3
  (1 shorter events, 0.0 us)
Async XLA Ops:
  0.6 0.8 copy-start.5
  0.6 0.8 copy-start.8
  0.7 0.8 copy-start.4
  1.4 16.1 %copy-start.3 = (s32[2,2,2]{2,1,0:T(2,128)S(1)}, s32[2,2,2]{2,1,0:T(2,128)}, u32[]{:S(2)}) copy-start(s32[2,2,2]{2,1,0:T(2,128)} %list_ref.1) | copy-start | bytes 100
  1.4 16.1 %copy-start.7 = (f32[2,32]{1,0:T(2,128)S(1)}, f32[2,32]{1,0:T(2,128)}, u32[]{:S(2)}) copy-start(f32[2,32]{1,0:T(2,128)} %angles_ref.1) | copy-start | bytes 772
  17.4 0.7 copy-start.2
  17.5 0.7 copy-start.6
  17.5 0.7 copy-start.9
  18.1 1.1 copy-start
  19.3 1.0 copy-start.1
